TPU v7x, 256 devices: a whole 4x4x8 slice. The times are simulated.
256 devices in a mesh: wide: 32 (over x, z_hi, y), kvh: 8 (over z_lo, core).
Axes of the slice: x: 4, y: 4, z: 8 (z_hi: 2, z_lo: 4; z = z_hi * 4 + z_lo), core: 2. Of those that a mesh axis runs over, the one named last changes fastest.
Arguments:
- prefill_rows: bfloat16 [32768, 5120], P('wide'), may hold values from -6 to 6
- in_gain: float32 [5120], replicated, may hold values from 0.1 to 1.9
- key_weight: bfloat16 [5120, 1024], P(None, 'kvh'), may hold values from -0.078125 to 0.078125
- value_weight: bfloat16 [5120, 1024], P(None, 'kvh'), may hold values from -0.078125 to 0.078125
- key_gain: float32 [128], replicated, may hold values from 0.5 to 8
- query_gain: float32 [128], replicated, may hold values from 0.5 to 8
- block_request: int32 [1024], P('wide'), may hold values from 0 to 15
- block_target: int32 [1024, 1], P('wide'), may hold values from 0 to 31; in each aligned block of 32 rows (0 to 31, 32 to 63, ...) at most 2 rows name the same one
- context_lengths: int32 [16], replicated, may hold values from 1 to 4096, as said below
- kv_cache: bfloat16 [2, 16, 4096, 1024], P(None, None, 'wide', 'kvh'), may hold values from -6 to 6
- decode_queries: bfloat16 [2, 16, 8192], P(None, None, 'kvh')
- decode_partials: float32 [8, 2, 16, 5120], P('kvh'), may hold values from -4 to 4
- decode_residual: float32 [2, 16, 5120], replicated, may hold values from -6 to 6
Outputs:
- attended: bfloat16 [2, 16, 8192], P(None, None, 'kvh')
- new_blocks: bfloat16 [2048, 32, 2, 1024], P('wide', None, None, 'kvh')
- new_tokens: bfloat16 [2, 16, 2, 1024], P(None, None, None, 'kvh')
Inputs may be any that keep to these rules, and one draw needn't show every extreme that they name: `block_target`: among the 32 blocks of one group no decode shard is named more than 2 times, a bound that some block reaches. `context_lengths`: some decode row fills all 4096 positions.
All inputs are finite; a program needn't handle non-finite values.
Results may differ from a plain program's by a relative error of at most 0.029.
Values may be sent and summed in bfloat16 or wider, within the bound.
No kernel may reach another device: no remote copies, remote signals or barrier semaphores. Data moves between devices by JAX's collectives and lax.ppermute only.
A program may use at most 64 MiB of HBM per device.

v0:
```python
import jax
import jax.numpy as jnp
from jax import lax
from jax.sharding import PartitionSpec as P

CAP = 2


EPS = 1e-06
THETA = 1000000.0
NEG_FILL = -1e30


def head_norm(vectors, gain_vec):
    mean_square = jnp.mean(vectors * vectors, axis=-1, keepdims=True)
    return vectors * lax.rsqrt(mean_square + EPS) * gain_vec


def rotate(vectors, positions):
    half_dim = vectors.shape[-1] // 2
    exponent = jnp.arange(half_dim, dtype=jnp.float32) * (2.0 / vectors.shape[-1])
    frequency = jnp.power(jnp.float32(THETA), -exponent)
    angles = positions.astype(jnp.float32)[..., None] * frequency
    cosine = jnp.cos(angles)
    sine_part = jnp.sin(angles)
    front = vectors[..., :half_dim]
    back = vectors[..., half_dim:]
    return jnp.concatenate(
        [front * cosine - back * sine_part, back * cosine + front * sine_part], axis=-1
    )


def local(
    prefill_rows,
    in_gain,
    key_weight,
    value_weight,
    key_gain,
    query_gain,
    block_request,
    block_target,
    context_lengths,
    kv_cache,
    decode_queries,
    decode_partials,
    decode_residual,
):
    wide_count = lax.axis_size("wide")
    position = lax.axis_index("wide")
    block_count = block_request.shape[0]
    block_len = prefill_rows.shape[0] // block_count
    head_dim = key_gain.shape[0]
    lane_width = key_weight.shape[1]
    local_heads = lane_width // head_dim
    row_count = context_lengths.shape[0]
    slot_count = kv_cache.shape[2]
    per_group = decode_queries.shape[2] // lane_width
    capacity = CAP
    all_request, all_target = (
        lax.all_gather(block_request, "wide", axis=0, tiled=True),
        lax.all_gather(block_target[:, 0], "wide", axis=0, tiled=True),
    )
    requests = jnp.arange(row_count, dtype=jnp.int32)
    owner_table = (all_request[:, None] == requests[None, :]).astype(jnp.int32)
    block_rank = jnp.sum((jnp.cumsum(owner_table, axis=0) - owner_table) * owner_table, axis=1)
    counts = jnp.sum(owner_table, axis=0)
    block_start = jnp.sum(owner_table * context_lengths[None, :], axis=1) + block_len * block_rank
    destinations = jnp.arange(wide_count, dtype=jnp.int32)
    sent_table = (
        (all_target[:, None] == destinations[None, :])
        .astype(jnp.int32)
        .reshape(wide_count, block_count, wide_count)
    )
    target_rank = jnp.sum(
        (jnp.cumsum(sent_table, axis=1) - sent_table) * sent_table, axis=2
    ).reshape(wide_count * block_count)
    source = jnp.arange(wide_count * block_count, dtype=jnp.int32) // block_count
    incoming = jnp.where(
        all_target == position, source * capacity + target_rank, wide_count * capacity
    )
    slot_request = (
        jnp.full((wide_count * capacity,), -1, jnp.int32).at[incoming].set(all_request, mode="drop")
    )
    own_start = lax.dynamic_slice_in_dim(block_start, position * block_count, block_count)
    own_slot = block_target[:, 0] * capacity + lax.dynamic_slice_in_dim(
        target_rank, position * block_count, block_count
    )
    rows_float = prefill_rows.astype(jnp.float32)
    row_scale = lax.rsqrt(jnp.mean(rows_float * rows_float, axis=-1, keepdims=True) + EPS)
    normed = (rows_float * row_scale * in_gain).astype(jnp.bfloat16)
    token_pos = (own_start[:, None] + jnp.arange(block_len, dtype=jnp.int32)[None, :]).reshape(-1)
    projected = jnp.dot(normed, key_weight, preferred_element_type=jnp.float32).reshape(
        -1, local_heads, head_dim
    )
    prefill_keys = rotate(head_norm(projected, key_gain), token_pos[:, None]).astype(jnp.bfloat16)
    prefill_values = jnp.dot(normed, value_weight, preferred_element_type=jnp.float32).astype(
        jnp.bfloat16
    )
    blocks = jnp.stack(
        [
            prefill_keys.reshape(block_count, block_len, lane_width),
            prefill_values.reshape(block_count, block_len, lane_width),
        ],
        axis=2,
    )
    outgoing = (
        jnp.zeros((wide_count * capacity, block_len, 2, lane_width), jnp.bfloat16)
        .at[own_slot]
        .set(blocks)
    )
    received = lax.all_to_all(
        outgoing.reshape(wide_count, capacity, block_len, 2, lane_width),
        "wide",
        split_axis=0,
        concat_axis=0,
        tiled=True,
    )
    new_blocks = received.reshape(wide_count * capacity, block_len, 2, lane_width)
    summed = lax.psum(decode_partials[0].astype(jnp.bfloat16), "kvh").astype(jnp.float32)
    hidden = decode_residual + summed
    hidden_scale = lax.rsqrt(jnp.mean(hidden * hidden, axis=-1, keepdims=True) + EPS)
    decode_normed = (hidden * hidden_scale * in_gain).astype(jnp.bfloat16)
    decode_pos = (context_lengths + block_len * counts)[None, :] + jnp.arange(2, dtype=jnp.int32)[
        :, None
    ]
    flat_rows = decode_normed.reshape(2 * row_count, -1)
    new_proj = jnp.dot(flat_rows, key_weight, preferred_element_type=jnp.float32).reshape(
        2, row_count, local_heads, head_dim
    )
    new_keys = rotate(head_norm(new_proj, key_gain), decode_pos[:, :, None]).astype(jnp.bfloat16)
    new_values = (
        jnp.dot(flat_rows, value_weight, preferred_element_type=jnp.float32)
        .astype(jnp.bfloat16)
        .reshape(2, row_count, lane_width)
    )
    new_tokens = jnp.stack([new_keys.reshape(2, row_count, lane_width), new_values], axis=2)
    query_heads = decode_queries.astype(jnp.float32).reshape(
        2, row_count, local_heads * per_group, head_dim
    )
    queries = rotate(head_norm(query_heads, query_gain), decode_pos[:, :, None]).astype(
        jnp.bfloat16
    )
    queries = queries.reshape(2, row_count, local_heads, per_group, head_dim)
    block_keys = new_blocks[:, :, 0].reshape(-1, local_heads, head_dim)
    block_values = new_blocks[:, :, 1].reshape(-1, local_heads, head_dim)
    block_owner = jnp.repeat(slot_request, block_len)
    score_scale = head_dim ** (-0.5)
    cache_keys = kv_cache[0].reshape(row_count, slot_count, local_heads, head_dim)
    cache_values = kv_cache[1].reshape(row_count, slot_count, local_heads, head_dim)
    live_cache = (position * slot_count + jnp.arange(slot_count, dtype=jnp.int32))[
        None, :
    ] < context_lengths[:, None]
    cache_mask = live_cache[None, :, None, None, :]
    block_mask = (block_owner[None, :] == requests[:, None])[None, :, None, None, :]
    causal = jnp.arange(2)[:, None] >= jnp.arange(2)[None, :]
    own_mask = (causal & (position == 0))[:, None, None, None, :]
    cache_scores = (
        jnp.einsum("srhgd,rchd->srhgc", queries, cache_keys, preferred_element_type=jnp.float32)
        * score_scale
    )
    block_scores = (
        jnp.einsum("srhgd,nhd->srhgn", queries, block_keys, preferred_element_type=jnp.float32)
        * score_scale
    )
    own_scores = (
        jnp.einsum("srhgd,trhd->srhgt", queries, new_keys, preferred_element_type=jnp.float32)
        * score_scale
    )
    row_top = jnp.maximum(
        jnp.maximum(
            jnp.max(jnp.where(cache_mask, cache_scores, NEG_FILL), axis=-1),
            jnp.max(jnp.where(block_mask, block_scores, NEG_FILL), axis=-1),
        ),
        jnp.max(jnp.where(own_mask, own_scores, NEG_FILL), axis=-1),
    )
    cache_weights = jnp.where(cache_mask, jnp.exp(cache_scores - row_top[..., None]), 0.0)
    block_weights = jnp.where(block_mask, jnp.exp(block_scores - row_top[..., None]), 0.0)
    own_weights = jnp.where(own_mask, jnp.exp(own_scores - row_top[..., None]), 0.0)
    row_total = (
        jnp.sum(cache_weights, axis=-1)
        + jnp.sum(block_weights, axis=-1)
        + jnp.sum(own_weights, axis=-1)
    )
    new_value_heads = new_values.reshape(2, row_count, local_heads, head_dim)
    weighted = jnp.einsum(
        "srhgc,rchd->srhgd",
        cache_weights.astype(jnp.bfloat16),
        cache_values,
        preferred_element_type=jnp.float32,
    )
    weighted = weighted + jnp.einsum(
        "srhgn,nhd->srhgd",
        block_weights.astype(jnp.bfloat16),
        block_values,
        preferred_element_type=jnp.float32,
    )
    weighted = weighted + jnp.einsum(
        "srhgt,trhd->srhgd",
        own_weights.astype(jnp.bfloat16),
        new_value_heads,
        preferred_element_type=jnp.float32,
    )
    global_top = lax.pmax(row_top, "wide")
    factor = jnp.exp(row_top - global_top)
    full_total, full_weighted = (
        lax.psum((row_total * factor).astype(jnp.bfloat16), "wide").astype(jnp.float32),
        lax.psum((weighted * factor[..., None]).astype(jnp.bfloat16), "wide").astype(jnp.float32),
    )
    attended = (
        (full_weighted / full_total[..., None]).astype(jnp.bfloat16).reshape(2, row_count, -1)
    )
    return (attended, new_blocks, new_tokens)


def solution(mesh):
    placed = (
        P("wide", None),
        P(),
        P(None, "kvh"),
        P(None, "kvh"),
        P(),
        P(),
        P("wide"),
        P("wide", None),
        P(),
        P(None, None, "wide", "kvh"),
        P(None, None, "kvh"),
        P("kvh", None, None, None),
        P(),
    )
    return jax.shard_map(
        local,
        mesh=mesh,
        in_specs=placed,
        out_specs=(P(None, None, "kvh"), P("wide", None, None, "kvh"), P(None, None, None, "kvh")),
        check_vma=False,
    )
```

profile of v0, /device:TPU:1, one launch (start us, length us, event | category | flops | bytes accessed | tf_op | source)
XLA Modules:
  0.0 709.6 jit_solution(17871531463804649037)
XLA Ops:
  7.2 1.9 convert_bitcast_fusion
  9.2 0.5 negate_power_fusion
  9.7 6.1 fusion
  15.9 0.6 add_rsqrt_fusion.2
  16.5 0.6 dynamic-slice
  17.7 0.2 dynamic-update-slice
  18.0 0.1 bitcast_dynamic-update-slice_fusion
  18.1 22.2 %all-reduce.2 = (s32[1024]{0:T(1024)S(1)}, s32[1024]{0:T(1024)S(1)}) all-reduce(s32[1024]{0:T(1024)S(1)} %dynamic-update-slice, s32[1024]{0:T(1024)S(1)} %bitcast_dynamic-update-slice_fusion), channel_id=1, replica_groups=mesh['wide'=32,'kvh'=8] {'wide'}, use_global_device_ids=true, to_apply=%add | all-reduce | flops 2048 | bytes 16384
  40.2 0.6 copy-done.8
  41.0 1.0 fusion.77
  42.2 4.5 reduce-window.6
  46.8 0.1 copy.140
  47.0 0.1 broadcast_add_fusion
  47.1 0.9 compare_select_fusion.1
  48.0 0.8 fusion.39
  48.9 0.1 dynamic_slice.7
  49.1 8.1 %fusion.10 = bf16[1024,128]{1,0:T(8,128)(2,1)} fusion(bf16[5120,128]{1,0:T(8,128)(2,1)} %param.16, bf16[1024,5120]{1,0:T(8,128)(2,1)} %param.13, f32[5120]{0:T(1024)} %param.14, f32[1024]{0:T(1024)} %add_rsqrt_fusion.2), kind=kOutput, calls=%fused_computation.15 | convolution fusion | flops 1363279872 | bytes 12083200 | tf_op jit(solution)/shard_map/dot_general | solution.py:96
  57.3 3.4 multiply_reduce_fusion.1
  60.8 0.1 multiply_bitcast_fusion
  60.9 1.2 fusion.32
  62.1 0.2 copy.142
  62.2 0.2 copy.143
  62.4 0.2 pad_maximum_fusion
  62.7 1.2 broadcast_in_dim.120
  63.9 4.4 scatter_fusion
  68.3 4.1 all-to-all-start
  72.4 0.5 compare_and_fusion
  73.0 4.5 scatter_custom_fusion
  77.8 0.3 multiply_cosine_fusion.2
  78.1 0.1 multiply_reduce_fusion.2
  78.3 0.1 copy.137
  78.4 0.1 multiply_multiply_fusion
  78.5 0.1 subtract_convert_fusion
  78.6 0.1 pad_maximum_fusion.1
  78.8 2.1 select_reduce_fusion.1
  80.9 4.0 all-reduce.6.cloned.1.call-done
  84.9 1.1 multiply_reduce_fusion
  86.0 1.1 multiply_convert_fusion
  87.1 0.4 multiply_reduce_fusion.3
  87.6 0.1 rsqrt.48
  87.7 0.1 copy.148
  87.8 1.7 convolution_convert_fusion
  89.4 0.1 fusion.55
  89.5 0.3 fusion.58
  89.9 0.5 select_reduce_fusion.3
  90.3 3.1 all-to-all-done
  93.4 0.1 copy.145
  93.5 0.9 fusion.76
  94.4 1.8 select_reduce_fusion
  96.4 0.2 fusion.36
  96.6 2.0 convolution_bitcast_fusion
  98.6 2.1 fusion.8
  100.7 0.1 copy.153
  100.8 192.5 %pmax.7 = f32[2,16,1,8]{3,0,1,2:T(2,128)S(1)} all-reduce(f32[2,16,1,8]{3,0,1,2:T(2,128)S(1)} %bitcast.169), channel_id=1, replica_groups=mesh['wide'=32,'kvh'=8] {'wide'}, use_global_device_ids=true, to_apply=%region_18.19 | all-reduce | flops 256 | bytes 2048 | tf_op jit(solution)/shard_map/pmax | solution.py:203
  293.3 0.8 fusion.69
  294.1 0.9 convolution_bitcast_fusion.2
  295.1 2.4 fusion.17
  297.5 0.1 pad_maximum_fusion.2
  297.6 0.6 copy.157
  298.2 2.1 copy.156
  300.3 96.0 %psum.23 = bf16[2,16,8]{2,0,1:T(2,128)(2,1)S(1)} all-reduce(bf16[2,16,8]{2,0,1:T(2,128)(2,1)S(1)} %get-tuple-element.37), channel_id=1, replica_groups=mesh['wide'=32,'kvh'=8] {'wide'}, use_global_device_ids=true, to_apply=%region_23.24 | all-reduce | flops 256 | bytes 1024 | tf_op jit(solution)/shard_map/psum | solution.py:206
  396.3 304.8 %all-reduce.8.cloned.1.call-done = bf16[2,16,1,8,128]{4,3,0,1,2:T(8,128)(2,1)} async-done(((bf16[2,16,1,8,128]{4,3,0,1,2:T(8,128)(2,1)}), bf16[2,16,1,8,128]{4,3,0,1,2:T(8,128)(2,1)}) %all-reduce.8.cloned.1.call-update) | async-done | bytes 65552 | tf_op jit(solution)/shard_map/psum | solution.py:207
  701.2 0.9 divide_convert_fusion
  702.2 0.6 copy.155
  (84 shorter events, 1.6 us)
Async XLA Ops:
  7.2 50.1 %copy-start = (bf16[5120,128]{1,0:T(8,128)(2,1)S(1)}, bf16[5120,128]{1,0:T(8,128)(2,1)}, u32[]{:S(2)}) copy-start(bf16[5120,128]{1,0:T(8,128)(2,1)} %param.15) | copy-start | bytes 3932164
  7.2 77.7 %all-reduce.6.cloned.1.call-start = ((), (), s32[]{:S(2)}) async-start(), calls=%async_computation.1 | async-start | bytes 655360 | tf_op jit(solution)/shard_map/psum | solution.py:119
  9.7 6.7 copy-start.18
  9.7 8.0 %copy-start.17 = (s32[32]{0:T(128)S(1)}, s32[32]{0:T(128)}, u32[]{:S(2)}) copy-start(s32[32]{0:T(128)} %param.19) | copy-start | bytes 388
  9.7 8.2 %copy-start.16 = (s32[32,1]{0,1:T(1,128)S(1)}, s32[32,1]{0,1:T(1,128)}, u32[]{:S(2)}) copy-start(s32[32,1]{0,1:T(1,128)} %param.20) | copy-start | bytes 388
  40.2 0.6 copy-start.8
  46.8 10.5 %slice-start = ((s8[10485760]{0:T(1024)(128)(4,1)}), s8[2097152]{0:T(1024)(128)(4,1)S(1)}, s32[]{:S(2)}) async-start(s8[10485760]{0:T(1024)(128)(4,1)} %bitcast.155), calls=%async_computation.3 | async-start | bytes 4194304
  49.1 8.1 %slice-start.1 = ((s8[10485760]{0:T(1024)(128)(4,1)}), s8[4194304]{0:T(1024)(128)(4,1)S(1)}, s32[]{:S(2)}) async-start(s8[10485760]{0:T(1024)(128)(4,1)} %bitcast.155), calls=%async_computation.4 | async-start | bytes 8388608
  49.1 8.1 %slice-start.2 = ((s8[10485760]{0:T(1024)(128)(4,1)}), s8[4194304]{0:T(1024)(128)(4,1)S(1)}, s32[]{:S(2)}) async-start(s8[10485760]{0:T(1024)(128)(4,1)} %bitcast.155), calls=%async_computation.5 | async-start | bytes 8388608
  49.1 8.1 %copy-start.5 = (f32[5120]{0:T(1024)S(1)}, f32[5120]{0:T(1024)}, u32[]{:S(2)}) copy-start(f32[5120]{0:T(1024)} %param.14) | copy-start | bytes 61444
  49.1 8.2 %copy-start.11 = (f32[1024]{0:T(1024)S(1)}, f32[1024]{0:T(1024)}, u32[]{:S(2)}) copy-start(f32[1024]{0:T(1024)} %add_rsqrt_fusion.2) | copy-start | bytes 12292
  57.3 3.5 copy-start.13
  57.3 3.6 copy-start.10
  60.7 1.7 copy-start.3
  63.9 8.5 %copy-start.9 = (s32[1024]{0:T(1024)S(1)}, s32[1024]{0:T(1024)}, u32[]{:S(2)}) copy-start(s32[1024]{0:T(1024)} %copy-done.8) | copy-start | bytes 12292
  63.9 9.0 %copy-start.12 = (s32[16]{0:T(128)S(1)}, s32[16]{0:T(128)}, u32[]{:S(2)}) copy-start(s32[16]{0:T(128)} %param.21) | copy-start | bytes 196
  63.9 14.2 %copy-start.4 = (bf16[2,16,1024]{2,1,0:T(8,128)(2,1)S(1)}, bf16[2,16,1024]{2,1,0:T(8,128)(2,1)}, u32[]{:S(2)}) copy-start(bf16[2,16,1024]{2,1,0:T(8,128)(2,1)} %param.23) | copy-start | bytes 196612
  63.9 14.5 %copy-start.14 = (f32[128]{0:T(128)S(1)}, f32[128]{0:T(128)}, u32[]{:S(2)}) copy-start(f32[128]{0:T(128)} %param.18) | copy-start | bytes 1540
  68.3 16.6 %copy-start.1 = (f32[2,16,5120]{2,1,0:T(8,128)S(1)}, f32[2,16,5120]{2,1,0:T(8,128)}, u32[]{:S(2)}) copy-start(f32[2,16,5120]{2,1,0:T(8,128)} %param.25) | copy-start | bytes 1966084
  68.3 25.1 %all-to-all-start = ((bf16[32,2,32,2,128]{4,2,3,1,0:T(8,128)(2,1)}), bf16[32,2,32,2,128]{4,2,3,1,0:T(8,128)(2,1)S(1)}, u32[]{:S(2)}, u32[]{:S(2)}) async-start(bf16[32,2,32,2,128]{4,2,3,1,0:T(8,128)(2,1)} %bitcast.18), calls=%async_computation | async-start | bytes 2097152 | tf_op jit(solution)/shard_map/all_to_all | solution.py:111
  72.3 628.8 %all-reduce.8.cloned.1.call-start = ((), (), s32[]{:S(2)}) async-start(), calls=%async_computation.2 | async-start | bytes 131072 | tf_op jit(solution)/shard_map/psum | solution.py:207
  73.0 5.7 copy-start.6
  87.1 2.7 copy-start.15
  93.5 2.9 copy-start.2
  93.5 2.9 copy-start.7
Sparse Core Ops, SparseCore 0:
  10.6 74.1 all-reduce.5
  297.7 403.4 all-reduce.7
where the time goes:
time: 719 us; the launch traced here: 710 us
  waiting for transfers between devices  312 us (43%)
  blocking collectives  311 us (43%)
  other arithmetic  26.5 us (4%)
  matrix products  23.4 us (3%)
  local copies, waits for them, and re-layouts  17.9 us (2%)
  between operations  15.2 us (2%)
    psum x1, waiting for transfers between devices, local(): lax.psum((weighted * factor[..., None]).astype(jnp.bfloat16), 'wide')  305 us
    pmax x1, blocking collectives, local(): global_top = lax.pmax(row_top, 'wide')  192 us
    psum x1, blocking collectives, local(): lax.psum((row_total * factor).astype(jnp.bfloat16), 'wide')  96 us
    unnamed x1, blocking collectives  22.2 us
  transfers between devices with their start and end apart: 3, of which 3 were waited for; matrix products, arithmetic and copies ran while one was open for 7% of the time, Pallas kernels for 0%

commit v1 on v0

v1 whole, which is shorter than its diff:
```python
import functools

import jax
import jax.numpy as jnp
import numpy as np
from jax import lax
from jax.experimental import pallas as pl
from jax.experimental.pallas import tpu as pltpu
from jax.sharding import PartitionSpec as P

CAP = 2
EPS = 1e-06
THETA = 1000000.0
MASKED = -3e38
FLOOR = -1e30
F32 = jnp.float32
BF16 = jnp.bfloat16
VMEM_LIMIT = 48 * 1024 * 1024

HD = 128
BLK = 32
STAT = 256
TOK = 272
ROWS = 336


def params(**kw):
    return pltpu.CompilerParams(vmem_limit_bytes=VMEM_LIMIT, **kw)


def dot(a, b):
    return jnp.dot(a, b, preferred_element_type=F32)


def dot_nt(a, b):
    return lax.dot_general(a, b, (((1,), (1,)), ((), ())), preferred_element_type=F32)


def rope_sign():
    lane = lax.broadcasted_iota(jnp.int32, (1, HD), 1)
    return jnp.where(lane < HD // 2, -1.0, 1.0).astype(F32)


def head_norm(x, gain):
    return x * lax.rsqrt(jnp.mean(x * x, axis=-1, keepdims=True) + EPS) * gain


def project_kernel(x_ref, gain_ref, wk_ref, wv_ref, kgain_ref, k_ref, v_ref, w_ref):
    depth = x_ref.shape[1]
    chunk = 512

    @pl.when(pl.program_id(0) == 0)
    def _():
        w_ref[:, :HD] = wk_ref[...]
        w_ref[:, HD:] = wv_ref[...]

    rows = x_ref.shape[0]
    acc = jnp.zeros((rows, 2 * HD), F32)
    squares = jnp.zeros((rows, HD), F32)
    for start in range(0, depth, chunk):
        x = x_ref[:, start : start + chunk].astype(F32)
        sq = x * x
        for part in range(0, chunk, HD):
            squares = squares + sq[:, part : part + HD]
        y = (x * gain_ref[:, start : start + chunk]).astype(BF16)
        acc = acc + dot(y, w_ref[start : start + chunk, :])
    scale = lax.rsqrt(jnp.sum(squares, axis=1, keepdims=True) * (1.0 / depth) + EPS)
    acc = acc * scale
    k_ref[...] = head_norm(acc[:, :HD], kgain_ref[...])
    v_ref[...] = acc[:, HD:].astype(BF16)


def project(rows, gain, wk, wv, kgain):
    count, depth = rows.shape
    tile = 256
    return pl.pallas_call(
        project_kernel,
        grid=(count // tile,),
        in_specs=[
            pl.BlockSpec((tile, depth), lambda i: (i, 0)),
            pl.BlockSpec((1, depth), lambda i: (0, 0)),
            pl.BlockSpec((depth, HD), lambda i: (0, 0)),
            pl.BlockSpec((depth, HD), lambda i: (0, 0)),
            pl.BlockSpec((1, HD), lambda i: (0, 0)),
        ],
        out_specs=[
            pl.BlockSpec((tile, HD), lambda i: (i, 0)),
            pl.BlockSpec((tile, HD), lambda i: (i, 0)),
        ],
        out_shape=[
            jax.ShapeDtypeStruct((count, HD), F32),
            jax.ShapeDtypeStruct((count, HD), BF16),
        ],
        scratch_shapes=[pltpu.VMEM((depth, 2 * HD), BF16)],
        compiler_params=params(),
        cost_estimate=pl.CostEstimate(
            flops=4 * count * depth * HD, bytes_accessed=2 * count * depth, transcendentals=0
        ),
        name="project",
    )(rows, gain, wk, wv, kgain)


def pack_kernel(slot_ref, k_ref, v_ref, ang_ref, ct_ref, st_ref, perm_ref, kr_ref, out_ref):
    sign = rope_sign()
    ang = ang_ref[...]
    cb, sb = jnp.cos(ang), jnp.sin(ang)
    ct, st = ct_ref[...], st_ref[...]
    perm = perm_ref[...]
    out_ref[...] = jnp.zeros(out_ref.shape, BF16)
    for b in range(slot_ref.shape[0]):
        rows = slice(b * BLK, (b + 1) * BLK)
        c1, s1 = cb[b : b + 1], sb[b : b + 1]
        c = c1 * ct - s1 * st
        s = (s1 * ct + c1 * st) * sign
        k = k_ref[rows, :]
        kr = (k * c + pltpu.roll(k, HD // 2, 1) * s).astype(BF16)
        kr_ref[rows, :] = kr
        both = jnp.concatenate([kr, v_ref[rows, :]], axis=0)
        place = pl.multiple_of(slot_ref[b] * (2 * BLK), 2 * BLK)
        out_ref[pl.ds(place, 2 * BLK), :] = dot(perm, both).astype(BF16)


def pack(slots, keys, values, angles, ct, st, perm, slot_count):
    vmem = pl.BlockSpec(memory_space=pltpu.VMEM)
    return pl.pallas_call(
        pack_kernel,
        in_specs=[pl.BlockSpec(memory_space=pltpu.SMEM)] + [vmem] * 6,
        out_specs=[vmem, vmem],
        out_shape=[
            jax.ShapeDtypeStruct(keys.shape, BF16),
            jax.ShapeDtypeStruct((slot_count * 2 * BLK, HD), BF16),
        ],
        compiler_params=params(),
        cost_estimate=pl.CostEstimate(
            flops=40_000_000, bytes_accessed=2_500_000, transcendentals=0
        ),
        name="pack",
    )(slots, keys, values, angles, ct, st, perm)


def token_kernel(row_ref, a_ref, b_ref, res_ref, gain_ref, wk_ref, wv_ref, kgain_ref, ang_ref, out_ref):
    hidden = res_ref[...] + (a_ref[...].astype(F32) + b_ref[...].astype(F32))
    scale = lax.rsqrt(jnp.mean(hidden * hidden, axis=-1, keepdims=True) + EPS)
    normed = hidden * scale * gain_ref[...]
    wide = jnp.broadcast_to(normed, (16, normed.shape[1])).astype(BF16)
    k = head_norm(dot(wide, wk_ref[...]), kgain_ref[...])
    ang = ang_ref[...]
    k = k * jnp.cos(ang) + pltpu.roll(k, HD // 2, 1) * (jnp.sin(ang) * rope_sign())
    v = dot(wide, wv_ref[...])
    both = jnp.concatenate([k, k, v, v], axis=0)
    row = lax.broadcasted_iota(jnp.int32, both.shape, 0) % 32
    out_ref[...] = jnp.where(row == row_ref[0], both, 0.0).astype(BF16)


def token(row, a, b, res, gain, wk, wv, kgain, ang):
    vmem = pl.BlockSpec(memory_space=pltpu.VMEM)
    return pl.pallas_call(
        token_kernel,
        in_specs=[pl.BlockSpec(memory_space=pltpu.SMEM)] + [vmem] * 8,
        out_specs=vmem,
        out_shape=jax.ShapeDtypeStruct((64, HD), BF16),
        compiler_params=params(),
        cost_estimate=pl.CostEstimate(
            flops=50_000_000, bytes_accessed=3_000_000, transcendentals=0
        ),
        name="token",
    )(row, a, b, res, gain, wk, wv, kgain, ang)


def put_stats(ref, c, total):
    hi = total.astype(BF16).astype(F32)
    stats = jnp.concatenate([c, hi, total - hi, jnp.zeros((10, HD), F32)], axis=0)
    ref[STAT:TOK, :] = stats.astype(BF16)


def attend_kernel(
    limit_ref, q_ref, qgain_ref, ang_ref, kr_ref, v_ref, cache_ref, owner_ref, tok_ref,
    out_ref, qr_ref, q_scr, s_scr, o_scr,
):
    heads = q_ref.shape[1] // HD
    rows = cache_ref.shape[1]
    pairs = q_ref.shape[0]
    queries = heads * pairs
    per_row = queries // rows
    score_scale = HD ** (-0.5)
    ang = ang_ref[...]
    cd, sd = jnp.cos(ang), jnp.sin(ang) * rope_sign()
    for h in range(heads):
        x = head_norm(q_ref[:, h * HD : (h + 1) * HD].astype(F32), qgain_ref[...])
        qr = (x * cd + pltpu.roll(x, HD // 2, 1) * sd).astype(BF16)
        qr_ref[h * pairs : (h + 1) * pairs, :] = qr
        q_scr[h * pairs : (h + 1) * pairs, :] = qr.astype(F32)
    lane = lax.broadcasted_iota(jnp.int32, (per_row, HD), 1)
    for r in range(rows):
        mine = pl.ds(r, per_row, stride=rows)
        s = dot_nt(q_scr[mine, :].astype(BF16), cache_ref[0, r]) * score_scale
        s_scr[mine, :] = jnp.where(lane < limit_ref[r], s, MASKED)
    block = dot_nt(qr_ref[...], kr_ref[...]) * score_scale
    row = lax.broadcasted_iota(jnp.int32, (queries, 1), 0) % rows
    block = jnp.where(row == owner_ref[...], block, MASKED)
    cache = s_scr[...]
    top = jnp.maximum(
        jnp.max(cache, axis=1, keepdims=True), jnp.max(block, axis=1, keepdims=True)
    )
    c = jnp.maximum(top, FLOOR).astype(BF16).astype(F32)
    cache = jnp.exp(cache - c)
    block = jnp.exp(block - c)
    total = jnp.sum(cache, axis=1, keepdims=True) + jnp.sum(block, axis=1, keepdims=True)
    s_scr[...] = cache
    for r in range(rows):
        mine = pl.ds(r, per_row, stride=rows)
        o_scr[mine, :] = dot(s_scr[mine, :].astype(BF16), cache_ref[1, r])
    out_ref[:STAT, :] = (dot(block.astype(BF16), v_ref[...]) + o_scr[...]).astype(BF16)
    lane = lax.broadcasted_iota(jnp.int32, (queries, HD), 1)
    both = jnp.where(lane == 0, c, jnp.where(lane == 1, total, 0.0))
    t0, t1 = both[:HD].T, both[HD:].T
    put_stats(
        out_ref,
        jnp.concatenate([t0[0:1], t1[0:1]], axis=0),
        jnp.concatenate([t0[1:2], t1[1:2]], axis=0),
    )
    out_ref[TOK:, :] = tok_ref[...]


def attend(limit, q, qgain, ang, kr, v, cache, owner, tok):
    vmem = pl.BlockSpec(memory_space=pltpu.VMEM)
    return pl.pallas_call(
        attend_kernel,
        in_specs=[pl.BlockSpec(memory_space=pltpu.SMEM)] + [vmem] * 8,
        out_specs=[vmem, vmem],
        out_shape=[
            jax.ShapeDtypeStruct((ROWS, HD), BF16),
            jax.ShapeDtypeStruct((STAT, HD), BF16),
        ],
        scratch_shapes=[pltpu.VMEM((STAT, HD), F32)] * 3,
        compiler_params=params(),
        cost_estimate=pl.CostEstimate(
            flops=400_000_000, bytes_accessed=3_000_000, transcendentals=300_000
        ),
        name="attend",
    )(limit, q, qgain, ang, kr, v, cache, owner, tok)


def merged(refs):
    cs = [ref[STAT : STAT + 2, :].astype(F32) for ref in refs]
    top = functools.reduce(jnp.maximum, cs)
    factors = [jnp.exp(c - top) for c in cs]
    total = jnp.zeros_like(top)
    for ref, f in zip(refs, factors):
        stats = ref[STAT:TOK, :].astype(F32)
        total = total + f * (stats[2:4] + stats[4:6])
    pad = jnp.zeros((HD - 2 * len(refs), HD), F32)
    cols = jnp.concatenate(factors + [pad], axis=0).T
    halves = []
    for g in range(2):
        acc = None
        for i, ref in enumerate(refs):
            term = ref[g * HD : (g + 1) * HD, :].astype(F32) * cols[:, 2 * i + g : 2 * i + g + 1]
            acc = term if acc is None else acc + term
        halves.append(acc)
    tok = functools.reduce(lambda a, b: a + b, [ref[TOK:, :].astype(F32) for ref in refs])
    return halves, top, total, tok


def merge_kernel(*refs):
    out_ref = refs[-1]
    halves, top, total, tok = merged(refs[:-1])
    for g in range(2):
        out_ref[g * HD : (g + 1) * HD, :] = halves[g].astype(BF16)
    put_stats(out_ref, top, total)
    out_ref[TOK:, :] = tok.astype(BF16)


def merge(parts):
    vmem = pl.BlockSpec(memory_space=pltpu.VMEM)
    return pl.pallas_call(
        merge_kernel,
        in_specs=[vmem] * len(parts),
        out_specs=vmem,
        out_shape=jax.ShapeDtypeStruct((ROWS, HD), BF16),
        compiler_params=params(),
        name="merge",
    )(*parts)


def final_kernel(qr_ref, perm_ref, *refs):
    out_ref, tok_out_ref = refs[-2:]
    halves, top, total, tok = merged(refs[:-2])
    tok = tok.astype(BF16)
    tok_out_ref[...] = dot(perm_ref[...], tok).astype(BF16)
    new_k, new_v = tok[:32], tok[32:]
    pad = jnp.zeros((HD - 4, HD), F32)
    cols = jnp.concatenate([top, total, pad], axis=0).T
    col = lax.broadcasted_iota(jnp.int32, (HD, 32), 1)
    row = lax.broadcasted_iota(jnp.int32, (HD, 32), 0)
    same = (col % 16 == row % 16) & (col // 16 <= (row // 16) % 2)
    for g in range(2):
        s = dot_nt(qr_ref[g * HD : (g + 1) * HD, :], new_k) * (HD ** (-0.5))
        s = jnp.where(same, s, MASKED)
        c, old = cols[:, g : g + 1], cols[:, 2 + g : 3 + g]
        m = jnp.maximum(c, jnp.max(s, axis=1, keepdims=True))
        f = jnp.exp(c - m)
        p = jnp.exp(s - m)
        whole = old * f + jnp.sum(p, axis=1, keepdims=True)
        o = ((halves[g] * f + dot(p.astype(BF16), new_v)) / whole).astype(BF16)
        for h in range(4):
            head = g * 4 + h
            out_ref[:, head * HD : (head + 1) * HD] = o[h * 32 : (h + 1) * 32]


def final(qr, perm, parts):
    vmem = pl.BlockSpec(memory_space=pltpu.VMEM)
    return pl.pallas_call(
        final_kernel,
        in_specs=[vmem] * (2 + len(parts)),
        out_specs=[vmem, vmem],
        out_shape=[
            jax.ShapeDtypeStruct((32, 8 * HD), BF16),
            jax.ShapeDtypeStruct((64, HD), BF16),
        ],
        compiler_params=params(),
        name="final",
    )(qr, perm, *parts)


Y_STEPS, Z_STEPS, X_STEPS = (1, 2, 3), (4,), (8, 16, 24)


def exchange(value, axis, steps):
    size = lax.axis_size(axis)
    return [lax.ppermute(value, axis, [(i, i ^ m) for i in range(size)]) for m in steps]


def local(
    prefill_rows,
    in_gain,
    key_weight,
    value_weight,
    key_gain,
    query_gain,
    block_request,
    block_target,
    context_lengths,
    kv_cache,
    decode_queries,
    decode_partials,
    decode_residual,
):
    me = lax.axis_index("wide")
    wide_count = lax.axis_size("wide")
    depth = prefill_rows.shape[1]
    row_count = context_lengths.shape[0]
    slot_count = kv_cache.shape[2]

    frequency = np.tile(THETA ** (-np.arange(HD // 2) / (HD // 2)), 2)
    offsets = np.arange(BLK)[:, None] * frequency[None, :]
    ct = jnp.asarray(np.cos(offsets), F32)
    st = jnp.asarray(np.sin(offsets), F32)
    freq = jnp.asarray(frequency, F32)
    perm_np = np.zeros((2 * BLK, 2 * BLK), np.float32)
    for i in range(BLK):
        perm_np[2 * i, i] = 1
        perm_np[2 * i + 1, BLK + i] = 1
    perm = jnp.asarray(perm_np, BF16)

    requests = jnp.arange(row_count, dtype=jnp.int32)
    owned = (block_request[:, None] == requests[None, :]).astype(jnp.int32)
    total = jnp.sum(owned, axis=0)
    ahead = jnp.zeros_like(total)
    for steps in (Y_STEPS, Z_STEPS, X_STEPS):
        others = exchange(total, "wide", steps)
        for m, other in zip(steps, others):
            ahead = ahead + jnp.where((me ^ m) < me, other, 0)
            total = total + other

    token_index, request_index = me // row_count, me % row_count
    part = lax.dynamic_slice(
        decode_partials, (0, token_index, request_index, 0), (1, 1, 1, depth)
    ).reshape(1, depth)
    part = part.astype(BF16)
    for m in (1, 2):
        (other,) = exchange(part, "kvh", (m,))
        part = (part.astype(F32) + other.astype(F32)).astype(BF16)
    (other,) = exchange(part, "kvh", (4,))
    residual = lax.dynamic_slice(
        decode_residual, (token_index, request_index, 0), (1, 1, depth)
    ).reshape(1, depth)

    keys, values = project(
        prefill_rows, in_gain.reshape(1, depth), key_weight, value_weight, key_gain.reshape(1, HD)
    )

    earlier = jnp.arange(BLK)[None, :] < jnp.arange(BLK)[:, None]
    rank = jnp.sum((block_request[:, None] == block_request[None, :]) & earlier, axis=1)
    start = jnp.sum(owned * (context_lengths + BLK * ahead)[None, :], axis=1) + BLK * rank
    angles = start.astype(F32)[:, None] * freq[None, :]
    target = block_target[:, 0]
    target_rank = jnp.sum((target[:, None] == target[None, :]) & earlier, axis=1)
    slots = (target * CAP + target_rank).astype(jnp.int32)
    decode_pos = (context_lengths + BLK * total)[None, :] + jnp.arange(2, dtype=jnp.int32)[:, None]
    decode_angles = decode_pos.reshape(-1).astype(F32)[:, None] * freq[None, :]
    my_angle = (
        jnp.sum(jnp.where(requests == request_index, context_lengths + BLK * total, 0))
        + token_index
    ).astype(F32) * freq[None, :]

    rotated, outgoing = pack(slots, keys, values, angles, ct, st, perm, wide_count * CAP)
    received = lax.all_to_all(
        outgoing.reshape(wide_count, CAP * 2 * BLK, HD),
        "wide",
        split_axis=0,
        concat_axis=0,
        tiled=True,
    )
    new_blocks = received.reshape(wide_count * CAP, BLK, 2, HD)

    tok = token(
        me.astype(jnp.int32).reshape(1), part, other, residual, in_gain.reshape(1, depth),
        key_weight, value_weight, key_gain.reshape(1, HD), my_angle,
    )
    limit = context_lengths - me * slot_count
    owner = jnp.repeat(block_request, BLK).reshape(1, -1)
    payload, queries = attend(
        limit, decode_queries.reshape(2 * row_count, -1), query_gain.reshape(1, HD), decode_angles,
        rotated, values, kv_cache, owner, tok,
    )
    payload = merge([payload] + exchange(payload, "wide", Y_STEPS))
    payload = merge([payload] + exchange(payload, "wide", Z_STEPS))
    attended, tokens = final(queries, perm, [payload] + exchange(payload, "wide", X_STEPS))
    return (
        attended.reshape(2, row_count, -1),
        new_blocks,
        tokens.reshape(2, row_count, 2, HD),
    )


def solution(mesh):
    placed = (
        P("wide", None),
        P(),
        P(None, "kvh"),
        P(None, "kvh"),
        P(),
        P(),
        P("wide"),
        P("wide", None),
        P(),
        P(None, None, "wide", "kvh"),
        P(None, None, "kvh"),
        P("kvh", None, None, None),
        P(),
    )
    return jax.shard_map(
        local,
        mesh=mesh,
        in_specs=placed,
        out_specs=(P(None, None, "kvh"), P("wide", None, None, "kvh"), P(None, None, None, "kvh")),
        check_vma=False,
    )
```

time: 719 us -> 120 us (0.17); the launches traced: 710 us -> 118 us
  blocking collectives: 311 us -> 0 us
  waiting for transfers between devices: 312 us -> 41.1 us
  starting transfers between devices: 4.14 us -> 38.4 us
  matrix products: 23.4 us -> 0 us
  other arithmetic: 26.5 us -> 7.76 us
  between operations: 15.2 us -> 1.52 us
  Pallas kernels: 0 us -> 12.8 us
    psum x2 -> x0, waiting for transfers between devices: 309 us -> none  [the longest x1 305 us: local(): lax.psum((weighted * factor[..., None]).astype(jnp.bfloat16), 'wide')]
    pmax x1 -> x0, blocking collectives: 192 us -> none  [local(): global_top = lax.pmax(row_top, 'wide')]
    psum x1 -> x0, blocking collectives: 96 us -> none  [local(): lax.psum((row_total * factor).astype(jnp.bfloat16), 'wide')]
    ppermute x0 -> x17, waiting for transfers between devices: none -> 41.1 us  [exchange(): lax.ppermute(value, axis, [(i, i ^ m) for i in range(size)])]
    ppermute x0 -> x17, starting transfers between devices: none -> 28.6 us  [exchange(): lax.ppermute(value, axis, [(i, i ^ m) for i in range(size)])]
    dot_general x10 -> x0, matrix products: 23.4 us -> none  [the longest x1 8.11 us: local(): jnp.dot(normed, value_weight, preferred_element_type=jnp.float32)]
    unnamed x1 -> x0, blocking collectives: 22.2 us -> none
    pallas_call x0 -> x7, Pallas kernels: none -> 12.8 us  [the longest x1 7.24 us: project(): pl.pallas_call(project_kernel, grid=(count // tile,), in_specs=[pl.BlockS...]
  transfers between devices with their start and end apart: 3 -> 18, of which waited for: 3 -> 10; matrix products, arithmetic and copies ran while one was open for 7% -> 10% of each run, Pallas kernels for 0% -> 11%
where the time goes in v1:
time: 120 us; the launch traced here: 118 us
  waiting for transfers between devices  41.1 us (34%)
  starting transfers between devices  38.4 us (32%)
  local copies, waits for them, and re-layouts  16.6 us (14%)
  Pallas kernels  12.8 us (11%)
  other arithmetic  7.76 us (6%)
  between operations  1.52 us (1%)
    ppermute x17, waiting for transfers between devices, exchange(): lax.ppermute(value, axis, [(i, i ^ m) for i in range(size)])  41.1 us
    ppermute x17, starting transfers between devices, exchange(): lax.ppermute(value, axis, [(i, i ^ m) for i in range(size)])  28.6 us
    unnamed x51, local copies, waits for them, and re-layouts  11.6 us
    all_to_all x1, starting transfers between devices, local(): lax.all_to_all(outgoing.reshape(wide_count, CAP * 2 * BLK, HD), 'wide', s...  9.76 us
    pallas_call x1, Pallas kernels, project(): pl.pallas_call(project_kernel, grid=(count // tile,), in_specs=[pl.BlockS...  7.24 us
  transfers between devices with their start and end apart: 18, of which 10 were waited for; matrix products, arithmetic and copies ran while one was open for 10% of the time, Pallas kernels for 11%

profile of v1, /device:TPU:1, one launch (start us, length us, event | category | flops | bytes accessed | tf_op | source)
XLA Modules:
  0.0 118.2 jit_solution(13922814350135157659)
XLA Ops:
  0.6 0.0 copy-start
  0.6 0.8 convert_reduce_fusion.2
  1.5 2.2 %collective-permute-start = (s32[16]{0:T(128)S(1)}, s32[16]{0:T(128)S(1)}, u32[]{:S(2)}, u32[]{:S(2)}) collective-permute-start(s32[16]{0:T(128)S(1)} %convert_reduce_fusion.2), channel_id=1, source_target_pairs={{0,8},{8,0},{16,24},{24,16},{32,40},{40,32},{48,56},{56,48},{64,72... | collective-permute-start | bytes 200 | tf_op jit(solution)/shard_map/ppermute | solution.py:331
  3.7 2.6 %collective-permute-start.1 = (s32[16]{0:T(128)S(1)}, s32[16]{0:T(128)S(1)}, u32[]{:S(2)}, u32[]{:S(2)}) collective-permute-start(s32[16]{0:T(128)S(1)} %convert_reduce_fusion.2), channel_id=1, source_target_pairs={{0,16},{8,24},{16,0},{24,8},{32,48},{40,56},{48,32},{56,40},{64,80... | collective-permute-start | bytes 200 | tf_op jit(solution)/shard_map/ppermute | solution.py:331
  6.3 1.5 %convert_bitcast_fusion = bf16[1,5120]{1,0:T(2,128)(2,1)} fusion(f32[1,2,16,5120]{3,2,1,0:T(8,128)} %param.28, s32[]{:T(128)S(6)} %select_n.82, s32[]{:T(128)S(6)} %select_n.84), kind=kLoop, calls=%fused_computation.3 | loop fusion | bytes 20488 | tf_op jit(solution)/shard_map/convert_element_type | solution.py:380
  7.9 3.2 %collective-permute-start.7 = (bf16[1,5120]{1,0:T(2,128)(2,1)}, bf16[1,5120]{1,0:T(2,128)(2,1)}, u32[]{:S(2)}, u32[]{:S(2)}) collective-permute-start(bf16[1,5120]{1,0:T(2,128)(2,1)} %convert_bitcast_fusion), channel_id=1, source_target_pairs={{0,1},{1,0},{2,3},{3,2},{4,5},{5,4},{6,7},{7,6},{8,9},{9,8},{10,11... | collective-permute-start | bytes 30728 | tf_op jit(solution)/shard_map/ppermute | solution.py:331
  11.0 0.9 convert_reduce_fusion
  12.0 0.9 convert_reduce_fusion.1
  12.9 0.7 multiply_add_fusion.1.slot_ref
  13.6 1.3 %copy-done.1 = bf16[5120,128]{1,0:T(8,128)(2,1)S(1)} copy-done((bf16[5120,128]{1,0:T(8,128)(2,1)S(1)}, bf16[5120,128]{1,0:T(8,128)(2,1)}, u32[]{:S(2)}) %copy-start.1) | copy-done | bytes 1310744
  14.9 1.3 %copy-done.3 = bf16[5120,128]{1,0:T(8,128)(2,1)S(1)} copy-done((bf16[5120,128]{1,0:T(8,128)(2,1)S(1)}, bf16[5120,128]{1,0:T(8,128)(2,1)}, u32[]{:S(2)}) %copy-start.3) | copy-done | bytes 1310744
  16.2 0.7 copy-done.9
  16.9 0.7 copy-done.19
  17.6 0.0 copy-start.16
  17.6 0.0 copy-start.17
  17.6 7.2 %project.1 = (f32[1024,128]{1,0:T(8,128)S(1)}, bf16[1024,128]{1,0:T(8,128)(2,1)S(1)}) custom-call(bf16[1024,5120]{1,0:T(8,128)(2,1)} %x_ref.1, f32[1,5120]{1,0:T(1,128)S(1)} %bitcast.20, bf16[5120,128]{1,0:T(8,128)(2,1)S(1)} %copy-done.1, bf16[5120,128]{1,0:T(8,128)(2,1)S(1)} %copy-done.3, f32[1,128]{1,0:T(1,128)S(1)} %bitcast.23), custom_call_target="tpu_custom_call" | custom-call | flops 2684354560 | bytes 10485760 | tf_op jit(solution)/shard_map/project/pallas_call | solution.py:76
  24.9 5.3 %collective-permute-start.3 = (s32[16]{0:T(128)S(1)}, s32[16]{0:T(128)S(1)}, u32[]{:S(2)}, u32[]{:S(2)}) collective-permute-start(s32[16]{0:T(128)S(1)} %add_add_fusion), channel_id=1, source_target_pairs={{0,32},{8,40},{16,48},{24,56},{32,0},{40,8},{48,16},{56,24},{64,96... | collective-permute-start | bytes 200 | tf_op jit(solution)/shard_map/ppermute | solution.py:331
  30.2 1.1 collective-permute-done.3
  31.3 1.0 collective-permute-start.4
  32.3 2.4 %collective-permute-start.5 = (s32[16]{0:T(128)S(1)}, s32[16]{0:T(128)S(1)}, u32[]{:S(2)}, u32[]{:S(2)}) collective-permute-start(s32[16]{0:T(128)S(1)} %add.100), channel_id=1, source_target_pairs={{0,128},{8,136},{16,144},{24,152},{32,160},{40,168},{48,176},{56,1... | collective-permute-start | bytes 200 | tf_op jit(solution)/shard_map/ppermute | solution.py:331
  34.8 0.4 collective-permute-start.6
  35.2 1.1 collective-permute-done.5
  36.2 2.2 %collective-permute-done.6 = s32[16]{0:T(128)S(1)} collective-permute-done((s32[16]{0:T(128)S(1)}, s32[16]{0:T(128)S(1)}, u32[]{:S(2)}, u32[]{:S(2)}) %collective-permute-start.6) | collective-permute-done | bytes 96 | tf_op jit(solution)/shard_map/ppermute | solution.py:331
  38.4 1.2 %fusion.8 = (s32[]{:T(128)}, s32[16]{0:T(128)S(1)}, s32[16]{0:T(128)S(1)}, s32[16]{0:T(128)}) fusion(s32[]{:T(128)S(6)} %select_n.83, s32[16]{0:T(128)S(1)} %copy-done.23, s32[16]{0:T(128)S(1)} %collective-permute-done.6, s32[16]{0:T(128)S(1)} %collective-permute-done.5, s32[16]{0:T(128)S(1)} %add.100, s32[16]{0:T(128)S(1)} %collective-permute-done.4, ...), kind=kLoop, calls=%fused_computation.29 | loop fusion | flops 383 | bytes 787 | tf_op jit(solution)/shard_map/reduce_sum | solution.py:403
  39.6 0.1 select_reduce_fusion
  39.7 0.1 convert_element_type.75
  39.8 0.1 broadcast_multiply_fusion
  39.9 1.1 pack.1
  41.0 1.0 copy-done.6
  42.0 0.7 copy-done.7
  42.7 9.8 %all-to-all-start = ((bf16[32,128,128]{2,1,0:T(8,128)(2,1)}), bf16[32,128,128]{2,1,0:T(8,128)(2,1)}, u32[]{:S(2)}, u32[]{:S(2)}) async-start(bf16[32,128,128]{2,1,0:T(8,128)(2,1)} %bitcast.19), calls=%async_computation | async-start | bytes 2097152 | tf_op jit(solution)/shard_map/all_to_all | solution.py:408
  52.5 1.6 %add_convert_fusion.1 = bf16[1,5120]{1,0:T(2,128)(2,1)} fusion(bf16[1,5120]{1,0:T(2,128)(2,1)} %collective-permute-done.7, f32[1,2,16,5120]{3,2,1,0:T(8,128)} %param.28, s32[]{:T(128)S(6)} %select_n.82, s32[]{:T(128)S(6)} %select_n.84), kind=kLoop, calls=%fused_computation.2 | loop fusion | flops 20480 | bytes 30728 | tf_op jit(solution)/shard_map/convert_element_type | solution.py:383
  54.1 0.7 collective-permute-start.8
  54.8 0.6 dynamic-slice_bitcast_fusion.res_ref
  55.4 1.3 %eq.53 = s32[32,32]{1,0:T(8,128)} broadcast(s32[32]{0:T(128)} %param.23), dimensions={0} | broadcast | bytes 4224 | tf_op jit(solution)/shard_map/eq | solution.py:394
  56.8 1.4 %reshape_reshape.3.owner_ref = s32[1,1024]{1,0:T(1,128)} reshape(s32[32,32]{1,0:T(8,128)} %eq.53) | data formatting | bytes 8192 | tf_op jit(solution)/shard_map/reshape;reshape | solution.py:422
  58.8 17.5 %collective-permute-done.8 = bf16[1,5120]{1,0:T(2,128)(2,1)} collective-permute-done((bf16[1,5120]{1,0:T(2,128)(2,1)}, bf16[1,5120]{1,0:T(2,128)(2,1)}, u32[]{:S(2)}, u32[]{:S(2)}) %collective-permute-start.8) | collective-permute-done | bytes 10272 | tf_op jit(solution)/shard_map/ppermute | solution.py:331
  76.2 0.8 add_convert_fusion.a_ref
  77.0 0.1 collective-permute-start.9
  77.1 0.7 multiply_bitcast_fusion.ang_ref
  77.8 4.5 %collective-permute-done.9.b_ref = bf16[1,5120]{1,0:T(2,128)(2,1)S(1)} collective-permute-done((bf16[1,5120]{1,0:T(2,128)(2,1)S(1)}, bf16[1,5120]{1,0:T(2,128)(2,1)S(1)}, u32[]{:S(2)}, u32[]{:S(2)}) %collective-permute-start.9) | collective-permute-done | bytes 10272 | tf_op jit(solution)/shard_map/ppermute | solution.py:331
  82.3 0.7 copy-done.10
  83.0 0.7 copy-done.11
  83.8 0.7 copy-done.20
  84.4 0.6 token_.1.tok_ref
  85.0 0.6 copy-done.5
  85.6 0.0 copy-done.8
  85.7 1.9 %attend.1 = (bf16[336,128]{1,0:T(8,128)(2,1)S(1)}, bf16[256,128]{1,0:T(8,128)(2,1)S(1)}) custom-call(s32[16]{0:T(128)S(1)} %copy-done.18, bf16[32,1024]{1,0:T(8,128)(2,1)S(1)} %bitcast.22, f32[1,128]{1,0:T(1,128)S(1)} %bitcast.25, f32[32,128]{1,0:T(8,128)S(1)} %get-tuple-element.23.ang_ref, bf16[1024,128]{1,0:T(8,128)(2,1)S(1)} %copy-done.8, ...), custom_call_target="tpu_custom_call" | custom-call | flops 400000000 | bytes 3000000 | tf_op jit(solution)/shard_map/attend/pallas_call | solution.py:227
  87.6 1.4 %collective-permute-start.10 = (bf16[336,128]{1,0:T(8,128)(2,1)S(1)}, bf16[336,128]{1,0:T(8,128)(2,1)S(1)}, u32[]{:S(2)}, u32[]{:S(2)}) collective-permute-start(bf16[336,128]{1,0:T(8,128)(2,1)S(1)} %get-tuple-element.15.refs_0_), channel_id=1, source_target_pairs={{0,8},{8,0},{16,24},{24,16},{32,40},{40,32},{48,56},{56,48},{64,72... | collective-permute-start | bytes 258056 | tf_op jit(solution)/shard_map/ppermute | solution.py:331
  89.0 2.0 %collective-permute-start.11 = (bf16[336,128]{1,0:T(8,128)(2,1)S(1)}, bf16[336,128]{1,0:T(8,128)(2,1)S(1)}, u32[]{:S(2)}, u32[]{:S(2)}) collective-permute-start(bf16[336,128]{1,0:T(8,128)(2,1)S(1)} %get-tuple-element.15.refs_0_), channel_id=1, source_target_pairs={{0,16},{8,24},{16,0},{24,8},{32,48},{40,56},{48,32},{56,40},{64,80... | collective-permute-start | bytes 258056 | tf_op jit(solution)/shard_map/ppermute | solution.py:331
  91.0 0.6 collective-permute-start.12
  91.5 2.3 %collective-permute-done.11.refs_2_ = bf16[336,128]{1,0:T(8,128)(2,1)S(1)} collective-permute-done((bf16[336,128]{1,0:T(8,128)(2,1)S(1)}, bf16[336,128]{1,0:T(8,128)(2,1)S(1)}, u32[]{:S(2)}, u32[]{:S(2)}) %collective-permute-start.11) | collective-permute-done | bytes 86048 | tf_op jit(solution)/shard_map/ppermute | solution.py:331
  93.8 2.6 %collective-permute-done.12.refs_3_ = bf16[336,128]{1,0:T(8,128)(2,1)S(1)} collective-permute-done((bf16[336,128]{1,0:T(8,128)(2,1)S(1)}, bf16[336,128]{1,0:T(8,128)(2,1)S(1)}, u32[]{:S(2)}, u32[]{:S(2)}) %collective-permute-start.12) | collective-permute-done | bytes 86048 | tf_op jit(solution)/shard_map/ppermute | solution.py:331
  96.4 0.3 merge.2.refs_0_
  96.8 2.7 %collective-permute-start.13 = (bf16[336,128]{1,0:T(8,128)(2,1)S(1)}, bf16[336,128]{1,0:T(8,128)(2,1)S(1)}, u32[]{:S(2)}, u32[]{:S(2)}) collective-permute-start(bf16[336,128]{1,0:T(8,128)(2,1)S(1)} %merge.2.refs_0_), channel_id=1, source_target_pairs={{0,32},{8,40},{16,48},{24,56},{32,0},{40,8},{48,16},{56,24},{64,96... | collective-permute-start | bytes 258056 | tf_op jit(solution)/shard_map/ppermute | solution.py:331
  99.5 5.6 %collective-permute-done.13.refs_1_ = bf16[336,128]{1,0:T(8,128)(2,1)S(1)} collective-permute-done((bf16[336,128]{1,0:T(8,128)(2,1)S(1)}, bf16[336,128]{1,0:T(8,128)(2,1)S(1)}, u32[]{:S(2)}, u32[]{:S(2)}) %collective-permute-start.13) | collective-permute-done | bytes 86048 | tf_op jit(solution)/shard_map/ppermute | solution.py:331
  105.1 0.3 merge.3.refs_0_
  105.4 1.3 %collective-permute-start.14 = (bf16[336,128]{1,0:T(8,128)(2,1)S(1)}, bf16[336,128]{1,0:T(8,128)(2,1)S(1)}, u32[]{:S(2)}, u32[]{:S(2)}) collective-permute-start(bf16[336,128]{1,0:T(8,128)(2,1)S(1)} %merge.3.refs_0_), channel_id=1, source_target_pairs={{0,64},{8,72},{16,80},{24,88},{32,96},{40,104},{48,112},{56,120},{... | collective-permute-start | bytes 258056 | tf_op jit(solution)/shard_map/ppermute | solution.py:331
  106.7 2.4 %collective-permute-start.15 = (bf16[336,128]{1,0:T(8,128)(2,1)S(1)}, bf16[336,128]{1,0:T(8,128)(2,1)S(1)}, u32[]{:S(2)}, u32[]{:S(2)}) collective-permute-start(bf16[336,128]{1,0:T(8,128)(2,1)S(1)} %merge.3.refs_0_), channel_id=1, source_target_pairs={{0,128},{8,136},{16,144},{24,152},{32,160},{40,168},{48,176},{56,1... | collective-permute-start | bytes 258056 | tf_op jit(solution)/shard_map/ppermute | solution.py:331
  109.1 0.2 collective-permute-start.16
  109.3 2.5 %collective-permute-done.15.refs_2_ = bf16[336,128]{1,0:T(8,128)(2,1)S(1)} collective-permute-done((bf16[336,128]{1,0:T(8,128)(2,1)S(1)}, bf16[336,128]{1,0:T(8,128)(2,1)S(1)}, u32[]{:S(2)}, u32[]{:S(2)}) %collective-permute-start.15) | collective-permute-done | bytes 86048 | tf_op jit(solution)/shard_map/ppermute | solution.py:331
  111.9 1.8 %collective-permute-done.16.refs_3_ = bf16[336,128]{1,0:T(8,128)(2,1)S(1)} collective-permute-done((bf16[336,128]{1,0:T(8,128)(2,1)S(1)}, bf16[336,128]{1,0:T(8,128)(2,1)S(1)}, u32[]{:S(2)}, u32[]{:S(2)}) %collective-permute-start.16) | collective-permute-done | bytes 86048 | tf_op jit(solution)/shard_map/ppermute | solution.py:331
  113.6 1.4 %final.1 = (bf16[32,1024]{1,0:T(8,128)(2,1)}, bf16[64,128]{1,0:T(8,128)(2,1)}) custom-call(bf16[256,128]{1,0:T(8,128)(2,1)S(1)} %get-tuple-element.14.qr_ref, bf16[64,64]{1,0:T(8,128)(2,1)S(1)} %copy-done.14, bf16[336,128]{1,0:T(8,128)(2,1)S(1)} %merge.3.refs_0_, bf16[336,128]{1,0:T(8,128)(2,1)S(1)} %collective-permute-done.14.refs_1_, ...), custom_call_target="tpu_custom_call" | custom-call | tf_op jit(solution)/shard_map/final/pallas_call | solution.py:313
  115.1 3.1 %copy.21 = bf16[64,32,2,128]{3,2,1,0:T(2,128)(2,1)} copy(bf16[64,32,2,128]{3,2,1,0:T(2,128)(2,1)} %bitcast.11) | data formatting | bytes 2097152
  (49 shorter events, 0.1 us)
Async XLA Ops:
  0.6 54.2 %copy-start = (f32[2,16,5120]{2,1,0:T(8,128)S(1)}, f32[2,16,5120]{2,1,0:T(8,128)}, u32[]{:S(2)}) copy-start(f32[2,16,5120]{2,1,0:T(8,128)} %param.29) | copy-start | bytes 1966084
  1.5 23.4 %collective-permute-start = (s32[16]{0:T(128)S(1)}, s32[16]{0:T(128)S(1)}, u32[]{:S(2)}, u32[]{:S(2)}) collective-permute-start(s32[16]{0:T(128)S(1)} %convert_reduce_fusion.2), channel_id=1, source_target_pairs={{0,8},{8,0},{16,24},{24,16},{32,40},{40,32},{48,56},{56,48},{64,72... | collective-permute-start | bytes 200 | tf_op jit(solution)/shard_map/ppermute | solution.py:331
  3.7 21.2 %collective-permute-start.1 = (s32[16]{0:T(128)S(1)}, s32[16]{0:T(128)S(1)}, u32[]{:S(2)}, u32[]{:S(2)}) collective-permute-start(s32[16]{0:T(128)S(1)} %convert_reduce_fusion.2), channel_id=1, source_target_pairs={{0,16},{8,24},{16,0},{24,8},{32,48},{40,56},{48,32},{56,40},{64,80... | collective-permute-start | bytes 200 | tf_op jit(solution)/shard_map/ppermute | solution.py:331
  6.3 18.6 %collective-permute-start.2 = (s32[16]{0:T(128)S(1)}, s32[16]{0:T(128)S(1)}, u32[]{:S(2)}, u32[]{:S(2)}) collective-permute-start(s32[16]{0:T(128)S(1)} %convert_reduce_fusion.2), channel_id=1, source_target_pairs={{0,24},{8,16},{16,8},{24,0},{32,56},{40,48},{48,40},{56,32},{64,88... | collective-permute-start | bytes 200 | tf_op jit(solution)/shard_map/ppermute | solution.py:331
  7.9 44.6 %collective-permute-start.7 = (bf16[1,5120]{1,0:T(2,128)(2,1)}, bf16[1,5120]{1,0:T(2,128)(2,1)}, u32[]{:S(2)}, u32[]{:S(2)}) collective-permute-start(bf16[1,5120]{1,0:T(2,128)(2,1)} %convert_bitcast_fusion), channel_id=1, source_target_pairs={{0,1},{1,0},{2,3},{3,2},{4,5},{5,4},{6,7},{7,6},{8,9},{9,8},{10,11... | collective-permute-start | bytes 30728 | tf_op jit(solution)/shard_map/ppermute | solution.py:331
  13.5 1.3 %copy-start.1 = (bf16[5120,128]{1,0:T(8,128)(2,1)S(1)}, bf16[5120,128]{1,0:T(8,128)(2,1)}, u32[]{:S(2)}) copy-start(bf16[5120,128]{1,0:T(8,128)(2,1)} %wk_ref.3) | copy-start | bytes 3932164
  14.9 1.3 %copy-start.3 = (bf16[5120,128]{1,0:T(8,128)(2,1)S(1)}, bf16[5120,128]{1,0:T(8,128)(2,1)}, u32[]{:S(2)}) copy-start(bf16[5120,128]{1,0:T(8,128)(2,1)} %wv_ref.3) | copy-start | bytes 3932164
  16.2 0.7 copy-start.9
  16.9 0.7 copy-start.19
  17.6 20.8 %copy-start.23 = (s32[16]{0:T(128)S(1)}, s32[16]{0:T(128)}, u32[]{:S(2)}) copy-start(s32[16]{0:T(128)} %param.25) | copy-start | bytes 196
  17.6 22.1 %copy-start.24 = (s32[32]{0:T(128)S(1)}, s32[32]{0:T(128)}, u32[]{:S(2)}) copy-start(s32[32]{0:T(128)} %param.23) | copy-start | bytes 388
  17.6 22.2 %copy-start.22 = (f32[128]{0:T(128)S(1)}, f32[128]{0:T(128)}, u32[]{:S(2)}) copy-start(f32[128]{0:T(128)} %constant.60.clone) | copy-start | bytes 1540
  17.6 22.3 %copy-start.13 = (bf16[64,64]{1,0:T(8,128)(2,1)S(1)}, bf16[64,64]{1,0:T(8,128)(2,1)}, u32[]{:S(2)}) copy-start(bf16[64,64]{1,0:T(8,128)(2,1)} %constant.61.clone.perm_ref) | copy-start | bytes 24580
  17.6 22.3 %copy-start.16 = (f32[32,128]{1,0:T(8,128)S(1)}, f32[32,128]{1,0:T(8,128)}, u32[]{:S(2)}) copy-start(f32[32,128]{1,0:T(8,128)} %constant.58.clone.ct_ref) | copy-start | bytes 49156
  17.6 22.3 %copy-start.17 = (f32[32,128]{1,0:T(8,128)S(1)}, f32[32,128]{1,0:T(8,128)}, u32[]{:S(2)}) copy-start(f32[32,128]{1,0:T(8,128)} %constant.59.clone.st_ref) | copy-start | bytes 49156
  24.9 6.4 %collective-permute-start.3 = (s32[16]{0:T(128)S(1)}, s32[16]{0:T(128)S(1)}, u32[]{:S(2)}, u32[]{:S(2)}) collective-permute-start(s32[16]{0:T(128)S(1)} %add_add_fusion), channel_id=1, source_target_pairs={{0,32},{8,40},{16,48},{24,56},{32,0},{40,8},{48,16},{56,24},{64,96... | collective-permute-start | bytes 200 | tf_op jit(solution)/shard_map/ppermute | solution.py:331
  31.3 3.9 %collective-permute-start.4 = (s32[16]{0:T(128)S(1)}, s32[16]{0:T(128)S(1)}, u32[]{:S(2)}, u32[]{:S(2)}) collective-permute-start(s32[16]{0:T(128)S(1)} %add.100), channel_id=1, source_target_pairs={{0,64},{8,72},{16,80},{24,88},{32,96},{40,104},{48,112},{56,120},{... | collective-permute-start | bytes 200 | tf_op jit(solution)/shard_map/ppermute | solution.py:331
  32.3 3.9 %collective-permute-start.5 = (s32[16]{0:T(128)S(1)}, s32[16]{0:T(128)S(1)}, u32[]{:S(2)}, u32[]{:S(2)}) collective-permute-start(s32[16]{0:T(128)S(1)} %add.100), channel_id=1, source_target_pairs={{0,128},{8,136},{16,144},{24,152},{32,160},{40,168},{48,176},{56,1... | collective-permute-start | bytes 200 | tf_op jit(solution)/shard_map/ppermute | solution.py:331
  34.8 3.6 %collective-permute-start.6 = (s32[16]{0:T(128)S(1)}, s32[16]{0:T(128)S(1)}, u32[]{:S(2)}, u32[]{:S(2)}) collective-permute-start(s32[16]{0:T(128)S(1)} %add.100), channel_id=1, source_target_pairs={{0,192},{8,200},{16,208},{24,216},{32,224},{40,232},{48,240},{56,2... | collective-permute-start | bytes 200 | tf_op jit(solution)/shard_map/ppermute | solution.py:331
  39.9 42.4 %copy-start.4 = (bf16[5120,128]{1,0:T(8,128)(2,1)S(1)}, bf16[5120,128]{1,0:T(8,128)(2,1)}, u32[]{:S(2)}) copy-start(bf16[5120,128]{1,0:T(8,128)(2,1)} %wv_ref.3) | copy-start | bytes 3932164
  41.0 1.0 copy-start.6
  42.0 0.7 copy-start.7
  42.7 39.6 %copy-start.2 = (bf16[5120,128]{1,0:T(8,128)(2,1)S(1)}, bf16[5120,128]{1,0:T(8,128)(2,1)}, u32[]{:S(2)}) copy-start(bf16[5120,128]{1,0:T(8,128)(2,1)} %wk_ref.3) | copy-start | bytes 3932164
  42.7 72.3 %all-to-all-start = ((bf16[32,128,128]{2,1,0:T(8,128)(2,1)}), bf16[32,128,128]{2,1,0:T(8,128)(2,1)}, u32[]{:S(2)}, u32[]{:S(2)}) async-start(bf16[32,128,128]{2,1,0:T(8,128)(2,1)} %bitcast.19), calls=%async_computation | async-start | bytes 2097152 | tf_op jit(solution)/shard_map/all_to_all | solution.py:408
  54.1 22.2 %collective-permute-start.8 = (bf16[1,5120]{1,0:T(2,128)(2,1)}, bf16[1,5120]{1,0:T(2,128)(2,1)}, u32[]{:S(2)}, u32[]{:S(2)}) collective-permute-start(bf16[1,5120]{1,0:T(2,128)(2,1)} %add_convert_fusion.1), channel_id=1, source_target_pairs={{0,2},{1,3},{2,0},{3,1},{4,6},{5,7},{6,4},{7,5},{8,10},{9,11},{10,... | collective-permute-start | bytes 30728 | tf_op jit(solution)/shard_map/ppermute | solution.py:331
  77.0 5.3 %collective-permute-start.9 = (bf16[1,5120]{1,0:T(2,128)(2,1)S(1)}, bf16[1,5120]{1,0:T(2,128)(2,1)S(1)}, u32[]{:S(2)}, u32[]{:S(2)}) collective-permute-start(bf16[1,5120]{1,0:T(2,128)(2,1)S(1)} %add_convert_fusion.a_ref), channel_id=1, source_target_pairs={{0,4},{1,5},{2,6},{3,7},{4,0},{5,1},{6,2},{7,3},{8,12},{9,13},{10,... | collective-permute-start | bytes 30728 | tf_op jit(solution)/shard_map/ppermute | solution.py:331
  82.3 0.7 copy-start.10
  83.0 0.7 copy-start.11
  83.8 0.7 copy-start.20
  84.4 1.2 %copy-start.5 = (bf16[2,16,128,128]{3,2,1,0:T(8,128)(2,1)S(1)}, bf16[2,16,128,128]{3,2,1,0:T(8,128)(2,1)}, u32[]{:S(2)}) copy-start(bf16[2,16,128,128]{3,2,1,0:T(8,128)(2,1)} %cache_ref.1) | copy-start | bytes 3145732
  84.4 1.3 %copy-start.8 = (bf16[1024,128]{1,0:T(8,128)(2,1)S(1)}, bf16[1024,128]{1,0:T(8,128)(2,1)}, u32[]{:S(2)}) copy-start(bf16[1024,128]{1,0:T(8,128)(2,1)} %copy-done.7) | copy-start | bytes 786436
  84.4 1.3 %copy-start.12 = (bf16[2,16,1024]{2,1,0:T(8,128)(2,1)S(1)}, bf16[2,16,1024]{2,1,0:T(8,128)(2,1)}, u32[]{:S(2)}) copy-start(bf16[2,16,1024]{2,1,0:T(8,128)(2,1)} %param.27) | copy-start | bytes 196612
  84.4 1.3 %copy-start.15 = (s32[1,1024]{1,0:T(1,128)S(1)}, s32[1,1024]{1,0:T(1,128)}, u32[]{:S(2)}) copy-start(s32[1,1024]{1,0:T(1,128)} %reshape_reshape.3.owner_ref) | copy-start | bytes 12292
  84.4 1.3 %copy-start.18 = (s32[16]{0:T(128)S(1)}, s32[16]{0:T(128)}, u32[]{:S(2)}) copy-start(s32[16]{0:T(128)} %get-tuple-element.24.limit_ref) | copy-start | bytes 196
  84.4 1.3 %copy-start.21 = (f32[128]{0:T(128)S(1)}, f32[128]{0:T(128)}, u32[]{:S(2)}) copy-start(f32[128]{0:T(128)} %param.22) | copy-start | bytes 1540
  85.0 28.6 %copy-start.14 = (bf16[64,64]{1,0:T(8,128)(2,1)S(1)}, bf16[64,64]{1,0:T(8,128)(2,1)}, u32[]{:S(2)}) copy-start(bf16[64,64]{1,0:T(8,128)(2,1)} %constant.61.clone.perm_ref) | copy-start | bytes 24580
  87.6 4.0 %collective-permute-start.10 = (bf16[336,128]{1,0:T(8,128)(2,1)S(1)}, bf16[336,128]{1,0:T(8,128)(2,1)S(1)}, u32[]{:S(2)}, u32[]{:S(2)}) collective-permute-start(bf16[336,128]{1,0:T(8,128)(2,1)S(1)} %get-tuple-element.15.refs_0_), channel_id=1, source_target_pairs={{0,8},{8,0},{16,24},{24,16},{32,40},{40,32},{48,56},{56,48},{64,72... | collective-permute-start | bytes 258056 | tf_op jit(solution)/shard_map/ppermute | solution.py:331
  89.0 4.8 %collective-permute-start.11 = (bf16[336,128]{1,0:T(8,128)(2,1)S(1)}, bf16[336,128]{1,0:T(8,128)(2,1)S(1)}, u32[]{:S(2)}, u32[]{:S(2)}) collective-permute-start(bf16[336,128]{1,0:T(8,128)(2,1)S(1)} %get-tuple-element.15.refs_0_), channel_id=1, source_target_pairs={{0,16},{8,24},{16,0},{24,8},{32,48},{40,56},{48,32},{56,40},{64,80... | collective-permute-start | bytes 258056 | tf_op jit(solution)/shard_map/ppermute | solution.py:331
  91.0 5.5 %collective-permute-start.12 = (bf16[336,128]{1,0:T(8,128)(2,1)S(1)}, bf16[336,128]{1,0:T(8,128)(2,1)S(1)}, u32[]{:S(2)}, u32[]{:S(2)}) collective-permute-start(bf16[336,128]{1,0:T(8,128)(2,1)S(1)} %get-tuple-element.15.refs_0_), channel_id=1, source_target_pairs={{0,24},{8,16},{16,8},{24,0},{32,56},{40,48},{48,40},{56,32},{64,88... | collective-permute-start | bytes 258056 | tf_op jit(solution)/shard_map/ppermute | solution.py:331
  96.8 8.4 %collective-permute-start.13 = (bf16[336,128]{1,0:T(8,128)(2,1)S(1)}, bf16[336,128]{1,0:T(8,128)(2,1)S(1)}, u32[]{:S(2)}, u32[]{:S(2)}) collective-permute-start(bf16[336,128]{1,0:T(8,128)(2,1)S(1)} %merge.2.refs_0_), channel_id=1, source_target_pairs={{0,32},{8,40},{16,48},{24,56},{32,0},{40,8},{48,16},{56,24},{64,96... | collective-permute-start | bytes 258056 | tf_op jit(solution)/shard_map/ppermute | solution.py:331
  105.4 3.9 %collective-permute-start.14 = (bf16[336,128]{1,0:T(8,128)(2,1)S(1)}, bf16[336,128]{1,0:T(8,128)(2,1)S(1)}, u32[]{:S(2)}, u32[]{:S(2)}) collective-permute-start(bf16[336,128]{1,0:T(8,128)(2,1)S(1)} %merge.3.refs_0_), channel_id=1, source_target_pairs={{0,64},{8,72},{16,80},{24,88},{32,96},{40,104},{48,112},{56,120},{... | collective-permute-start | bytes 258056 | tf_op jit(solution)/shard_map/ppermute | solution.py:331
  106.7 5.2 %collective-permute-start.15 = (bf16[336,128]{1,0:T(8,128)(2,1)S(1)}, bf16[336,128]{1,0:T(8,128)(2,1)S(1)}, u32[]{:S(2)}, u32[]{:S(2)}) collective-permute-start(bf16[336,128]{1,0:T(8,128)(2,1)S(1)} %merge.3.refs_0_), channel_id=1, source_target_pairs={{0,128},{8,136},{16,144},{24,152},{32,160},{40,168},{48,176},{56,1... | collective-permute-start | bytes 258056 | tf_op jit(solution)/shard_map/ppermute | solution.py:331
  109.1 4.5 %collective-permute-start.16 = (bf16[336,128]{1,0:T(8,128)(2,1)S(1)}, bf16[336,128]{1,0:T(8,128)(2,1)S(1)}, u32[]{:S(2)}, u32[]{:S(2)}) collective-permute-start(bf16[336,128]{1,0:T(8,128)(2,1)S(1)} %merge.3.refs_0_), channel_id=1, source_target_pairs={{0,192},{8,200},{16,208},{24,216},{32,224},{40,232},{48,240},{56,2... | collective-permute-start | bytes 258056 | tf_op jit(solution)/shard_map/ppermute | solution.py:331

commit v2 on v1

v2 whole, which is shorter than its diff:
```python
import functools

import jax
import jax.numpy as jnp
import numpy as np
from jax import lax
from jax.experimental import pallas as pl
from jax.experimental.pallas import tpu as pltpu
from jax.sharding import PartitionSpec as P

CAP = 2
EPS = 1e-06
THETA = 1000000.0
MASKED = -3e38
FLOOR = -1e30
F32 = jnp.float32
BF16 = jnp.bfloat16

HD = 128
BLK = 32
STAT = 256
STAGES = ((1, 2, 3), (8, 16, 24), (4,))


def params(limit=16):
    return pltpu.CompilerParams(vmem_limit_bytes=limit * 1024 * 1024)


VMEM = pl.BlockSpec(memory_space=pltpu.VMEM)
SMEM = pl.BlockSpec(memory_space=pltpu.SMEM)
HBM = pl.BlockSpec(memory_space=pltpu.HBM)


def dot(a, b):
    return jnp.dot(a, b, preferred_element_type=F32)


def dot_nt(a, b):
    return lax.dot_general(a, b, (((1,), (1,)), ((), ())), preferred_element_type=F32)


def iota(shape, axis):
    return lax.broadcasted_iota(jnp.int32, shape, axis)


def rope_sign():
    return jnp.where(iota((1, HD), 1) < HD // 2, -1.0, 1.0).astype(F32)


def head_norm(x, gain):
    return x * lax.rsqrt(jnp.mean(x * x, axis=-1, keepdims=True) + EPS) * gain


def one_hot_rows(req_ref, scr):
    lane = iota((1, HD), 1)
    for b in range(BLK):
        scr[b : b + 1, :] = jnp.where(lane == req_ref[b], 1.0, 0.0)
    return scr[...]


def stay(*arrays):
    return [pltpu.with_memory_space_constraint(x, pltpu.HBM) for x in arrays]


def start_all(pairs, sems):
    copies = [pltpu.make_async_copy(src, dst, sems.at[i]) for i, (src, dst) in enumerate(pairs)]
    for copy in copies:
        copy.start()
    return copies


def wait_all(copies):
    for copy in copies:
        copy.wait()


def tile_of_rows(ref, me, rows):
    return ref.at[me // rows, pl.ds(pl.multiple_of(me % rows // 8 * 8, 8), 8), :]


def meta_kernel(req_hbm, target_hbm, out_ref, place_ref, req_ref, target_ref, hot_ref, used_ref, seen_ref, sems):
    copies = start_all([(req_hbm, req_ref), (target_hbm, target_ref)], sems)
    wide_count = out_ref.shape[0]
    for d in range(wide_count):
        used_ref[d] = 0
        seen_ref[d] = 0
    out_ref[...] = jnp.zeros(out_ref.shape, F32)
    wait_all(copies)
    totals = jnp.sum(one_hot_rows(req_ref, hot_ref), axis=0, keepdims=True)
    for d in range(wide_count):
        out_ref[d, 0:1, :] = totals
    for b in range(BLK):
        target, request = target_ref[b], req_ref[b]
        slot, rank = used_ref[target], seen_ref[request]
        used_ref[target] = slot + 1
        seen_ref[request] = rank + 1
        place_ref[b] = target * META + slot * (2 * BLK)
        out_ref[target, pl.ds(slot + 1, 1), :] = hot_ref[b : b + 1, :]
        out_ref[target, pl.ds(slot + 3, 1), :] = jnp.full((1, HD), rank, jnp.int32).astype(F32)


def describe(req, target, wide_count):
    return pl.pallas_call(
        meta_kernel,
        in_specs=[HBM, HBM],
        out_specs=[VMEM, SMEM],
        out_shape=[
            jax.ShapeDtypeStruct((wide_count, 8, HD), F32),
            jax.ShapeDtypeStruct((BLK,), jnp.int32),
        ],
        scratch_shapes=[
            pltpu.SMEM((BLK,), jnp.int32),
            pltpu.SMEM((BLK,), jnp.int32),
            pltpu.VMEM((BLK, HD), F32),
            pltpu.SMEM((wide_count,), jnp.int32),
            pltpu.SMEM((wide_count,), jnp.int32),
            pltpu.SemaphoreType.DMA((2,)),
        ],
        compiler_params=params(),
        name="describe",
    )(*stay(req, target))


def begin_kernel(me_ref, part_hbm, after_ref, row_ref, rows_ref, sems):
    me = me_ref[0]
    wait_all(start_all([(tile_of_rows(part_hbm.at[0], me, part_hbm.shape[2]), rows_ref)], sems))
    row_ref[...] = rows_ref[pl.ds(me % 8, 1), :].astype(BF16)


def begin(me, partials, after):
    depth = partials.shape[3]
    return pl.pallas_call(
        begin_kernel,
        in_specs=[SMEM, HBM, SMEM],
        out_specs=VMEM,
        out_shape=jax.ShapeDtypeStruct((1, depth), BF16),
        scratch_shapes=[pltpu.VMEM((8, depth), F32), pltpu.SemaphoreType.DMA((1,))],
        compiler_params=params(),
        name="begin",
    )(me, *stay(partials), after)


META = CAP * 2 * BLK


def project_kernel(
    x_hbm, gain_hbm, wk_hbm, wv_hbm, kgain_hbm, place_ref, after_ref,
    k_ref, v_ref, w_ref, going_hbm,
    x_ref, gain_ref, wk_ref, wv_ref, kgain_ref, going_ref, sems,
):
    count, depth = x_ref.shape
    tile, chunk = 256, depth // 4
    small = start_all([(gain_hbm, gain_ref), (kgain_hbm, kgain_ref)], sems)
    pieces = [
        pltpu.make_async_copy(x_hbm.at[pl.ds(at, tile)], x_ref.at[pl.ds(at, tile)], sems.at[4 + i])
        for i, at in enumerate(range(0, count, tile))
    ]
    weights = [
        pltpu.make_async_copy(src.at[pl.ds(at, chunk)], dst.at[pl.ds(at, chunk)], sems.at[8 + i])
        for i, (at, src, dst) in enumerate(
            (at, src, dst)
            for at in range(0, depth, chunk)
            for src, dst in ((wk_hbm, wk_ref), (wv_hbm, wv_ref))
        )
    ]
    for copy in weights:
        copy.start()
    pieces[0].start()

    going_ref[...] = jnp.zeros(going_ref.shape, BF16)
    wait_all(small)
    parts = depth // HD

    def scale(i):
        squares = jnp.zeros((tile, HD), F32)
        for p in range(0, parts, 2):
            a, b = [x_ref[i * tile : (i + 1) * tile, q * HD : (q + 1) * HD] for q in (p, p + 1)]
            squares = squares + (a * a + b * b).astype(F32)
        mean = jnp.sum(squares, axis=1, keepdims=True) * (1.0 / depth)
        return lax.rsqrt(mean + EPS)

    gain = jnp.concatenate([gain_ref[...], jnp.zeros((HD - parts, HD), F32)], axis=0).T
    for i in range(4):
        wait_all(weights[2 * i : 2 * i + 2])
        if i == 3:
            pieces[1].start()
        for p in range(i * parts // 4, (i + 1) * parts // 4):
            rows = slice(p * HD, (p + 1) * HD)
            g = gain[:, p : p + 1]
            w_ref[rows, :HD] = (wk_ref[rows, :].astype(F32) * g).astype(BF16)
            w_ref[rows, HD:] = (wv_ref[rows, :].astype(F32) * g).astype(BF16)
    pieces[0].wait()
    pieces[2].start()
    scales = scale(0)
    for i in range(len(pieces)):
        rows = slice(i * tile, (i + 1) * tile)
        if i + 1 < len(pieces):
            pieces[i + 1].wait()
            if i + 3 < len(pieces):
                pieces[i + 3].start()
        out = dot(x_ref[rows, :], w_ref[...]) * scales
        if i + 1 < len(pieces):
            scales = scale(i + 1)
        k, v = head_norm(out[:, :HD], kgain_ref[...]), out[:, HD:].astype(BF16)
        k_ref[rows, :] = k
        v_ref[rows, :] = v
        k = k.astype(BF16)
        for b in range(tile // BLK):
            part = slice(b * BLK, (b + 1) * BLK)
            both = jnp.concatenate([k[part], v[part]], axis=0)
            place = pl.multiple_of(place_ref[i * (tile // BLK) + b], 2 * BLK)
            going_ref[pl.ds(place, 2 * BLK), :] = both
    out = pltpu.make_async_copy(going_ref, going_hbm, sems.at[16])
    out.start()
    out.wait()


def project(rows, gain, wk, wv, kgain, place, after, wide_count):
    count, depth = rows.shape
    return pl.pallas_call(
        project_kernel,
        in_specs=[HBM] * 5 + [SMEM, VMEM],
        out_specs=[VMEM] * 3 + [HBM],
        out_shape=[
            jax.ShapeDtypeStruct((count, HD), F32),
            jax.ShapeDtypeStruct((count, HD), BF16),
            jax.ShapeDtypeStruct((depth, 2 * HD), BF16),
            pltpu.HBM((wide_count * META, HD), BF16),
        ],
        scratch_shapes=[
            pltpu.VMEM((count, depth), BF16),
            pltpu.VMEM((depth // HD, HD), F32),
            pltpu.VMEM((depth, HD), BF16),
            pltpu.VMEM((depth, HD), BF16),
            pltpu.VMEM((1, HD), F32),
            pltpu.VMEM((wide_count * META, HD), BF16),
            pltpu.SemaphoreType.DMA((17,)),
        ],
        compiler_params=params(28),
        cost_estimate=pl.CostEstimate(
            flops=4 * count * depth * HD, bytes_accessed=2 * count * depth, transcendentals=0
        ),
        name="project",
    )(*stay(rows, gain.reshape(depth // HD, HD), wk, wv, kgain), place, after)


def hold_kernel(*refs):
    pass


def hold(going, *after):
    return pl.pallas_call(
        hold_kernel,
        in_specs=[HBM] + [VMEM] * len(after),
        out_specs=HBM,
        out_shape=pltpu.HBM(going.shape, going.dtype),
        input_output_aliases={0: 0},
        compiler_params=params(),
        name="hold",
    )(*stay(going), *after)


def token_kernel(me_ref, a_ref, b_ref, c_ref, d_ref, res_hbm, w_ref, kgain_hbm, out_ref, res_ref, kgain_ref, sems):
    me = me_ref[0]
    copies = start_all(
        [(tile_of_rows(res_hbm, me, res_hbm.shape[1]), res_ref), (kgain_hbm, kgain_ref)], sems
    )
    added = tree([ref[...].astype(F32) for ref in (a_ref, b_ref, c_ref, d_ref)], jnp.add)
    wait_all(copies)
    hidden = res_ref[pl.ds(me % 8, 1), :] + added
    normed = hidden * lax.rsqrt(jnp.mean(hidden * hidden, axis=-1, keepdims=True) + EPS)
    wide = jnp.broadcast_to(normed, (16, normed.shape[1])).astype(BF16)
    out = dot(wide, w_ref[...])
    k, v = head_norm(out[:, :HD], kgain_ref[...]), out[:, HD:]
    out_ref[...] = jnp.where(iota(k.shape, 0) % 2 == 0, k, v)


def token(me, parts, res, w, kgain):
    return pl.pallas_call(
        token_kernel,
        in_specs=[SMEM] + [VMEM] * 4 + [HBM, VMEM, HBM],
        out_specs=VMEM,
        out_shape=jax.ShapeDtypeStruct((16, HD), F32),
        scratch_shapes=[
            pltpu.VMEM((8, res.shape[2]), F32),
            pltpu.VMEM((1, HD), F32),
            pltpu.SemaphoreType.DMA((2,)),
        ],
        compiler_params=params(),
        cost_estimate=pl.CostEstimate(
            flops=50_000_000, bytes_accessed=3_000_000, transcendentals=0
        ),
        name="token",
    )(me, *parts, *stay(res), w, *stay(kgain))


def payload_rows(tokens):
    return STAT + -(-(6 + 2 * tokens) // 16) * 16


def put_stats(ref, c, total, tok):
    hi = total.astype(BF16).astype(F32)
    pad = ref.shape[0] - STAT - 6 - tok.shape[0]
    pieces = [c, hi, total - hi, tok] + ([jnp.zeros((pad, HD), F32)] if pad else [])
    ref[STAT:, :] = jnp.concatenate(pieces, axis=0).astype(BF16)


def frequencies():
    lane = iota((1, HD), 1) % (HD // 2)
    freq = jnp.zeros((1, HD), F32)
    for i in range(HD // 2):
        freq = jnp.where(lane == i, float(np.float32(THETA ** (-2.0 * i / HD))), freq)
    return freq


def context_row(ctx_ref):
    lane = iota((1, HD), 1)
    ctx = jnp.zeros((1, HD), F32)
    for r in range(ctx_ref.shape[0]):
        ctx = jnp.where(lane == r, ctx_ref[r].astype(F32), ctx)
    return ctx


def below(size):
    return jnp.where(iota((size, size), 1) < iota((size, size), 0), 1.0, 0.0).astype(BF16)


def turns(start, sign):
    freq = frequencies()
    ang = start * freq
    cb, sb = jnp.cos(ang), jnp.sin(ang)
    ang = iota((BLK, HD), 0).astype(F32) * freq
    ct, st = jnp.cos(ang), jnp.sin(ang)

    def turned(k, b):
        c1, s1 = cb[b : b + 1], sb[b : b + 1]
        c = c1 * ct - s1 * st
        s = (s1 * ct + c1 * st) * sign
        return (k * c + pltpu.roll(k, HD // 2, 1) * s).astype(BF16)

    return turned


def attend_kernel(
    me_ref, req_hbm, ctx_hbm, q_hbm, qgain_hbm, cache_hbm, meta_ref, k_ref, v_ref, tok_ref,
    out_ref, qr_ref,
    req_ref, ctx_ref, q_ref, qgain_ref, cache_ref, hot_ref, ang_ref, kr_ref,
    q_scr, s_scr, o_scr, sems,
):
    me = me_ref[0]
    copies = start_all(
        [
            (req_hbm, req_ref),
            (ctx_hbm, ctx_ref),
            (q_hbm, q_ref),
            (qgain_hbm, qgain_ref),
            (cache_hbm, cache_ref),
        ],
        sems,
    )
    rows, slots = cache_ref.shape[1], cache_ref.shape[2]
    pairs = q_ref.shape[0]
    heads = q_ref.shape[1] // HD
    queries = heads * pairs
    per_row = queries // rows
    score_scale = HD ** (-0.5)
    freq = frequencies()
    sign = rope_sign()
    lane = iota((1, HD), 1)
    wait_all(copies[:2])

    ctx = context_row(ctx_ref)
    counts = meta_ref[:, 0, :]
    ahead = jnp.sum(jnp.where(iota(counts.shape, 0) < me, counts, 0.0), axis=0, keepdims=True)
    last = ctx + BLK * jnp.sum(counts, axis=0, keepdims=True)
    hot = one_hot_rows(req_ref, hot_ref)
    earlier = dot(below(BLK), hot.astype(BF16))
    start = jnp.sum(hot * (ctx + BLK * (ahead + earlier)), axis=1, keepdims=True)
    turned = turns(start, sign)
    for b in range(BLK):
        part = slice(b * BLK, (b + 1) * BLK)
        kr_ref[part, :] = turned(k_ref[part, :], b)

    wait_all(copies[2:])
    last = jnp.broadcast_to(last, (HD, HD)).T[:rows]
    ang = jnp.concatenate([last, last + 1.0], axis=0) * freq
    cd, sd = jnp.cos(ang), jnp.sin(ang) * sign
    for h in range(heads):
        x = head_norm(q_ref[:, h * HD : (h + 1) * HD].astype(F32), qgain_ref[...])
        qr = (x * cd + pltpu.roll(x, HD // 2, 1) * sd).astype(BF16)
        qr_ref[h * pairs : (h + 1) * pairs, :] = qr
        q_scr[h * pairs : (h + 1) * pairs, :] = qr.astype(F32)

    ang_ref[...] = cd
    cos_row = ang_ref[pl.ds(me, 1), :]
    ang_ref[...] = sd
    sin_row = ang_ref[pl.ds(me, 1), :]
    tok = tok_ref[0:8, :]
    turned = tok * cos_row + pltpu.roll(tok, HD // 2, 1) * sin_row
    tok = jnp.where(iota(tok.shape, 0) % 2 == 0, turned, tok)

    place = me * slots + iota((per_row, slots), 1)
    for r in range(rows):
        mine = pl.ds(r, per_row, stride=rows)
        s = dot_nt(q_scr[mine, :].astype(BF16), cache_ref[0, r]) * score_scale
        s_scr[mine, :] = jnp.where(place < ctx_ref[r], s, MASKED)
    owners = []
    for j in range(0, BLK, 4):
        own = jnp.where(lane < BLK, req_ref[j], req_ref[j + 1])
        own = jnp.where(lane < 2 * BLK, own, jnp.where(lane < 3 * BLK, req_ref[j + 2], req_ref[j + 3]))
        owners.append(own)
    owner = jnp.concatenate(owners, axis=1)
    block = dot_nt(qr_ref[...], kr_ref[...]) * score_scale
    block = jnp.where(iota((queries, 1), 0) % rows == owner, block, MASKED)
    cache = s_scr[...]
    top = jnp.maximum(
        jnp.max(cache, axis=1, keepdims=True), jnp.max(block, axis=1, keepdims=True)
    )
    c = jnp.maximum(top, FLOOR).astype(BF16).astype(F32)
    cache = jnp.exp(cache - c)
    block = jnp.exp(block - c)
    total = jnp.sum(cache, axis=1, keepdims=True) + jnp.sum(block, axis=1, keepdims=True)
    s_scr[...] = cache
    for r in range(rows):
        mine = pl.ds(r, per_row, stride=rows)
        o_scr[mine, :] = dot(s_scr[mine, :].astype(BF16), cache_ref[1, r])
    out_ref[:STAT, :] = (dot(block.astype(BF16), v_ref[...]) + o_scr[...]).astype(BF16)
    lane = iota((queries, HD), 1)
    both = jnp.where(lane == 0, c, jnp.where(lane == 1, total, 0.0))
    t0, t1 = both[:HD].T, both[HD:].T
    put_stats(
        out_ref,
        jnp.concatenate([t0[0:1], t1[0:1]], axis=0),
        jnp.concatenate([t0[1:2], t1[1:2]], axis=0),
        tok[0:2, :],
    )


def attend(me, req, ctx, q, qgain, cache, meta, keys, values, tok):
    return pl.pallas_call(
        attend_kernel,
        in_specs=[SMEM] + [HBM] * 5 + [VMEM] * 4,
        out_specs=[VMEM, VMEM],
        out_shape=[
            jax.ShapeDtypeStruct((payload_rows(1), HD), BF16),
            jax.ShapeDtypeStruct((STAT, HD), BF16),
        ],
        scratch_shapes=[
            pltpu.SMEM(req.shape, jnp.int32),
            pltpu.SMEM(ctx.shape, jnp.int32),
            pltpu.VMEM(q.shape, BF16),
            pltpu.VMEM(qgain.shape, F32),
            pltpu.VMEM(cache.shape, BF16),
            pltpu.VMEM((BLK, HD), F32),
            pltpu.VMEM((2 * ctx.shape[0], HD), F32),
            pltpu.VMEM(keys.shape, BF16),
        ]
        + [pltpu.VMEM((STAT, HD), F32)] * 3
        + [pltpu.SemaphoreType.DMA((5,))],
        compiler_params=params(),
        cost_estimate=pl.CostEstimate(
            flops=400_000_000, bytes_accessed=5_000_000, transcendentals=300_000
        ),
        name="attend",
    )(me, *stay(req, ctx, q, qgain, cache), meta, keys, values, tok)


def finish_kernel(ctx_hbm, came_hbm, meta_ref, after_ref, out_hbm, token_ref, ctx_ref, came_ref, out_ref, sems):
    wait_all(start_all([(ctx_hbm, ctx_ref), (came_hbm, came_ref)], sems))
    groups = came_ref.shape[0]
    counts = meta_ref[:, 0, :]
    base = context_row(ctx_ref) + BLK * dot(below(groups), counts.astype(BF16))
    sign = rope_sign()
    turned = [
        turns(
            jnp.sum(
                meta_ref[:, 1 + slot, :] * (base + BLK * meta_ref[:, 3 + slot, :]), axis=1, keepdims=True
            ),
            sign,
        )
        for slot in range(CAP)
    ]
    pr, pc = iota((2 * BLK, 2 * BLK), 0), iota((2 * BLK, 2 * BLK), 1)
    perm = jnp.where(pc == pr // 2 + BLK * (pr % 2), 1.0, 0.0).astype(BF16)
    for g in range(groups):
        for slot in range(CAP):
            at = slot * 2 * BLK
            k = turned[slot](came_ref[g, at : at + BLK, :].astype(F32), g)
            both = jnp.concatenate([k, came_ref[g, at + BLK : at + 2 * BLK, :]], axis=0)
            to = (g * CAP + slot) * 2 * BLK
            out_ref[to : to + 2 * BLK, :] = dot(perm, both).astype(BF16)
    token_ref[...] = base[:8]
    out = pltpu.make_async_copy(out_ref, out_hbm, sems.at[2])
    out.start()
    out.wait()


def finish(ctx, came, meta, after):
    shape = (came.shape[0] * META, HD)
    return pl.pallas_call(
        finish_kernel,
        in_specs=[HBM, HBM, VMEM, VMEM],
        out_specs=[HBM, VMEM],
        out_shape=[pltpu.HBM(shape, BF16), jax.ShapeDtypeStruct((8, HD), F32)],
        scratch_shapes=[
            pltpu.SMEM(ctx.shape, jnp.int32),
            pltpu.VMEM(came.shape, BF16),
            pltpu.VMEM(shape, BF16),
            pltpu.SemaphoreType.DMA((3,)),
        ],
        compiler_params=params(),
        cost_estimate=pl.CostEstimate(
            flops=80_000_000, bytes_accessed=3_000_000, transcendentals=0
        ),
        name="finish",
    )(*stay(ctx, came), meta, after)


def tree(values, op):
    while len(values) > 1:
        values = [op(values[i], values[i + 1]) for i in range(0, len(values), 2)]
    return values[0]


def merged(refs, tokens):
    add = lambda a, b: a + b
    stats = [ref[STAT:, :].astype(F32) for ref in refs]
    cs = [s[0:2] for s in stats]
    top = tree(cs, jnp.maximum)
    factors = [jnp.exp(c - top) for c in cs]
    total = tree([f * (s[2:4] + s[4:6]) for s, f in zip(stats, factors)], add)
    cols = jnp.concatenate(factors + [jnp.zeros((HD - 2 * len(refs), HD), F32)], axis=0).T
    halves = []
    for g in range(2):
        terms = [
            ref[g * HD : (g + 1) * HD, :].astype(F32) * cols[:, 2 * i + g : 2 * i + g + 1]
            for i, ref in enumerate(refs)
        ]
        halves.append(tree(terms, add))
    tok = jnp.concatenate([s[6 : 6 + 2 * tokens] for s in stats], axis=0)
    return halves, top, total, tok


def merge_kernel(*refs, tokens):
    out_ref = refs[-1]
    halves, top, total, tok = merged(refs[:-1], tokens)
    for g in range(2):
        out_ref[g * HD : (g + 1) * HD, :] = halves[g].astype(BF16)
    put_stats(out_ref, top, total, tok)


def merge(parts, tokens):
    return pl.pallas_call(
        functools.partial(merge_kernel, tokens=tokens),
        in_specs=[VMEM] * len(parts),
        out_specs=VMEM,
        out_shape=jax.ShapeDtypeStruct((payload_rows(len(parts) * tokens), HD), BF16),
        compiler_params=params(),
        name="merge",
    )(*parts)


def slot_token(slot, me):
    return me ^ (slot & 3) ^ (((slot >> 2) & 3) * 8) ^ ((slot >> 4) * 4)


def final_kernel(me_ref, qr_ref, after_ref, *refs):
    out_ref, tok_out_ref = refs[-2:]
    me = me_ref[0]
    halves, top, total, tok = merged(refs[:-2], 16)
    keys = tok.astype(BF16)
    shape = (64, 64)
    to, of = iota(shape, 0), iota(shape, 1)
    moves = (to % 2 == of % 2) & (to // 2 == slot_token(of // 2, me))
    tok_out_ref[...] = dot(jnp.where(moves, 1.0, 0.0).astype(BF16), keys).astype(BF16)
    vals = pltpu.roll(tok, 63, 0).astype(BF16)
    cols = jnp.concatenate([top, total, jnp.zeros((HD - 4, HD), F32)], axis=0).T
    row, col = iota((HD, 64), 0), iota((HD, 64), 1)
    held = slot_token(col // 2, me)
    same = (col % 2 == 0) & (held % 16 == row % 16) & (held // 16 <= (row // 16) % 2)
    for g in range(2):
        s = dot_nt(qr_ref[g * HD : (g + 1) * HD, :], keys) * (HD ** (-0.5))
        s = jnp.where(same, s, MASKED)
        c, old = cols[:, g : g + 1], cols[:, 2 + g : 3 + g]
        m = jnp.maximum(c, jnp.max(s, axis=1, keepdims=True))
        f = jnp.exp(c - m)
        p = jnp.exp(s - m)
        whole = old * f + jnp.sum(p, axis=1, keepdims=True)
        o = ((halves[g] * f + dot(p.astype(BF16), vals)) / whole).astype(BF16)
        for h in range(4):
            head = g * 4 + h
            out_ref[:, head * HD : (head + 1) * HD] = o[h * 32 : (h + 1) * 32]


def final(me, qr, after, parts):
    return pl.pallas_call(
        final_kernel,
        in_specs=[SMEM] + [VMEM] * (2 + len(parts)),
        out_specs=[VMEM, VMEM],
        out_shape=[
            jax.ShapeDtypeStruct((32, 8 * HD), BF16),
            jax.ShapeDtypeStruct((64, HD), BF16),
        ],
        compiler_params=params(),
        name="final",
    )(me, qr, after, *parts)


def exchange(value, axis, step):
    size = lax.axis_size(axis)
    return lax.ppermute(value, axis, [(i, i ^ step) for i in range(size)])


def all_to_all(value):
    return lax.all_to_all(value, "wide", split_axis=0, concat_axis=0, tiled=True)


def local(
    prefill_rows,
    in_gain,
    key_weight,
    value_weight,
    key_gain,
    query_gain,
    block_request,
    block_target,
    context_lengths,
    kv_cache,
    decode_queries,
    decode_partials,
    decode_residual,
):
    me = lax.axis_index("wide").astype(jnp.int32).reshape(1)
    wide_count = lax.axis_size("wide")
    row_count = context_lengths.shape[0]
    kgain = key_gain.reshape(1, HD)

    meta, place = describe(block_request, block_target.reshape(-1), wide_count)
    meta = all_to_all(meta)

    part = begin(me, decode_partials, place)
    other = exchange(part, "kvh", 1)
    part = (part.astype(F32) + other.astype(F32)).astype(BF16)
    decode_parts = [part] + [exchange(part, "kvh", step) for step in (2, 4, 6)]

    keys, values, weight, going = project(
        prefill_rows, in_gain, key_weight, value_weight, kgain, place, part, wide_count,
    )
    going = hold(going, *decode_parts)
    came = all_to_all(going.reshape(wide_count, META, HD))
    tok = token(me, decode_parts, decode_residual, weight, kgain)
    payload, queries = attend(
        me, block_request, context_lengths, decode_queries.reshape(2 * row_count, -1),
        query_gain.reshape(1, HD), kv_cache, meta, keys, values, tok,
    )
    parts = [payload] + [exchange(payload, "wide", step) for step in STAGES[0]]
    payload = merge(parts, 1)
    parts = [payload] + [exchange(payload, "wide", step) for step in STAGES[1]]
    payload = merge(parts, 4)
    parts = [payload] + [exchange(payload, "wide", step) for step in STAGES[2]]
    new_blocks, done = finish(context_lengths, came, meta, payload)
    attended, new = final(me, queries, done, parts)
    return (
        attended.reshape(2, row_count, -1),
        new_blocks.reshape(wide_count * CAP, BLK, 2, HD),
        new.reshape(2, row_count, 2, HD),
    )


def solution(mesh):
    placed = (
        P("wide", None),
        P(),
        P(None, "kvh"),
        P(None, "kvh"),
        P(),
        P(),
        P("wide"),
        P("wide", None),
        P(),
        P(None, None, "wide", "kvh"),
        P(None, None, "kvh"),
        P("kvh", None, None, None),
        P(),
    )
    return jax.shard_map(
        local,
        mesh=mesh,
        in_specs=placed,
        out_specs=(P(None, None, "kvh"), P("wide", None, None, "kvh"), P(None, None, None, "kvh")),
        check_vma=False,
    )
```

time: 120 us -> 82.1 us (0.68); the launches traced: 118 us -> 81.7 us
  waiting for transfers between devices: 41.1 us -> 13.2 us
  local copies, waits for them, and re-layouts: 16.6 us -> 0.7 us
  Pallas kernels: 12.8 us -> 23.9 us
  other arithmetic: 7.76 us -> 0.04 us
  starting transfers between devices: 38.4 us -> 43.1 us
    ppermute x17 -> x11, waiting for transfers between devices: 41.1 us -> 13.2 us  [exchange(): return lax.ppermute(value, axis, [(i, i ^ step) for i in range(size)])]
    all_to_all x1 -> x2, starting transfers between devices: 9.76 us -> 23.7 us  [all_to_all(): lax.all_to_all(value, 'wide', split_axis=0, concat_axis=0, tiled=True)]
    pallas_call x7 -> x10, Pallas kernels: 12.8 us -> 23.9 us  [the longest x1 11.1 us: project(): pl.pallas_call(project_kernel, in_specs=[HBM] * 5 + [SMEM, VMEM], out_spe...]
    unnamed x51 -> x4, local copies, waits for them, and re-layouts: 11.6 us -> 0.7 us
    ppermute x17 -> x11, starting transfers between devices: 28.6 us -> 19.4 us  [exchange(): return lax.ppermute(value, axis, [(i, i ^ step) for i in range(size)])]
    reduce_sum x5 -> x0, other arithmetic: 3.99 us -> none  [the longest x1 1.25 us: local(): jnp.sum(jnp.where(requests == request_index, context_lengths + BLK * tota...]
    convert_element_type x2 -> x1, other arithmetic: 2.35 us -> 0.04 us  [local(): part = (part.astype(F32) + other.astype(F32)).astype(BF16)]
    convert_element_type x2 -> x0, local copies, waits for them, and re-layouts: 1.63 us -> none  [the longest x1 1.54 us: local(): part = part.astype(BF16)]
  transfers between devices with their start and end apart: 18 -> 13, of which waited for: 10 -> 4; matrix products, arithmetic and copies ran while one was open for 10% -> 0% of each run, Pallas kernels for 11% -> 24%
where the time goes in v2:
time: 82.1 us; the launch traced here: 81.7 us
  starting transfers between devices  43.1 us (52%)
  Pallas kernels  23.9 us (29%)
  waiting for transfers between devices  13.2 us (16%)
    all_to_all x2, starting transfers between devices, all_to_all(): lax.all_to_all(value, 'wide', split_axis=0, concat_axis=0, tiled=True)  23.7 us
    ppermute x11, starting transfers between devices, exchange(): return lax.ppermute(value, axis, [(i, i ^ step) for i in range(size)])  19.4 us
    ppermute x11, waiting for transfers between devices, exchange(): return lax.ppermute(value, axis, [(i, i ^ step) for i in range(size)])  13.2 us
    pallas_call x1, Pallas kernels, project(): pl.pallas_call(project_kernel, in_specs=[HBM] * 5 + [SMEM, VMEM], out_spe...  11.1 us
    pallas_call x1, Pallas kernels, finish(): pl.pallas_call(finish_kernel, in_specs=[HBM, HBM, VMEM, VMEM], out_specs=...  3.28 us
    pallas_call x1, Pallas kernels, attend(): pl.pallas_call(attend_kernel, in_specs=[SMEM] + [HBM] * 5 + [VMEM] * 4, o...  2.72 us
  transfers between devices with their start and end apart: 13, of which 4 were waited for; matrix products, arithmetic and copies ran while one was open for 0% of the time, Pallas kernels for 24%

profile of v2, /device:TPU:1, one launch (start us, length us, event | category | flops | bytes accessed | tf_op | source)
XLA Modules:
  0.0 81.7 jit_solution(10990289592304890762)
XLA Ops:
  0.6 1.5 %describe.1 = (f32[32,8,128]{2,1,0:T(8,128)}, s32[32]{0:T(128)S(1)}) custom-call(s32[32]{0:T(128)} %req_hbm.3, s32[32]{0:T(128)} %bitcast.19), custom_call_target="tpu_custom_call" | custom-call | tf_op jit(solution)/shard_map/describe/pallas_call | solution.py:103
  2.1 1.5 %begin.1 = bf16[1,5120]{1,0:T(2,128)(2,1)S(1)} custom-call(s32[1]{0:T(128)} %bitcast.me_ref, f32[1,2,16,5120]{3,2,1,0:T(8,128)} %part_hbm.1, s32[32]{0:T(128)S(1)} %get-tuple-element.16.after_ref.place_ref), custom_call_target="tpu_custom_call" | custom-call | tf_op jit(solution)/shard_map/begin/pallas_call | solution.py:132
  3.7 3.3 %collective-permute-start = (bf16[1,5120]{1,0:T(2,128)(2,1)S(1)}, bf16[1,5120]{1,0:T(2,128)(2,1)S(1)}, u32[]{:S(2)}, u32[]{:S(2)}) collective-permute-start(bf16[1,5120]{1,0:T(2,128)(2,1)S(1)} %begin.1), channel_id=1, source_target_pairs={{0,1},{1,0},{2,3},{3,2},{4,5},{5,4},{6,7},{7,6},{8,9},{9,8},{10,11... | collective-permute-start | bytes 30728 | tf_op jit(solution)/shard_map/ppermute | solution.py:611
  7.0 11.9 %all-to-all-start = ((f32[32,8,128]{2,1,0:T(8,128)}), f32[32,8,128]{2,1,0:T(8,128)S(1)}, u32[]{:S(2)}, u32[]{:S(2)}) async-start(f32[32,8,128]{2,1,0:T(8,128)} %get-tuple-element.15), calls=%async_computation | async-start | bytes 262144 | tf_op jit(solution)/shard_map/all_to_all | solution.py:615
  18.9 0.0 collective-permute-done
  19.0 1.7 %collective-permute-start.3 = (bf16[1,5120]{1,0:T(2,128)(2,1)S(1)}, bf16[1,5120]{1,0:T(2,128)(2,1)S(1)}, u32[]{:S(2)}, u32[]{:S(2)}) collective-permute-start(bf16[1,5120]{1,0:T(2,128)(2,1)S(1)} %add_convert_fusion.after_ref.a_ref.refs_1_), channel_id=1, source_target_pairs={{0,6},{1,7},{2,4},{3,5},{4,2},{5,3},{6,0},{7,1},{8,14},{9,15},{10,... | collective-permute-start | bytes 30728 | tf_op jit(solution)/shard_map/ppermute | solution.py:611
  20.7 0.3 collective-permute-start.2
  21.0 1.6 %collective-permute-start.1 = (bf16[1,5120]{1,0:T(2,128)(2,1)S(1)}, bf16[1,5120]{1,0:T(2,128)(2,1)S(1)}, u32[]{:S(2)}, u32[]{:S(2)}) collective-permute-start(bf16[1,5120]{1,0:T(2,128)(2,1)S(1)} %add_convert_fusion.after_ref.a_ref.refs_1_), channel_id=1, source_target_pairs={{0,2},{1,3},{2,0},{3,1},{4,6},{5,7},{6,4},{7,5},{8,10},{9,11},{10,... | collective-permute-start | bytes 30728 | tf_op jit(solution)/shard_map/ppermute | solution.py:611
  22.6 11.1 %project.1 = (f32[1024,128]{1,0:T(8,128)S(1)}, bf16[1024,128]{1,0:T(8,128)(2,1)S(1)}, bf16[5120,256]{1,0:T(8,128)(2,1)S(1)}, bf16[4096,128]{1,0:T(8,128)(2,1)}) custom-call(bf16[1024,5120]{1,0:T(8,128)(2,1)} %x_hbm.1, f32[40,128]{1,0:T(8,128)} %bitcast.12, bf16[5120,128]{1,0:T(8,128)(2,1)} %wk_hbm.1, bf16[5120,128]{1,0:T(8,128)(2,1)} %wv_hbm.1, ...), custom_call_target="tpu_custom_call" | custom-call | flops 2684354560 | bytes 10485760 | tf_op jit(solution)/shard_map/project/pallas_call | solution.py:220
  33.7 0.0 copy-start
  33.7 0.7 copy-done
  34.4 0.0 collective-permute-done.3.d_ref.refs_4_
  34.4 0.0 collective-permute-done.2.c_ref.refs_3_
  34.4 0.0 collective-permute-done.1.b_ref.refs_2_
  34.4 0.0 all-to-all-done.meta_ref
  34.4 11.8 %all-to-all-start.1 = ((bf16[32,128,128]{2,1,0:T(8,128)(2,1)}), bf16[32,128,128]{2,1,0:T(8,128)(2,1)}, u32[]{:S(2)}, u32[]{:S(2)}) async-start(bf16[32,128,128]{2,1,0:T(8,128)(2,1)} %bitcast.10), calls=%async_computation.1 | async-start | bytes 2097152 | tf_op jit(solution)/shard_map/all_to_all | solution.py:615
  46.2 0.0 copy-start.1
  46.2 1.6 %token_.1.tok_ref = f32[16,128]{1,0:T(8,128)S(1)} custom-call(s32[1]{0:T(128)} %bitcast.me_ref, bf16[1,5120]{1,0:T(2,128)(2,1)S(1)} %add_convert_fusion.after_ref.a_ref.refs_1_, bf16[1,5120]{1,0:T(2,128)(2,1)S(1)} %collective-permute-done.1.b_ref.refs_2_, bf16[1,5120]{1,0:T(2,128)(2,1)S(1)} %collective-permute-done.2.c_ref.refs_3_, ...), custom_call_target="tpu_custom_call" | custom-call | flops 50000000 | bytes 3000000 | tf_op jit(solution)/shard_map/token/pallas_call | solution.py:279
  47.9 0.0 copy-done.1
  47.9 2.7 %attend.1 = (bf16[272,128]{1,0:T(8,128)(2,1)S(1)}, bf16[256,128]{1,0:T(8,128)(2,1)S(1)}) custom-call(s32[1]{0:T(128)} %bitcast.me_ref, s32[32]{0:T(128)} %req_hbm.3, s32[16]{0:T(128)} %ctx_hbm.3, bf16[32,1024]{1,0:T(8,128)(2,1)} %bitcast.11, f32[1,128]{1,0:T(1,128)} %bitcast.15, bf16[2,16,128,128]{3,2,1,0:T(8,128)(2,1)} %cache_hbm.1, ...), custom_call_target="tpu_custom_call" | custom-call | flops 400000000 | bytes 5000000 | tf_op jit(solution)/shard_map/attend/pallas_call | solution.py:440
  50.6 2.5 %collective-permute-start.6 = (bf16[272,128]{1,0:T(8,128)(2,1)S(1)}, bf16[272,128]{1,0:T(8,128)(2,1)S(1)}, u32[]{:S(2)}, u32[]{:S(2)}) collective-permute-start(bf16[272,128]{1,0:T(8,128)(2,1)S(1)} %get-tuple-element.22.refs_0_), channel_id=1, source_target_pairs={{0,24},{8,16},{16,8},{24,0},{32,56},{40,48},{48,40},{56,32},{64,88... | collective-permute-start | bytes 208904 | tf_op jit(solution)/shard_map/ppermute | solution.py:611
  53.1 0.6 collective-permute-start.5
  53.6 0.3 collective-permute-start.4
  54.0 5.6 %collective-permute-done.6.refs_3_ = bf16[272,128]{1,0:T(8,128)(2,1)S(1)} collective-permute-done((bf16[272,128]{1,0:T(8,128)(2,1)S(1)}, bf16[272,128]{1,0:T(8,128)(2,1)S(1)}, u32[]{:S(2)}, u32[]{:S(2)}) %collective-permute-start.6) | collective-permute-done | bytes 69664 | tf_op jit(solution)/shard_map/ppermute | solution.py:611
  59.5 0.0 collective-permute-done.5.refs_2_
  59.5 3.6 %collective-permute-done.4.refs_1_ = bf16[272,128]{1,0:T(8,128)(2,1)S(1)} collective-permute-done((bf16[272,128]{1,0:T(8,128)(2,1)S(1)}, bf16[272,128]{1,0:T(8,128)(2,1)S(1)}, u32[]{:S(2)}, u32[]{:S(2)}) %collective-permute-start.4) | collective-permute-done | bytes 69664 | tf_op jit(solution)/shard_map/ppermute | solution.py:611
  63.1 0.3 merge.2.refs_0_
  63.5 0.1 collective-permute-start.9
  63.6 0.1 collective-permute-start.8
  63.7 3.1 %collective-permute-start.7 = (bf16[272,128]{1,0:T(8,128)(2,1)S(1)}, bf16[272,128]{1,0:T(8,128)(2,1)S(1)}, u32[]{:S(2)}, u32[]{:S(2)}) collective-permute-start(bf16[272,128]{1,0:T(8,128)(2,1)S(1)} %merge.2.refs_0_), channel_id=1, source_target_pairs={{0,64},{8,72},{16,80},{24,88},{32,96},{40,104},{48,112},{56,120},{... | collective-permute-start | bytes 208904 | tf_op jit(solution)/shard_map/ppermute | solution.py:611
  66.8 3.9 %collective-permute-done.9.refs_3_ = bf16[272,128]{1,0:T(8,128)(2,1)S(1)} collective-permute-done((bf16[272,128]{1,0:T(8,128)(2,1)S(1)}, bf16[272,128]{1,0:T(8,128)(2,1)S(1)}, u32[]{:S(2)}, u32[]{:S(2)}) %collective-permute-start.9) | collective-permute-done | bytes 69664 | tf_op jit(solution)/shard_map/ppermute | solution.py:611
  70.7 0.0 collective-permute-done.8.refs_2_
  70.7 0.1 collective-permute-done.7.refs_1_
  70.8 0.3 merge.3.after_ref.refs_0_
  71.2 5.7 %collective-permute-start.10 = (bf16[304,128]{1,0:T(8,128)(2,1)S(1)}, bf16[304,128]{1,0:T(8,128)(2,1)S(1)}, u32[]{:S(2)}, u32[]{:S(2)}) collective-permute-start(bf16[304,128]{1,0:T(8,128)(2,1)S(1)} %merge.3.after_ref.refs_0_), channel_id=1, source_target_pairs={{0,32},{8,40},{16,48},{24,56},{32,0},{40,8},{48,16},{56,24},{64,96... | collective-permute-start | bytes 233480 | tf_op jit(solution)/shard_map/ppermute | solution.py:611
  76.9 0.0 all-to-all-done.1.came_hbm
  76.9 3.3 %finish.1 = (bf16[4096,128]{1,0:T(8,128)(2,1)}, f32[8,128]{1,0:T(8,128)S(1)}) custom-call(s32[16]{0:T(128)} %ctx_hbm.3, bf16[32,128,128]{2,1,0:T(8,128)(2,1)} %all-to-all-done.1.came_hbm, f32[32,8,128]{2,1,0:T(8,128)S(1)} %all-to-all-done.meta_ref, bf16[304,128]{1,0:T(8,128)(2,1)S(1)} %merge.3.after_ref.refs_0_), custom_call_target="tpu_custom_call" | custom-call | flops 80000000 | bytes 3000000 | tf_op jit(solution)/shard_map/finish/pallas_call | solution.py:500
  80.2 0.0 collective-permute-done.10.refs_1_
  80.2 1.5 %final.1 = (bf16[32,1024]{1,0:T(8,128)(2,1)}, bf16[64,128]{1,0:T(8,128)(2,1)}) custom-call(s32[1]{0:T(128)} %bitcast.me_ref, bf16[256,128]{1,0:T(8,128)(2,1)S(1)} %get-tuple-element.20.qr_ref, f32[8,128]{1,0:T(8,128)S(1)} %get-tuple-element.23.after_ref, bf16[304,128]{1,0:T(8,128)(2,1)S(1)} %merge.3.after_ref.refs_0_, ...), custom_call_target="tpu_custom_call" | custom-call | tf_op jit(solution)/shard_map/final/pallas_call | solution.py:596
  (2 shorter events, 0.0 us)
Async XLA Ops:
  3.7 15.3 %collective-permute-start = (bf16[1,5120]{1,0:T(2,128)(2,1)S(1)}, bf16[1,5120]{1,0:T(2,128)(2,1)S(1)}, u32[]{:S(2)}, u32[]{:S(2)}) collective-permute-start(bf16[1,5120]{1,0:T(2,128)(2,1)S(1)} %begin.1), channel_id=1, source_target_pairs={{0,1},{1,0},{2,3},{3,2},{4,5},{5,4},{6,7},{7,6},{8,9},{9,8},{10,11... | collective-permute-start | bytes 30728 | tf_op jit(solution)/shard_map/ppermute | solution.py:611
  7.0 27.4 %all-to-all-start = ((f32[32,8,128]{2,1,0:T(8,128)}), f32[32,8,128]{2,1,0:T(8,128)S(1)}, u32[]{:S(2)}, u32[]{:S(2)}) async-start(f32[32,8,128]{2,1,0:T(8,128)} %get-tuple-element.15), calls=%async_computation | async-start | bytes 262144 | tf_op jit(solution)/shard_map/all_to_all | solution.py:615
  19.0 15.4 %collective-permute-start.3 = (bf16[1,5120]{1,0:T(2,128)(2,1)S(1)}, bf16[1,5120]{1,0:T(2,128)(2,1)S(1)}, u32[]{:S(2)}, u32[]{:S(2)}) collective-permute-start(bf16[1,5120]{1,0:T(2,128)(2,1)S(1)} %add_convert_fusion.after_ref.a_ref.refs_1_), channel_id=1, source_target_pairs={{0,6},{1,7},{2,4},{3,5},{4,2},{5,3},{6,0},{7,1},{8,14},{9,15},{10,... | collective-permute-start | bytes 30728 | tf_op jit(solution)/shard_map/ppermute | solution.py:611
  20.7 13.7 %collective-permute-start.2 = (bf16[1,5120]{1,0:T(2,128)(2,1)S(1)}, bf16[1,5120]{1,0:T(2,128)(2,1)S(1)}, u32[]{:S(2)}, u32[]{:S(2)}) collective-permute-start(bf16[1,5120]{1,0:T(2,128)(2,1)S(1)} %add_convert_fusion.after_ref.a_ref.refs_1_), channel_id=1, source_target_pairs={{0,4},{1,5},{2,6},{3,7},{4,0},{5,1},{6,2},{7,3},{8,12},{9,13},{10,... | collective-permute-start | bytes 30728 | tf_op jit(solution)/shard_map/ppermute | solution.py:611
  21.0 13.4 %collective-permute-start.1 = (bf16[1,5120]{1,0:T(2,128)(2,1)S(1)}, bf16[1,5120]{1,0:T(2,128)(2,1)S(1)}, u32[]{:S(2)}, u32[]{:S(2)}) collective-permute-start(bf16[1,5120]{1,0:T(2,128)(2,1)S(1)} %add_convert_fusion.after_ref.a_ref.refs_1_), channel_id=1, source_target_pairs={{0,2},{1,3},{2,0},{3,1},{4,6},{5,7},{6,4},{7,5},{8,10},{9,11},{10,... | collective-permute-start | bytes 30728 | tf_op jit(solution)/shard_map/ppermute | solution.py:611
  33.7 0.7 copy-start
  34.4 42.4 %all-to-all-start.1 = ((bf16[32,128,128]{2,1,0:T(8,128)(2,1)}), bf16[32,128,128]{2,1,0:T(8,128)(2,1)}, u32[]{:S(2)}, u32[]{:S(2)}) async-start(bf16[32,128,128]{2,1,0:T(8,128)(2,1)} %bitcast.10), calls=%async_computation.1 | async-start | bytes 2097152 | tf_op jit(solution)/shard_map/all_to_all | solution.py:615
  46.2 1.7 %copy-start.1 = (bf16[1024,128]{1,0:T(8,128)(2,1)S(1)}, bf16[1024,128]{1,0:T(8,128)(2,1)}, u32[]{:S(2)}) copy-start(bf16[1024,128]{1,0:T(8,128)(2,1)} %copy-done) | copy-start | bytes 786436
  50.6 8.9 %collective-permute-start.6 = (bf16[272,128]{1,0:T(8,128)(2,1)S(1)}, bf16[272,128]{1,0:T(8,128)(2,1)S(1)}, u32[]{:S(2)}, u32[]{:S(2)}) collective-permute-start(bf16[272,128]{1,0:T(8,128)(2,1)S(1)} %get-tuple-element.22.refs_0_), channel_id=1, source_target_pairs={{0,24},{8,16},{16,8},{24,0},{32,56},{40,48},{48,40},{56,32},{64,88... | collective-permute-start | bytes 208904 | tf_op jit(solution)/shard_map/ppermute | solution.py:611
  53.1 6.5 %collective-permute-start.5 = (bf16[272,128]{1,0:T(8,128)(2,1)S(1)}, bf16[272,128]{1,0:T(8,128)(2,1)S(1)}, u32[]{:S(2)}, u32[]{:S(2)}) collective-permute-start(bf16[272,128]{1,0:T(8,128)(2,1)S(1)} %get-tuple-element.22.refs_0_), channel_id=1, source_target_pairs={{0,16},{8,24},{16,0},{24,8},{32,48},{40,56},{48,32},{56,40},{64,80... | collective-permute-start | bytes 208904 | tf_op jit(solution)/shard_map/ppermute | solution.py:611
  53.6 9.5 %collective-permute-start.4 = (bf16[272,128]{1,0:T(8,128)(2,1)S(1)}, bf16[272,128]{1,0:T(8,128)(2,1)S(1)}, u32[]{:S(2)}, u32[]{:S(2)}) collective-permute-start(bf16[272,128]{1,0:T(8,128)(2,1)S(1)} %get-tuple-element.22.refs_0_), channel_id=1, source_target_pairs={{0,8},{8,0},{16,24},{24,16},{32,40},{40,32},{48,56},{56,48},{64,72... | collective-permute-start | bytes 208904 | tf_op jit(solution)/shard_map/ppermute | solution.py:611
  63.5 7.3 %collective-permute-start.9 = (bf16[272,128]{1,0:T(8,128)(2,1)S(1)}, bf16[272,128]{1,0:T(8,128)(2,1)S(1)}, u32[]{:S(2)}, u32[]{:S(2)}) collective-permute-start(bf16[272,128]{1,0:T(8,128)(2,1)S(1)} %merge.2.refs_0_), channel_id=1, source_target_pairs={{0,192},{8,200},{16,208},{24,216},{32,224},{40,232},{48,240},{56,2... | collective-permute-start | bytes 208904 | tf_op jit(solution)/shard_map/ppermute | solution.py:611
  63.6 7.2 %collective-permute-start.8 = (bf16[272,128]{1,0:T(8,128)(2,1)S(1)}, bf16[272,128]{1,0:T(8,128)(2,1)S(1)}, u32[]{:S(2)}, u32[]{:S(2)}) collective-permute-start(bf16[272,128]{1,0:T(8,128)(2,1)S(1)} %merge.2.refs_0_), channel_id=1, source_target_pairs={{0,128},{8,136},{16,144},{24,152},{32,160},{40,168},{48,176},{56,1... | collective-permute-start | bytes 208904 | tf_op jit(solution)/shard_map/ppermute | solution.py:611
  63.7 7.1 %collective-permute-start.7 = (bf16[272,128]{1,0:T(8,128)(2,1)S(1)}, bf16[272,128]{1,0:T(8,128)(2,1)S(1)}, u32[]{:S(2)}, u32[]{:S(2)}) collective-permute-start(bf16[272,128]{1,0:T(8,128)(2,1)S(1)} %merge.2.refs_0_), channel_id=1, source_target_pairs={{0,64},{8,72},{16,80},{24,88},{32,96},{40,104},{48,112},{56,120},{... | collective-permute-start | bytes 208904 | tf_op jit(solution)/shard_map/ppermute | solution.py:611
  71.2 9.0 %collective-permute-start.10 = (bf16[304,128]{1,0:T(8,128)(2,1)S(1)}, bf16[304,128]{1,0:T(8,128)(2,1)S(1)}, u32[]{:S(2)}, u32[]{:S(2)}) collective-permute-start(bf16[304,128]{1,0:T(8,128)(2,1)S(1)} %merge.3.after_ref.refs_0_), channel_id=1, source_target_pairs={{0,32},{8,40},{16,48},{24,56},{32,0},{40,8},{48,16},{56,24},{64,96... | collective-permute-start | bytes 233480 | tf_op jit(solution)/shard_map/ppermute | solution.py:611

commit v3 on v2

--- a/solution.py
+++ b/solution.py
@@ -78,14 +78,27 @@
     return ref.at[me // rows, pl.ds(pl.multiple_of(me % rows // 8 * 8, 8), 8), :]
 
 
-def meta_kernel(req_hbm, target_hbm, out_ref, place_ref, req_ref, target_ref, hot_ref, used_ref, seen_ref, sems):
-    copies = start_all([(req_hbm, req_ref), (target_hbm, target_ref)], sems)
+def meta_kernel(
+    me_ref, req_hbm, target_hbm, part_hbm, out_ref, place_ref, slots_hbm, row_ref,
+    req_ref, target_ref, hot_ref, used_ref, seen_ref, zero_ref, rows_ref, sems,
+):
+    me = me_ref[0]
+    own_rows = tile_of_rows(part_hbm.at[0], me, part_hbm.shape[2])
+    zero_ref[...] = jnp.zeros(zero_ref.shape, BF16)
+    size = zero_ref.shape[0]
+    fills = [
+        pltpu.make_async_copy(zero_ref, slots_hbm.at[pl.ds(i * size, size)], sems.at[3 + i])
+        for i in range(slots_hbm.shape[0] // size)
+    ]
+    copies = start_all([(req_hbm, req_ref), (target_hbm, target_ref), (own_rows, rows_ref)], sems)
+    for fill in fills:
+        fill.start()
     wide_count = out_ref.shape[0]
     for d in range(wide_count):
         used_ref[d] = 0
         seen_ref[d] = 0
     out_ref[...] = jnp.zeros(out_ref.shape, F32)
-    wait_all(copies)
+    wait_all(copies[:2])
     totals = jnp.sum(one_hot_rows(req_ref, hot_ref), axis=0, keepdims=True)
     for d in range(wide_count):
         out_ref[d, 0:1, :] = totals
@@ -97,16 +110,22 @@
         place_ref[b] = target * META + slot * (2 * BLK)
         out_ref[target, pl.ds(slot + 1, 1), :] = hot_ref[b : b + 1, :]
         out_ref[target, pl.ds(slot + 3, 1), :] = jnp.full((1, HD), rank, jnp.int32).astype(F32)
-
-
-def describe(req, target, wide_count):
+    copies[2].wait()
+    row_ref[...] = rows_ref[pl.ds(me % 8, 1), :].astype(BF16)
+    wait_all(fills)
+
+
+def describe(me, req, target, partials, wide_count):
+    depth = partials.shape[3]
     return pl.pallas_call(
         meta_kernel,
-        in_specs=[HBM, HBM],
-        out_specs=[VMEM, SMEM],
+        in_specs=[SMEM, HBM, HBM, HBM],
+        out_specs=[VMEM, SMEM, HBM, VMEM],
         out_shape=[
             jax.ShapeDtypeStruct((wide_count, 8, HD), F32),
             jax.ShapeDtypeStruct((BLK,), jnp.int32),
+            pltpu.HBM((wide_count * META, HD), BF16),
+            jax.ShapeDtypeStruct((1, depth), BF16),
         ],
         scratch_shapes=[
             pltpu.SMEM((BLK,), jnp.int32),
@@ -114,134 +133,124 @@
             pltpu.VMEM((BLK, HD), F32),
             pltpu.SMEM((wide_count,), jnp.int32),
             pltpu.SMEM((wide_count,), jnp.int32),
-            pltpu.SemaphoreType.DMA((2,)),
+            pltpu.VMEM((1024, HD), BF16),
+            pltpu.VMEM((8, depth), F32),
+            pltpu.SemaphoreType.DMA((3 + wide_count * META // 1024,)),
         ],
         compiler_params=params(),
         name="describe",
-    )(*stay(req, target))
-
-
-def begin_kernel(me_ref, part_hbm, after_ref, row_ref, rows_ref, sems):
-    me = me_ref[0]
-    wait_all(start_all([(tile_of_rows(part_hbm.at[0], me, part_hbm.shape[2]), rows_ref)], sems))
-    row_ref[...] = rows_ref[pl.ds(me % 8, 1), :].astype(BF16)
-
-
-def begin(me, partials, after):
-    depth = partials.shape[3]
-    return pl.pallas_call(
-        begin_kernel,
-        in_specs=[SMEM, HBM, SMEM],
-        out_specs=VMEM,
-        out_shape=jax.ShapeDtypeStruct((1, depth), BF16),
-        scratch_shapes=[pltpu.VMEM((8, depth), F32), pltpu.SemaphoreType.DMA((1,))],
-        compiler_params=params(),
-        name="begin",
-    )(me, *stay(partials), after)
+    )(me, *stay(req, target, partials))
 
 
 META = CAP * 2 * BLK
 
 
 def project_kernel(
-    x_hbm, gain_hbm, wk_hbm, wv_hbm, kgain_hbm, place_ref, after_ref,
-    k_ref, v_ref, w_ref, going_hbm,
-    x_ref, gain_ref, wk_ref, wv_ref, kgain_ref, going_ref, sems,
+    x_hbm, gain_hbm, wk_hbm, wv_hbm, kgain_hbm, place_ref, after_ref, slots_hbm, w_ref, going_hbm,
+    x_ref, gain_ref, wk_ref, wv_ref, kgain_ref, block_ref, sems,
 ):
     count, depth = x_ref.shape
-    tile, chunk = 256, depth // 4
-    small = start_all([(gain_hbm, gain_ref), (kgain_hbm, kgain_ref)], sems)
-    pieces = [
-        pltpu.make_async_copy(x_hbm.at[pl.ds(at, tile)], x_ref.at[pl.ds(at, tile)], sems.at[4 + i])
-        for i, at in enumerate(range(0, count, tile))
+    tile, chunk, parts = 256, 512, depth // HD
+    tiles, load, blocks = count // tile, 1024, tile // BLK
+    given = []
+
+    def copy(src, dst):
+        given.append(0)
+        return pltpu.make_async_copy(src, dst, sems.at[len(given) - 1])
+
+    xs = []
+    for i in range(tiles):
+        step = tile // (4, 2, 1, 1)[min(i, 3)]
+        xs.append(
+            [
+                copy(x_hbm.at[pl.ds(at, step)], x_ref.at[pl.ds(at, step)])
+                for at in range(i * tile, (i + 1) * tile, step)
+            ]
+        )
+    weights = [
+        [
+            copy(src.at[pl.ds(at, load)], dst.at[pl.ds(at, load)])
+            for src, dst in ((wk_hbm, wk_ref), (wv_hbm, wv_ref))
+        ]
+        for at in range(0, depth, load)
     ]
-    weights = [
-        pltpu.make_async_copy(src.at[pl.ds(at, chunk)], dst.at[pl.ds(at, chunk)], sems.at[8 + i])
-        for i, (at, src, dst) in enumerate(
-            (at, src, dst)
-            for at in range(0, depth, chunk)
-            for src, dst in ((wk_hbm, wk_ref), (wv_hbm, wv_ref))
-        )
-    ]
-    for copy in weights:
-        copy.start()
-    pieces[0].start()
-
-    going_ref[...] = jnp.zeros(going_ref.shape, BF16)
+    small = [copy(gain_hbm, gain_ref), copy(kgain_hbm, kgain_ref)]
+    outs = []
+    for c in small + xs[0] + sum(weights, []) + xs[1]:
+        c.start()
     wait_all(small)
-    parts = depth // HD
-
-    def scale(i):
+    gain = jnp.concatenate([gain_ref[...], jnp.zeros((HD - parts, HD), F32)], axis=0).T
+    wait_all(xs[0])
+
+    def put(i, acc, squares):
+        mean = jnp.sum(squares, axis=1, keepdims=True) * (1.0 / depth)
+        full = acc * lax.rsqrt(mean + EPS)
+        k, v = head_norm(full[:, :HD], kgain_ref[...]).astype(BF16), full[:, HD:].astype(BF16)
+        for b in range(blocks):
+            part, own = slice(b * BLK, (b + 1) * BLK), i * blocks + b
+            block_ref[own] = jnp.concatenate([k[part], v[part]], axis=0)
+        for own in range(i * blocks, (i + 1) * blocks):
+            place = pl.multiple_of(place_ref[own], 2 * BLK)
+            outs.append(copy(block_ref.at[own], going_hbm.at[pl.ds(place, 2 * BLK)]))
+            outs[-1].start()
+
+    for i in range(tiles):
+        rows = slice(i * tile, (i + 1) * tile)
+        if i + 2 < tiles:
+            for c in xs[i + 2]:
+                c.start()
+        acc = jnp.zeros((tile, 2 * HD), F32)
         squares = jnp.zeros((tile, HD), F32)
-        for p in range(0, parts, 2):
-            a, b = [x_ref[i * tile : (i + 1) * tile, q * HD : (q + 1) * HD] for q in (p, p + 1)]
-            squares = squares + (a * a + b * b).astype(F32)
-        mean = jnp.sum(squares, axis=1, keepdims=True) * (1.0 / depth)
-        return lax.rsqrt(mean + EPS)
-
-    gain = jnp.concatenate([gain_ref[...], jnp.zeros((HD - parts, HD), F32)], axis=0).T
-    for i in range(4):
-        wait_all(weights[2 * i : 2 * i + 2])
-        if i == 3:
-            pieces[1].start()
-        for p in range(i * parts // 4, (i + 1) * parts // 4):
-            rows = slice(p * HD, (p + 1) * HD)
-            g = gain[:, p : p + 1]
-            w_ref[rows, :HD] = (wk_ref[rows, :].astype(F32) * g).astype(BF16)
-            w_ref[rows, HD:] = (wv_ref[rows, :].astype(F32) * g).astype(BF16)
-    pieces[0].wait()
-    pieces[2].start()
-    scales = scale(0)
-    for i in range(len(pieces)):
-        rows = slice(i * tile, (i + 1) * tile)
-        if i + 1 < len(pieces):
-            pieces[i + 1].wait()
-            if i + 3 < len(pieces):
-                pieces[i + 3].start()
-        out = dot(x_ref[rows, :], w_ref[...]) * scales
-        if i + 1 < len(pieces):
-            scales = scale(i + 1)
-        k, v = head_norm(out[:, :HD], kgain_ref[...]), out[:, HD:].astype(BF16)
-        k_ref[rows, :] = k
-        v_ref[rows, :] = v
-        k = k.astype(BF16)
-        for b in range(tile // BLK):
-            part = slice(b * BLK, (b + 1) * BLK)
-            both = jnp.concatenate([k[part], v[part]], axis=0)
-            place = pl.multiple_of(place_ref[i * (tile // BLK) + b], 2 * BLK)
-            going_ref[pl.ds(place, 2 * BLK), :] = both
-    out = pltpu.make_async_copy(going_ref, going_hbm, sems.at[16])
-    out.start()
-    out.wait()
-
-
-def project(rows, gain, wk, wv, kgain, place, after, wide_count):
+        for at in range(0, depth, chunk):
+            if i == 0:
+                if at % load == 0:
+                    wait_all(weights[at // load])
+                for p in range(at // HD, (at + chunk) // HD):
+                    part = slice(p * HD, (p + 1) * HD)
+                    g = gain[:, p : p + 1]
+                    w_ref[part, :HD] = (wk_ref[part, :].astype(F32) * g).astype(BF16)
+                    w_ref[part, HD:] = (wv_ref[part, :].astype(F32) * g).astype(BF16)
+            x = x_ref[rows, at : at + chunk]
+            xf = x.astype(F32)
+            sq = xf * xf
+            for p in range(0, chunk, HD):
+                squares = squares + sq[:, p : p + HD]
+            acc = acc + dot(x, w_ref[at : at + chunk, :])
+        if i > 0:
+            put(i - 1, *held)
+        held = acc, squares
+        if i + 1 < tiles:
+            wait_all(xs[i + 1])
+    put(tiles - 1, *held)
+    wait_all(outs)
+
+
+def project(rows, gain, wk, wv, kgain, place, after, slots):
     count, depth = rows.shape
     return pl.pallas_call(
         project_kernel,
-        in_specs=[HBM] * 5 + [SMEM, VMEM],
-        out_specs=[VMEM] * 3 + [HBM],
+        in_specs=[HBM] * 5 + [SMEM, VMEM, HBM],
+        out_specs=[VMEM, HBM],
         out_shape=[
-            jax.ShapeDtypeStruct((count, HD), F32),
-            jax.ShapeDtypeStruct((count, HD), BF16),
             jax.ShapeDtypeStruct((depth, 2 * HD), BF16),
-            pltpu.HBM((wide_count * META, HD), BF16),
+            pltpu.HBM(slots.shape, BF16),
         ],
+        input_output_aliases={7: 1},
         scratch_shapes=[
             pltpu.VMEM((count, depth), BF16),
             pltpu.VMEM((depth // HD, HD), F32),
             pltpu.VMEM((depth, HD), BF16),
             pltpu.VMEM((depth, HD), BF16),
             pltpu.VMEM((1, HD), F32),
-            pltpu.VMEM((wide_count * META, HD), BF16),
-            pltpu.SemaphoreType.DMA((17,)),
+            pltpu.VMEM((count // BLK, 2 * BLK, HD), BF16),
+            pltpu.SemaphoreType.DMA((52,)),
         ],
         compiler_params=params(28),
         cost_estimate=pl.CostEstimate(
             flops=4 * count * depth * HD, bytes_accessed=2 * count * depth, transcendentals=0
         ),
         name="project",
-    )(*stay(rows, gain.reshape(depth // HD, HD), wk, wv, kgain), place, after)
+    )(*stay(rows, gain.reshape(depth // HD, HD), wk, wv, kgain), place, after, *stay(slots))
 
 
 def hold_kernel(*refs):
@@ -260,38 +269,13 @@
     )(*stay(going), *after)
 
 
-def token_kernel(me_ref, a_ref, b_ref, c_ref, d_ref, res_hbm, w_ref, kgain_hbm, out_ref, res_ref, kgain_ref, sems):
-    me = me_ref[0]
-    copies = start_all(
-        [(tile_of_rows(res_hbm, me, res_hbm.shape[1]), res_ref), (kgain_hbm, kgain_ref)], sems
-    )
-    added = tree([ref[...].astype(F32) for ref in (a_ref, b_ref, c_ref, d_ref)], jnp.add)
-    wait_all(copies)
-    hidden = res_ref[pl.ds(me % 8, 1), :] + added
+def token(parts, res, w, kgain):
+    hidden = res + tree(parts, jnp.add)
     normed = hidden * lax.rsqrt(jnp.mean(hidden * hidden, axis=-1, keepdims=True) + EPS)
     wide = jnp.broadcast_to(normed, (16, normed.shape[1])).astype(BF16)
-    out = dot(wide, w_ref[...])
-    k, v = head_norm(out[:, :HD], kgain_ref[...]), out[:, HD:]
-    out_ref[...] = jnp.where(iota(k.shape, 0) % 2 == 0, k, v)
-
-
-def token(me, parts, res, w, kgain):
-    return pl.pallas_call(
-        token_kernel,
-        in_specs=[SMEM] + [VMEM] * 4 + [HBM, VMEM, HBM],
-        out_specs=VMEM,
-        out_shape=jax.ShapeDtypeStruct((16, HD), F32),
-        scratch_shapes=[
-            pltpu.VMEM((8, res.shape[2]), F32),
-            pltpu.VMEM((1, HD), F32),
-            pltpu.SemaphoreType.DMA((2,)),
-        ],
-        compiler_params=params(),
-        cost_estimate=pl.CostEstimate(
-            flops=50_000_000, bytes_accessed=3_000_000, transcendentals=0
-        ),
-        name="token",
-    )(me, *parts, *stay(res), w, *stay(kgain))
+    out = dot(wide, w)
+    k, v = head_norm(out[:, :HD], kgain), out[:, HD:]
+    return jnp.where(iota(k.shape, 0) % 2 == 0, k, v)[0:8]
 
 
 def payload_rows(tokens):
@@ -342,9 +326,11 @@
 
 
 def attend_kernel(
-    me_ref, req_hbm, ctx_hbm, q_hbm, qgain_hbm, cache_hbm, meta_ref, k_ref, v_ref, tok_ref,
-    out_ref, qr_ref,
-    req_ref, ctx_ref, q_ref, qgain_ref, cache_ref, hot_ref, ang_ref, kr_ref,
+    me_ref, place_ref, req_hbm, ctx_hbm, q_hbm, qgain_hbm, cache_hbm, res_hbm, kgain_hbm, going_hbm,
+    meta_ref, w_ref,
+    a_ref, b_ref, out_ref, qr_ref,
+    req_ref, ctx_ref, q_ref, qgain_ref, cache_ref, res_ref, kgain_ref, block_ref, hot_ref, ang_ref,
+    kr_ref, v_ref,
     q_scr, s_scr, o_scr, sems,
 ):
     me = me_ref[0]
@@ -352,8 +338,11 @@
         [
             (req_hbm, req_ref),
             (ctx_hbm, ctx_ref),
+            (going_hbm, block_ref),
             (q_hbm, q_ref),
             (qgain_hbm, qgain_ref),
+            (tile_of_rows(res_hbm, me_ref[0], res_hbm.shape[1]), res_ref),
+            (kgain_hbm, kgain_ref),
             (cache_hbm, cache_ref),
         ],
         sems,
@@ -377,9 +366,6 @@
     earlier = dot(below(BLK), hot.astype(BF16))
     start = jnp.sum(hot * (ctx + BLK * (ahead + earlier)), axis=1, keepdims=True)
     turned = turns(start, sign)
-    for b in range(BLK):
-        part = slice(b * BLK, (b + 1) * BLK)
-        kr_ref[part, :] = turned(k_ref[part, :], b)
 
     wait_all(copies[2:])
     last = jnp.broadcast_to(last, (HD, HD)).T[:rows]
@@ -395,15 +381,23 @@
     cos_row = ang_ref[pl.ds(me, 1), :]
     ang_ref[...] = sd
     sin_row = ang_ref[pl.ds(me, 1), :]
-    tok = tok_ref[0:8, :]
-    turned = tok * cos_row + pltpu.roll(tok, HD // 2, 1) * sin_row
-    tok = jnp.where(iota(tok.shape, 0) % 2 == 0, turned, tok)
+    tok = token(
+        [ref[...].astype(F32) for ref in (a_ref, b_ref)],
+        res_ref[pl.ds(me % 8, 1), :], w_ref[...], kgain_ref[...],
+    )
+    spun = tok * cos_row + pltpu.roll(tok, HD // 2, 1) * sin_row
+    tok = jnp.where(iota(tok.shape, 0) % 2 == 0, spun, tok)
 
     place = me * slots + iota((per_row, slots), 1)
     for r in range(rows):
         mine = pl.ds(r, per_row, stride=rows)
         s = dot_nt(q_scr[mine, :].astype(BF16), cache_ref[0, r]) * score_scale
         s_scr[mine, :] = jnp.where(place < ctx_ref[r], s, MASKED)
+    for b in range(BLK):
+        part = slice(b * BLK, (b + 1) * BLK)
+        place = pl.multiple_of(place_ref[b], 2 * BLK)
+        kr_ref[part, :] = turned(block_ref[pl.ds(place, BLK), :].astype(F32), b)
+        v_ref[part, :] = block_ref[pl.ds(place + BLK, BLK), :]
     owners = []
     for j in range(0, BLK, 4):
         own = jnp.where(lane < BLK, req_ref[j], req_ref[j + 1])
@@ -436,10 +430,10 @@
     )
 
 
-def attend(me, req, ctx, q, qgain, cache, meta, keys, values, tok):
+def attend(me, place, req, ctx, q, qgain, cache, res, kgain, going, meta, weight, parts):
     return pl.pallas_call(
         attend_kernel,
-        in_specs=[SMEM] + [HBM] * 5 + [VMEM] * 4,
+        in_specs=[SMEM, SMEM] + [HBM] * 8 + [VMEM] * 4,
         out_specs=[VMEM, VMEM],
         out_shape=[
             jax.ShapeDtypeStruct((payload_rows(1), HD), BF16),
@@ -451,26 +445,51 @@
             pltpu.VMEM(q.shape, BF16),
             pltpu.VMEM(qgain.shape, F32),
             pltpu.VMEM(cache.shape, BF16),
+            pltpu.VMEM((8, res.shape[2]), F32),
+            pltpu.VMEM(kgain.shape, F32),
+            pltpu.VMEM(going.shape, BF16),
             pltpu.VMEM((BLK, HD), F32),
             pltpu.VMEM((2 * ctx.shape[0], HD), F32),
-            pltpu.VMEM(keys.shape, BF16),
+            pltpu.VMEM((BLK * BLK, HD), BF16),
+            pltpu.VMEM((BLK * BLK, HD), BF16),
         ]
         + [pltpu.VMEM((STAT, HD), F32)] * 3
-        + [pltpu.SemaphoreType.DMA((5,))],
+        + [pltpu.SemaphoreType.DMA((8,))],
         compiler_params=params(),
         cost_estimate=pl.CostEstimate(
             flops=400_000_000, bytes_accessed=5_000_000, transcendentals=300_000
         ),
         name="attend",
-    )(me, *stay(req, ctx, q, qgain, cache), meta, keys, values, tok)
+    )(me, place, *stay(req, ctx, q, qgain, cache, res, kgain, going), meta, weight, *parts)
 
 
 def finish_kernel(ctx_hbm, came_hbm, meta_ref, after_ref, out_hbm, token_ref, ctx_ref, came_ref, out_ref, sems):
-    wait_all(start_all([(ctx_hbm, ctx_ref), (came_hbm, came_ref)], sems))
     groups = came_ref.shape[0]
+    step = groups // 4
+    size = step * META
+    context = pltpu.make_async_copy(ctx_hbm, ctx_ref, sems.at[0])
+    context.start()
+    loads = [
+        pltpu.make_async_copy(
+            came_hbm.at[pl.ds(i * step, step)], came_ref.at[pl.ds(i * step, step)], sems.at[1 + i]
+        )
+        for i in range(4)
+    ]
+    stores = [
+        pltpu.make_async_copy(
+            out_ref.at[pl.ds(i * size, size)], out_hbm.at[pl.ds(i * size, size)], sems.at[5 + i]
+        )
+        for i in range(4)
+    ]
+    for load in loads:
+        load.start()
+    sign = rope_sign()
+    pr, pc = iota((2 * BLK, 2 * BLK), 0), iota((2 * BLK, 2 * BLK), 1)
+    perm = jnp.where(pc == pr // 2 + BLK * (pr % 2), 1.0, 0.0).astype(BF16)
     counts = meta_ref[:, 0, :]
-    base = context_row(ctx_ref) + BLK * dot(below(groups), counts.astype(BF16))
-    sign = rope_sign()
+    ahead = BLK * dot(below(groups), counts.astype(BF16))
+    context.wait()
+    base = context_row(ctx_ref) + ahead
     turned = [
         turns(
             jnp.sum(
@@ -480,19 +499,18 @@
         )
         for slot in range(CAP)
     ]
-    pr, pc = iota((2 * BLK, 2 * BLK), 0), iota((2 * BLK, 2 * BLK), 1)
-    perm = jnp.where(pc == pr // 2 + BLK * (pr % 2), 1.0, 0.0).astype(BF16)
-    for g in range(groups):
-        for slot in range(CAP):
-            at = slot * 2 * BLK
-            k = turned[slot](came_ref[g, at : at + BLK, :].astype(F32), g)
-            both = jnp.concatenate([k, came_ref[g, at + BLK : at + 2 * BLK, :]], axis=0)
-            to = (g * CAP + slot) * 2 * BLK
-            out_ref[to : to + 2 * BLK, :] = dot(perm, both).astype(BF16)
     token_ref[...] = base[:8]
-    out = pltpu.make_async_copy(out_ref, out_hbm, sems.at[2])
-    out.start()
-    out.wait()
+    for i in range(4):
+        loads[i].wait()
+        for g in range(i * step, (i + 1) * step):
+            for slot in range(CAP):
+                at = slot * 2 * BLK
+                k = turned[slot](came_ref[g, at : at + BLK, :].astype(F32), g)
+                both = jnp.concatenate([k, came_ref[g, at + BLK : at + 2 * BLK, :]], axis=0)
+                to = (g * CAP + slot) * 2 * BLK
+                out_ref[to : to + 2 * BLK, :] = dot(perm, both).astype(BF16)
+        stores[i].start()
+    wait_all(stores)
 
 
 def finish(ctx, came, meta, after):
@@ -506,7 +524,7 @@
             pltpu.SMEM(ctx.shape, jnp.int32),
             pltpu.VMEM(came.shape, BF16),
             pltpu.VMEM(shape, BF16),
-            pltpu.SemaphoreType.DMA((3,)),
+            pltpu.SemaphoreType.DMA((9,)),
         ],
         compiler_params=params(),
         cost_estimate=pl.CostEstimate(
@@ -611,6 +629,10 @@
     return lax.ppermute(value, axis, [(i, i ^ step) for i in range(size)])
 
 
+def add_bf16(a, b):
+    return (a.astype(F32) + b.astype(F32)).astype(BF16)
+
+
 def all_to_all(value):
     return lax.all_to_all(value, "wide", split_axis=0, concat_axis=0, tiled=True)
 
@@ -635,23 +657,24 @@
     row_count = context_lengths.shape[0]
     kgain = key_gain.reshape(1, HD)
 
-    meta, place = describe(block_request, block_target.reshape(-1), wide_count)
+    meta, place, slots, part = describe(
+        me, block_request, block_target.reshape(-1), decode_partials, wide_count
+    )
     meta = all_to_all(meta)
 
-    part = begin(me, decode_partials, place)
-    other = exchange(part, "kvh", 1)
-    part = (part.astype(F32) + other.astype(F32)).astype(BF16)
-    decode_parts = [part] + [exchange(part, "kvh", step) for step in (2, 4, 6)]
-
-    keys, values, weight, going = project(
-        prefill_rows, in_gain, key_weight, value_weight, kgain, place, part, wide_count,
+    first = part = add_bf16(part, exchange(part, "kvh", 1))
+    part = add_bf16(part, exchange(part, "kvh", 2))
+    decode_parts = [part, exchange(part, "kvh", 4)]
+
+    weight, going = project(
+        prefill_rows, in_gain, key_weight, value_weight, kgain, place, first, slots,
     )
     going = hold(going, *decode_parts)
     came = all_to_all(going.reshape(wide_count, META, HD))
-    tok = token(me, decode_parts, decode_residual, weight, kgain)
     payload, queries = attend(
-        me, block_request, context_lengths, decode_queries.reshape(2 * row_count, -1),
-        query_gain.reshape(1, HD), kv_cache, meta, keys, values, tok,
+        me, place, block_request, context_lengths, decode_queries.reshape(2 * row_count, -1),
+        query_gain.reshape(1, HD), kv_cache,
+        decode_residual, kgain, going, meta, weight, decode_parts,
     )
     parts = [payload] + [exchange(payload, "wide", step) for step in STAGES[0]]
     payload = merge(parts, 1)

time: 82.1 us -> 80 us (0.974)
  Pallas kernels: 23.9 us -> 21.4 us
  starting transfers between devices: 43.1 us -> 45.4 us
  waiting for transfers between devices: 13.2 us -> 12.1 us
    pallas_call x5 -> x3, Pallas kernels: 18.4 us -> 16.3 us  [the longest x1 10.4 us: project(): pl.pallas_call(project_kernel, in_specs=[HBM] * 5 + [SMEM, VMEM, HBM], ou...]
    ppermute x11 -> x10, starting transfers between devices: 19.4 us -> 21 us  [exchange(): return lax.ppermute(value, axis, [(i, i ^ step) for i in range(size)])]
    ppermute x11 -> x10, waiting for transfers between devices: 13.2 us -> 12 us  [exchange(): return lax.ppermute(value, axis, [(i, i ^ step) for i in range(size)])]
  transfers between devices with their start and end apart: 13 -> 12, of which waited for: 4 -> 7; matrix products, arithmetic and copies ran while one was open for 0% -> 0% of each run, Pallas kernels for 24% -> 23%
where the time goes in v3:
time: 80 us; the launch traced here: 79.7 us
  starting transfers between devices  45.4 us (57%)
  Pallas kernels  21.4 us (27%)
  waiting for transfers between devices  12.1 us (15%)
    all_to_all x2, starting transfers between devices, all_to_all(): lax.all_to_all(value, 'wide', split_axis=0, concat_axis=0, tiled=True)  24.4 us
    ppermute x10, starting transfers between devices, exchange(): return lax.ppermute(value, axis, [(i, i ^ step) for i in range(size)])  21 us
    ppermute x10, waiting for transfers between devices, exchange(): return lax.ppermute(value, axis, [(i, i ^ step) for i in range(size)])  12 us
    pallas_call x1, Pallas kernels, project(): pl.pallas_call(project_kernel, in_specs=[HBM] * 5 + [SMEM, VMEM, HBM], ou...  10.4 us
    pallas_call x1, Pallas kernels, attend(): pl.pallas_call(attend_kernel, in_specs=[SMEM, SMEM] + [HBM] * 8 + [VMEM]...  3.99 us
    pallas_call x1, Pallas kernels, finish(): pl.pallas_call(finish_kernel, in_specs=[HBM, HBM, VMEM, VMEM], out_specs=...  2.9 us
    pallas_call x1, Pallas kernels, describe(): pl.pallas_call(meta_kernel, in_specs=[SMEM, HBM, HBM, HBM], out_specs=[VM...  1.88 us
  transfers between devices with their start and end apart: 12, of which 7 were waited for; matrix products, arithmetic and copies ran while one was open for 0% of the time, Pallas kernels for 23%

profile of v3, /device:TPU:1, one launch (start us, length us, event | category | flops | bytes accessed | tf_op | source)
XLA Modules:
  0.0 79.7 jit_solution(395491726279023217)
XLA Ops:
  0.6 1.9 %describe.1 = (f32[32,8,128]{2,1,0:T(8,128)}, s32[32]{0:T(128)S(1)}, bf16[4096,128]{1,0:T(8,128)(2,1)}, bf16[1,5120]{1,0:T(2,128)(2,1)S(1)}) custom-call(s32[1]{0:T(128)} %bitcast.me_ref, s32[32]{0:T(128)} %req_hbm.3, s32[32]{0:T(128)} %bitcast.16, f32[1,2,16,5120]{3,2,1,0:T(8,128)} %part_hbm.1), custom_call_target="tpu_custom_call" | custom-call | tf_op jit(solution)/shard_map/describe/pallas_call | solution.py:120
  2.5 3.3 %collective-permute-start = (bf16[1,5120]{1,0:T(2,128)(2,1)S(1)}, bf16[1,5120]{1,0:T(2,128)(2,1)S(1)}, u32[]{:S(2)}, u32[]{:S(2)}) collective-permute-start(bf16[1,5120]{1,0:T(2,128)(2,1)S(1)} %get-tuple-element.16), channel_id=1, source_target_pairs={{0,1},{1,0},{2,3},{3,2},{4,5},{5,4},{6,7},{7,6},{8,9},{9,8},{10,11... | collective-permute-start | bytes 30728 | tf_op jit(solution)/shard_map/ppermute | solution.py:629
  5.8 0.8 %collective-permute-done = bf16[1,5120]{1,0:T(2,128)(2,1)S(1)} collective-permute-done((bf16[1,5120]{1,0:T(2,128)(2,1)S(1)}, bf16[1,5120]{1,0:T(2,128)(2,1)S(1)}, u32[]{:S(2)}, u32[]{:S(2)}) %collective-permute-start) | collective-permute-done | bytes 10272 | tf_op jit(solution)/shard_map/ppermute | solution.py:629
  6.7 0.1 collective-permute-start.1
  6.8 12.7 %all-to-all-start = ((f32[32,8,128]{2,1,0:T(8,128)}), f32[32,8,128]{2,1,0:T(8,128)S(1)}, u32[]{:S(2)}, u32[]{:S(2)}) async-start(f32[32,8,128]{2,1,0:T(8,128)} %get-tuple-element.19), calls=%async_computation | async-start | bytes 262144 | tf_op jit(solution)/shard_map/all_to_all | solution.py:637
  19.5 0.0 collective-permute-done.1
  19.5 1.3 %collective-permute-start.2 = (bf16[1,5120]{1,0:T(2,128)(2,1)S(1)}, bf16[1,5120]{1,0:T(2,128)(2,1)S(1)}, u32[]{:S(2)}, u32[]{:S(2)}) collective-permute-start(bf16[1,5120]{1,0:T(2,128)(2,1)S(1)} %add_convert_fusion.refs_1_.a_ref), channel_id=1, source_target_pairs={{0,4},{1,5},{2,6},{3,7},{4,0},{5,1},{6,2},{7,3},{8,12},{9,13},{10,... | collective-permute-start | bytes 30728 | tf_op jit(solution)/shard_map/ppermute | solution.py:629
  20.8 10.4 %project.1 = (bf16[5120,256]{1,0:T(8,128)(2,1)S(1)}, bf16[4096,128]{1,0:T(8,128)(2,1)}) custom-call(bf16[1024,5120]{1,0:T(8,128)(2,1)} %x_hbm.1, f32[40,128]{1,0:T(8,128)} %bitcast.12, bf16[5120,128]{1,0:T(8,128)(2,1)} %wk_hbm.1, bf16[5120,128]{1,0:T(8,128)(2,1)} %wv_hbm.1, f32[1,128]{1,0:T(1,128)} %bitcast.13, ...), custom_call_target="tpu_custom_call", output_to_operand_aliasing={{1}: (7, {})} | custom-call | flops 2684354560 | bytes 10485760 | tf_op jit(solution)/shard_map/project/pallas_call | solution.py:230
  31.2 0.0 collective-permute-done.2.refs_2_.b_ref
  31.2 0.0 all-to-all-done.meta_ref
  31.3 11.8 %all-to-all-start.1 = ((bf16[32,128,128]{2,1,0:T(8,128)(2,1)}), bf16[32,128,128]{2,1,0:T(8,128)(2,1)}, u32[]{:S(2)}, u32[]{:S(2)}) async-start(bf16[32,128,128]{2,1,0:T(8,128)(2,1)} %bitcast.10), calls=%async_computation.1 | async-start | bytes 2097152 | tf_op jit(solution)/shard_map/all_to_all | solution.py:637
  43.0 4.0 %attend.1 = (bf16[272,128]{1,0:T(8,128)(2,1)S(1)}, bf16[256,128]{1,0:T(8,128)(2,1)S(1)}) custom-call(s32[1]{0:T(128)} %bitcast.me_ref, s32[32]{0:T(128)S(1)} %get-tuple-element.15.place_ref, s32[32]{0:T(128)} %req_hbm.3, s32[16]{0:T(128)} %ctx_hbm.3, bf16[32,1024]{1,0:T(8,128)(2,1)} %bitcast.11, f32[1,128]{1,0:T(1,128)} %bitcast.15, ...), custom_call_target="tpu_custom_call" | custom-call | flops 400000000 | bytes 5000000 | tf_op jit(solution)/shard_map/attend/pallas_call | solution.py:434
  47.0 1.2 %collective-permute-start.3 = (bf16[272,128]{1,0:T(8,128)(2,1)S(1)}, bf16[272,128]{1,0:T(8,128)(2,1)S(1)}, u32[]{:S(2)}, u32[]{:S(2)}) collective-permute-start(bf16[272,128]{1,0:T(8,128)(2,1)S(1)} %get-tuple-element.22.refs_0_), channel_id=1, source_target_pairs={{0,8},{8,0},{16,24},{24,16},{32,40},{40,32},{48,56},{56,48},{64,72... | collective-permute-start | bytes 208904 | tf_op jit(solution)/shard_map/ppermute | solution.py:629
  48.3 2.4 %collective-permute-start.4 = (bf16[272,128]{1,0:T(8,128)(2,1)S(1)}, bf16[272,128]{1,0:T(8,128)(2,1)S(1)}, u32[]{:S(2)}, u32[]{:S(2)}) collective-permute-start(bf16[272,128]{1,0:T(8,128)(2,1)S(1)} %get-tuple-element.22.refs_0_), channel_id=1, source_target_pairs={{0,16},{8,24},{16,0},{24,8},{32,48},{40,56},{48,32},{56,40},{64,80... | collective-permute-start | bytes 208904 | tf_op jit(solution)/shard_map/ppermute | solution.py:629
  50.7 0.3 collective-permute-start.5
  51.0 5.7 %collective-permute-done.3.refs_1_ = bf16[272,128]{1,0:T(8,128)(2,1)S(1)} collective-permute-done((bf16[272,128]{1,0:T(8,128)(2,1)S(1)}, bf16[272,128]{1,0:T(8,128)(2,1)S(1)}, u32[]{:S(2)}, u32[]{:S(2)}) %collective-permute-start.3) | collective-permute-done | bytes 69664 | tf_op jit(solution)/shard_map/ppermute | solution.py:629
  56.7 1.0 %collective-permute-done.4.refs_2_ = bf16[272,128]{1,0:T(8,128)(2,1)S(1)} collective-permute-done((bf16[272,128]{1,0:T(8,128)(2,1)S(1)}, bf16[272,128]{1,0:T(8,128)(2,1)S(1)}, u32[]{:S(2)}, u32[]{:S(2)}) %collective-permute-start.4) | collective-permute-done | bytes 69664 | tf_op jit(solution)/shard_map/ppermute | solution.py:629
  57.7 2.5 %collective-permute-done.5.refs_3_ = bf16[272,128]{1,0:T(8,128)(2,1)S(1)} collective-permute-done((bf16[272,128]{1,0:T(8,128)(2,1)S(1)}, bf16[272,128]{1,0:T(8,128)(2,1)S(1)}, u32[]{:S(2)}, u32[]{:S(2)}) %collective-permute-start.5) | collective-permute-done | bytes 69664 | tf_op jit(solution)/shard_map/ppermute | solution.py:629
  60.2 0.3 merge.2.refs_0_
  60.5 0.1 collective-permute-start.6
  60.6 1.2 %collective-permute-start.7 = (bf16[272,128]{1,0:T(8,128)(2,1)S(1)}, bf16[272,128]{1,0:T(8,128)(2,1)S(1)}, u32[]{:S(2)}, u32[]{:S(2)}) collective-permute-start(bf16[272,128]{1,0:T(8,128)(2,1)S(1)} %merge.2.refs_0_), channel_id=1, source_target_pairs={{0,128},{8,136},{16,144},{24,152},{32,160},{40,168},{48,176},{56,1... | collective-permute-start | bytes 208904 | tf_op jit(solution)/shard_map/ppermute | solution.py:629
  61.8 2.6 %collective-permute-start.8 = (bf16[272,128]{1,0:T(8,128)(2,1)S(1)}, bf16[272,128]{1,0:T(8,128)(2,1)S(1)}, u32[]{:S(2)}, u32[]{:S(2)}) collective-permute-start(bf16[272,128]{1,0:T(8,128)(2,1)S(1)} %merge.2.refs_0_), channel_id=1, source_target_pairs={{0,192},{8,200},{16,208},{24,216},{32,224},{40,232},{48,240},{56,2... | collective-permute-start | bytes 208904 | tf_op jit(solution)/shard_map/ppermute | solution.py:629
  64.5 0.3 collective-permute-done.6.refs_1_
  64.8 1.3 %collective-permute-done.7.refs_2_ = bf16[272,128]{1,0:T(8,128)(2,1)S(1)} collective-permute-done((bf16[272,128]{1,0:T(8,128)(2,1)S(1)}, bf16[272,128]{1,0:T(8,128)(2,1)S(1)}, u32[]{:S(2)}, u32[]{:S(2)}) %collective-permute-start.7) | collective-permute-done | bytes 69664 | tf_op jit(solution)/shard_map/ppermute | solution.py:629
  66.0 0.4 collective-permute-done.8.refs_3_
  66.5 0.3 merge.3.after_ref.refs_0_
  66.8 8.4 %collective-permute-start.9 = (bf16[304,128]{1,0:T(8,128)(2,1)S(1)}, bf16[304,128]{1,0:T(8,128)(2,1)S(1)}, u32[]{:S(2)}, u32[]{:S(2)}) collective-permute-start(bf16[304,128]{1,0:T(8,128)(2,1)S(1)} %merge.3.after_ref.refs_0_), channel_id=1, source_target_pairs={{0,32},{8,40},{16,48},{24,56},{32,0},{40,8},{48,16},{56,24},{64,96... | collective-permute-start | bytes 233480 | tf_op jit(solution)/shard_map/ppermute | solution.py:629
  75.3 0.0 all-to-all-done.1.came_hbm
  75.3 2.9 %finish.1 = (bf16[4096,128]{1,0:T(8,128)(2,1)}, f32[8,128]{1,0:T(8,128)S(1)}) custom-call(s32[16]{0:T(128)} %ctx_hbm.3, bf16[32,128,128]{2,1,0:T(8,128)(2,1)} %all-to-all-done.1.came_hbm, f32[32,8,128]{2,1,0:T(8,128)S(1)} %all-to-all-done.meta_ref, bf16[304,128]{1,0:T(8,128)(2,1)S(1)} %merge.3.after_ref.refs_0_), custom_call_target="tpu_custom_call" | custom-call | flops 80000000 | bytes 3000000 | tf_op jit(solution)/shard_map/finish/pallas_call | solution.py:518
  78.2 0.0 collective-permute-done.9.refs_1_
  78.2 1.5 %final.1 = (bf16[32,1024]{1,0:T(8,128)(2,1)}, bf16[64,128]{1,0:T(8,128)(2,1)}) custom-call(s32[1]{0:T(128)} %bitcast.me_ref, bf16[256,128]{1,0:T(8,128)(2,1)S(1)} %get-tuple-element.21.qr_ref, f32[8,128]{1,0:T(8,128)S(1)} %get-tuple-element.23.after_ref, bf16[304,128]{1,0:T(8,128)(2,1)S(1)} %merge.3.after_ref.refs_0_, ...), custom_call_target="tpu_custom_call" | custom-call | tf_op jit(solution)/shard_map/final/pallas_call | solution.py:614
  (3 shorter events, 0.1 us)
Async XLA Ops:
  2.5 4.2 %collective-permute-start = (bf16[1,5120]{1,0:T(2,128)(2,1)S(1)}, bf16[1,5120]{1,0:T(2,128)(2,1)S(1)}, u32[]{:S(2)}, u32[]{:S(2)}) collective-permute-start(bf16[1,5120]{1,0:T(2,128)(2,1)S(1)} %get-tuple-element.16), channel_id=1, source_target_pairs={{0,1},{1,0},{2,3},{3,2},{4,5},{5,4},{6,7},{7,6},{8,9},{9,8},{10,11... | collective-permute-start | bytes 30728 | tf_op jit(solution)/shard_map/ppermute | solution.py:629
  6.7 12.8 %collective-permute-start.1 = (bf16[1,5120]{1,0:T(2,128)(2,1)S(1)}, bf16[1,5120]{1,0:T(2,128)(2,1)S(1)}, u32[]{:S(2)}, u32[]{:S(2)}) collective-permute-start(bf16[1,5120]{1,0:T(2,128)(2,1)S(1)} %add_convert_fusion.1.after_ref), channel_id=1, source_target_pairs={{0,2},{1,3},{2,0},{3,1},{4,6},{5,7},{6,4},{7,5},{8,10},{9,11},{10,... | collective-permute-start | bytes 30728 | tf_op jit(solution)/shard_map/ppermute | solution.py:629
  6.8 24.4 %all-to-all-start = ((f32[32,8,128]{2,1,0:T(8,128)}), f32[32,8,128]{2,1,0:T(8,128)S(1)}, u32[]{:S(2)}, u32[]{:S(2)}) async-start(f32[32,8,128]{2,1,0:T(8,128)} %get-tuple-element.19), calls=%async_computation | async-start | bytes 262144 | tf_op jit(solution)/shard_map/all_to_all | solution.py:637
  19.5 11.7 %collective-permute-start.2 = (bf16[1,5120]{1,0:T(2,128)(2,1)S(1)}, bf16[1,5120]{1,0:T(2,128)(2,1)S(1)}, u32[]{:S(2)}, u32[]{:S(2)}) collective-permute-start(bf16[1,5120]{1,0:T(2,128)(2,1)S(1)} %add_convert_fusion.refs_1_.a_ref), channel_id=1, source_target_pairs={{0,4},{1,5},{2,6},{3,7},{4,0},{5,1},{6,2},{7,3},{8,12},{9,13},{10,... | collective-permute-start | bytes 30728 | tf_op jit(solution)/shard_map/ppermute | solution.py:629
  31.3 44.0 %all-to-all-start.1 = ((bf16[32,128,128]{2,1,0:T(8,128)(2,1)}), bf16[32,128,128]{2,1,0:T(8,128)(2,1)}, u32[]{:S(2)}, u32[]{:S(2)}) async-start(bf16[32,128,128]{2,1,0:T(8,128)(2,1)} %bitcast.10), calls=%async_computation.1 | async-start | bytes 2097152 | tf_op jit(solution)/shard_map/all_to_all | solution.py:637
  47.0 9.7 %collective-permute-start.3 = (bf16[272,128]{1,0:T(8,128)(2,1)S(1)}, bf16[272,128]{1,0:T(8,128)(2,1)S(1)}, u32[]{:S(2)}, u32[]{:S(2)}) collective-permute-start(bf16[272,128]{1,0:T(8,128)(2,1)S(1)} %get-tuple-element.22.refs_0_), channel_id=1, source_target_pairs={{0,8},{8,0},{16,24},{24,16},{32,40},{40,32},{48,56},{56,48},{64,72... | collective-permute-start | bytes 208904 | tf_op jit(solution)/shard_map/ppermute | solution.py:629
  48.3 9.4 %collective-permute-start.4 = (bf16[272,128]{1,0:T(8,128)(2,1)S(1)}, bf16[272,128]{1,0:T(8,128)(2,1)S(1)}, u32[]{:S(2)}, u32[]{:S(2)}) collective-permute-start(bf16[272,128]{1,0:T(8,128)(2,1)S(1)} %get-tuple-element.22.refs_0_), channel_id=1, source_target_pairs={{0,16},{8,24},{16,0},{24,8},{32,48},{40,56},{48,32},{56,40},{64,80... | collective-permute-start | bytes 208904 | tf_op jit(solution)/shard_map/ppermute | solution.py:629
  50.7 9.5 %collective-permute-start.5 = (bf16[272,128]{1,0:T(8,128)(2,1)S(1)}, bf16[272,128]{1,0:T(8,128)(2,1)S(1)}, u32[]{:S(2)}, u32[]{:S(2)}) collective-permute-start(bf16[272,128]{1,0:T(8,128)(2,1)S(1)} %get-tuple-element.22.refs_0_), channel_id=1, source_target_pairs={{0,24},{8,16},{16,8},{24,0},{32,56},{40,48},{48,40},{56,32},{64,88... | collective-permute-start | bytes 208904 | tf_op jit(solution)/shard_map/ppermute | solution.py:629
  60.5 4.2 %collective-permute-start.6 = (bf16[272,128]{1,0:T(8,128)(2,1)S(1)}, bf16[272,128]{1,0:T(8,128)(2,1)S(1)}, u32[]{:S(2)}, u32[]{:S(2)}) collective-permute-start(bf16[272,128]{1,0:T(8,128)(2,1)S(1)} %merge.2.refs_0_), channel_id=1, source_target_pairs={{0,64},{8,72},{16,80},{24,88},{32,96},{40,104},{48,112},{56,120},{... | collective-permute-start | bytes 208904 | tf_op jit(solution)/shard_map/ppermute | solution.py:629
  60.6 5.4 %collective-permute-start.7 = (bf16[272,128]{1,0:T(8,128)(2,1)S(1)}, bf16[272,128]{1,0:T(8,128)(2,1)S(1)}, u32[]{:S(2)}, u32[]{:S(2)}) collective-permute-start(bf16[272,128]{1,0:T(8,128)(2,1)S(1)} %merge.2.refs_0_), channel_id=1, source_target_pairs={{0,128},{8,136},{16,144},{24,152},{32,160},{40,168},{48,176},{56,1... | collective-permute-start | bytes 208904 | tf_op jit(solution)/shard_map/ppermute | solution.py:629
  61.8 4.6 %collective-permute-start.8 = (bf16[272,128]{1,0:T(8,128)(2,1)S(1)}, bf16[272,128]{1,0:T(8,128)(2,1)S(1)}, u32[]{:S(2)}, u32[]{:S(2)}) collective-permute-start(bf16[272,128]{1,0:T(8,128)(2,1)S(1)} %merge.2.refs_0_), channel_id=1, source_target_pairs={{0,192},{8,200},{16,208},{24,216},{32,224},{40,232},{48,240},{56,2... | collective-permute-start | bytes 208904 | tf_op jit(solution)/shard_map/ppermute | solution.py:629
  66.8 11.3 %collective-permute-start.9 = (bf16[304,128]{1,0:T(8,128)(2,1)S(1)}, bf16[304,128]{1,0:T(8,128)(2,1)S(1)}, u32[]{:S(2)}, u32[]{:S(2)}) collective-permute-start(bf16[304,128]{1,0:T(8,128)(2,1)S(1)} %merge.3.after_ref.refs_0_), channel_id=1, source_target_pairs={{0,32},{8,40},{16,48},{24,56},{32,0},{40,8},{48,16},{56,24},{64,96... | collective-permute-start | bytes 233480 | tf_op jit(solution)/shard_map/ppermute | solution.py:629

commit v4 on v3

--- a/solution.py
+++ b/solution.py
@@ -51,6 +51,16 @@
     return x * lax.rsqrt(jnp.mean(x * x, axis=-1, keepdims=True) + EPS) * gain
 
 
+def slots_of(target_ref, used_ref, place_ref):
+    for d in range(used_ref.shape[0]):
+        used_ref[d] = 0
+    for b in range(BLK):
+        target = target_ref[b]
+        slot = used_ref[target]
+        used_ref[target] = slot + 1
+        place_ref[b] = target * META + slot * (2 * BLK)
+
+
 def one_hot_rows(req_ref, scr):
     lane = iota((1, HD), 1)
     for b in range(BLK):
@@ -79,10 +89,10 @@
 
 
 def meta_kernel(
-    me_ref, req_hbm, target_hbm, part_hbm, out_ref, place_ref, slots_hbm, row_ref,
+    req_hbm, target_hbm, part_hbm, out_ref, slots_hbm, row_ref,
     req_ref, target_ref, hot_ref, used_ref, seen_ref, zero_ref, rows_ref, sems,
 ):
-    me = me_ref[0]
+    me = lax.axis_index("wide")
     own_rows = tile_of_rows(part_hbm.at[0], me, part_hbm.shape[2])
     zero_ref[...] = jnp.zeros(zero_ref.shape, BF16)
     size = zero_ref.shape[0]
@@ -100,30 +110,30 @@
     out_ref[...] = jnp.zeros(out_ref.shape, F32)
     wait_all(copies[:2])
     totals = jnp.sum(one_hot_rows(req_ref, hot_ref), axis=0, keepdims=True)
+    lane = iota((1, HD), 1)
     for d in range(wide_count):
-        out_ref[d, 0:1, :] = totals
+        out_ref[d] = totals
     for b in range(BLK):
         target, request = target_ref[b], req_ref[b]
         slot, rank = used_ref[target], seen_ref[request]
         used_ref[target] = slot + 1
         seen_ref[request] = rank + 1
-        place_ref[b] = target * META + slot * (2 * BLK)
-        out_ref[target, pl.ds(slot + 1, 1), :] = hot_ref[b : b + 1, :]
-        out_ref[target, pl.ds(slot + 3, 1), :] = jnp.full((1, HD), rank, jnp.int32).astype(F32)
+        row = out_ref[target]
+        row = jnp.where(lane == 16 + slot, (request + 1).astype(F32), row)
+        out_ref[target] = jnp.where(lane == 18 + slot, rank.astype(F32), row)
     copies[2].wait()
     row_ref[...] = rows_ref[pl.ds(me % 8, 1), :].astype(BF16)
     wait_all(fills)
 
 
-def describe(me, req, target, partials, wide_count):
+def describe(req, target, partials, wide_count):
     depth = partials.shape[3]
     return pl.pallas_call(
         meta_kernel,
-        in_specs=[SMEM, HBM, HBM, HBM],
-        out_specs=[VMEM, SMEM, HBM, VMEM],
+        in_specs=[HBM, HBM, HBM],
+        out_specs=[VMEM, HBM, VMEM],
         out_shape=[
-            jax.ShapeDtypeStruct((wide_count, 8, HD), F32),
-            jax.ShapeDtypeStruct((BLK,), jnp.int32),
+            jax.ShapeDtypeStruct((wide_count, 1, HD), F32),
             pltpu.HBM((wide_count * META, HD), BF16),
             jax.ShapeDtypeStruct((1, depth), BF16),
         ],
@@ -139,15 +149,15 @@
         ],
         compiler_params=params(),
         name="describe",
-    )(me, *stay(req, target, partials))
+    )(*stay(req, target, partials))
 
 
 META = CAP * 2 * BLK
 
 
 def project_kernel(
-    x_hbm, gain_hbm, wk_hbm, wv_hbm, kgain_hbm, place_ref, after_ref, slots_hbm, w_ref, going_hbm,
-    x_ref, gain_ref, wk_ref, wv_ref, kgain_ref, block_ref, sems,
+    x_hbm, gain_hbm, wk_hbm, wv_hbm, kgain_hbm, target_hbm, after_ref, slots_hbm, w_ref, going_hbm,
+    x_ref, gain_ref, wk_ref, wv_ref, kgain_ref, target_ref, used_ref, place_ref, block_ref, sems,
 ):
     count, depth = x_ref.shape
     tile, chunk, parts = 256, 512, depth // HD
@@ -174,11 +184,12 @@
         ]
         for at in range(0, depth, load)
     ]
-    small = [copy(gain_hbm, gain_ref), copy(kgain_hbm, kgain_ref)]
+    small = [copy(gain_hbm, gain_ref), copy(kgain_hbm, kgain_ref), copy(target_hbm, target_ref)]
     outs = []
     for c in small + xs[0] + sum(weights, []) + xs[1]:
         c.start()
     wait_all(small)
+    slots_of(target_ref, used_ref, place_ref)
     gain = jnp.concatenate([gain_ref[...], jnp.zeros((HD - parts, HD), F32)], axis=0).T
     wait_all(xs[0])
 
@@ -225,11 +236,11 @@
     wait_all(outs)
 
 
-def project(rows, gain, wk, wv, kgain, place, after, slots):
+def project(rows, gain, wk, wv, kgain, target, after, slots, wide_count):
     count, depth = rows.shape
     return pl.pallas_call(
         project_kernel,
-        in_specs=[HBM] * 5 + [SMEM, VMEM, HBM],
+        in_specs=[HBM] * 6 + [VMEM, HBM],
         out_specs=[VMEM, HBM],
         out_shape=[
             jax.ShapeDtypeStruct((depth, 2 * HD), BF16),
@@ -242,15 +253,18 @@
             pltpu.VMEM((depth, HD), BF16),
             pltpu.VMEM((depth, HD), BF16),
             pltpu.VMEM((1, HD), F32),
+            pltpu.SMEM(target.shape, jnp.int32),
+            pltpu.SMEM((wide_count,), jnp.int32),
+            pltpu.SMEM(target.shape, jnp.int32),
             pltpu.VMEM((count // BLK, 2 * BLK, HD), BF16),
-            pltpu.SemaphoreType.DMA((52,)),
+            pltpu.SemaphoreType.DMA((53,)),
         ],
         compiler_params=params(28),
         cost_estimate=pl.CostEstimate(
             flops=4 * count * depth * HD, bytes_accessed=2 * count * depth, transcendentals=0
         ),
         name="project",
-    )(*stay(rows, gain.reshape(depth // HD, HD), wk, wv, kgain), place, after, *stay(slots))
+    )(*stay(rows, gain.reshape(depth // HD, HD), wk, wv, kgain, target), after, *stay(slots))
 
 
 def hold_kernel(*refs):
@@ -326,22 +340,23 @@
 
 
 def attend_kernel(
-    me_ref, place_ref, req_hbm, ctx_hbm, q_hbm, qgain_hbm, cache_hbm, res_hbm, kgain_hbm, going_hbm,
+    req_hbm, target_hbm, ctx_hbm, q_hbm, qgain_hbm, cache_hbm, res_hbm, kgain_hbm, going_hbm,
     meta_ref, w_ref,
     a_ref, b_ref, out_ref, qr_ref,
-    req_ref, ctx_ref, q_ref, qgain_ref, cache_ref, res_ref, kgain_ref, block_ref, hot_ref, ang_ref,
+    req_ref, target_ref, ctx_ref, used_ref, place_ref, q_ref, qgain_ref, cache_ref, res_ref, kgain_ref, block_ref, hot_ref, ang_ref,
     kr_ref, v_ref,
     q_scr, s_scr, o_scr, sems,
 ):
-    me = me_ref[0]
+    me = lax.axis_index("wide")
     copies = start_all(
         [
             (req_hbm, req_ref),
+            (target_hbm, target_ref),
             (ctx_hbm, ctx_ref),
             (going_hbm, block_ref),
             (q_hbm, q_ref),
             (qgain_hbm, qgain_ref),
-            (tile_of_rows(res_hbm, me_ref[0], res_hbm.shape[1]), res_ref),
+            (tile_of_rows(res_hbm, me, res_hbm.shape[1]), res_ref),
             (kgain_hbm, kgain_ref),
             (cache_hbm, cache_ref),
         ],
@@ -356,10 +371,12 @@
     freq = frequencies()
     sign = rope_sign()
     lane = iota((1, HD), 1)
-    wait_all(copies[:2])
+    wait_all(copies[:3])
+    slots_of(target_ref, used_ref, place_ref)
 
     ctx = context_row(ctx_ref)
     counts = meta_ref[:, 0, :]
+    counts = jnp.where(iota(counts.shape, 1) < rows, counts, 0.0)
     ahead = jnp.sum(jnp.where(iota(counts.shape, 0) < me, counts, 0.0), axis=0, keepdims=True)
     last = ctx + BLK * jnp.sum(counts, axis=0, keepdims=True)
     hot = one_hot_rows(req_ref, hot_ref)
@@ -367,7 +384,7 @@
     start = jnp.sum(hot * (ctx + BLK * (ahead + earlier)), axis=1, keepdims=True)
     turned = turns(start, sign)
 
-    wait_all(copies[2:])
+    wait_all(copies[3:])
     last = jnp.broadcast_to(last, (HD, HD)).T[:rows]
     ang = jnp.concatenate([last, last + 1.0], axis=0) * freq
     cd, sd = jnp.cos(ang), jnp.sin(ang) * sign
@@ -430,10 +447,10 @@
     )
 
 
-def attend(me, place, req, ctx, q, qgain, cache, res, kgain, going, meta, weight, parts):
+def attend(req, target, ctx, q, qgain, cache, res, kgain, going, meta, weight, parts):
     return pl.pallas_call(
         attend_kernel,
-        in_specs=[SMEM, SMEM] + [HBM] * 8 + [VMEM] * 4,
+        in_specs=[HBM] * 9 + [VMEM] * 4,
         out_specs=[VMEM, VMEM],
         out_shape=[
             jax.ShapeDtypeStruct((payload_rows(1), HD), BF16),
@@ -441,7 +458,10 @@
         ],
         scratch_shapes=[
             pltpu.SMEM(req.shape, jnp.int32),
+            pltpu.SMEM(target.shape, jnp.int32),
             pltpu.SMEM(ctx.shape, jnp.int32),
+            pltpu.SMEM((meta.shape[0],), jnp.int32),
+            pltpu.SMEM(target.shape, jnp.int32),
             pltpu.VMEM(q.shape, BF16),
             pltpu.VMEM(qgain.shape, F32),
             pltpu.VMEM(cache.shape, BF16),
@@ -454,13 +474,13 @@
             pltpu.VMEM((BLK * BLK, HD), BF16),
         ]
         + [pltpu.VMEM((STAT, HD), F32)] * 3
-        + [pltpu.SemaphoreType.DMA((8,))],
+        + [pltpu.SemaphoreType.DMA((9,))],
         compiler_params=params(),
         cost_estimate=pl.CostEstimate(
             flops=400_000_000, bytes_accessed=5_000_000, transcendentals=300_000
         ),
         name="attend",
-    )(me, place, *stay(req, ctx, q, qgain, cache, res, kgain, going), meta, weight, *parts)
+    )(*stay(req, target, ctx, q, qgain, cache, res, kgain, going), meta, weight, *parts)
 
 
 def finish_kernel(ctx_hbm, came_hbm, meta_ref, after_ref, out_hbm, token_ref, ctx_ref, came_ref, out_ref, sems):
@@ -486,19 +506,21 @@
     sign = rope_sign()
     pr, pc = iota((2 * BLK, 2 * BLK), 0), iota((2 * BLK, 2 * BLK), 1)
     perm = jnp.where(pc == pr // 2 + BLK * (pr % 2), 1.0, 0.0).astype(BF16)
-    counts = meta_ref[:, 0, :]
+    facts = meta_ref[:, 0, :]
+    lane = iota(facts.shape, 1)
+    counts = jnp.where(lane < ctx_ref.shape[0], facts, 0.0)
     ahead = BLK * dot(below(groups), counts.astype(BF16))
     context.wait()
     base = context_row(ctx_ref) + ahead
-    turned = [
-        turns(
-            jnp.sum(
-                meta_ref[:, 1 + slot, :] * (base + BLK * meta_ref[:, 3 + slot, :]), axis=1, keepdims=True
-            ),
-            sign,
-        )
-        for slot in range(CAP)
-    ]
+
+    def fact(at):
+        return jnp.sum(jnp.where(lane == at, facts, 0.0), axis=1, keepdims=True)
+
+    turned = []
+    for slot in range(CAP):
+        hot = lane.astype(F32) == fact(16 + slot) - 1.0
+        start = jnp.sum(jnp.where(hot, base, 0.0), axis=1, keepdims=True) + BLK * fact(18 + slot)
+        turned.append(turns(start, sign))
     token_ref[...] = base[:8]
     for i in range(4):
         loads[i].wait()
@@ -582,9 +604,9 @@
     return me ^ (slot & 3) ^ (((slot >> 2) & 3) * 8) ^ ((slot >> 4) * 4)
 
 
-def final_kernel(me_ref, qr_ref, after_ref, *refs):
+def final_kernel(qr_ref, after_ref, *refs):
     out_ref, tok_out_ref = refs[-2:]
-    me = me_ref[0]
+    me = lax.axis_index("wide")
     halves, top, total, tok = merged(refs[:-2], 16)
     keys = tok.astype(BF16)
     shape = (64, 64)
@@ -610,10 +632,10 @@
             out_ref[:, head * HD : (head + 1) * HD] = o[h * 32 : (h + 1) * 32]
 
 
-def final(me, qr, after, parts):
+def final(qr, after, parts):
     return pl.pallas_call(
         final_kernel,
-        in_specs=[SMEM] + [VMEM] * (2 + len(parts)),
+        in_specs=[VMEM] * (2 + len(parts)),
         out_specs=[VMEM, VMEM],
         out_shape=[
             jax.ShapeDtypeStruct((32, 8 * HD), BF16),
@@ -621,7 +643,7 @@
         ],
         compiler_params=params(),
         name="final",
-    )(me, qr, after, *parts)
+    )(qr, after, *parts)
 
 
 def exchange(value, axis, step):
@@ -652,14 +674,12 @@
     decode_partials,
     decode_residual,
 ):
-    me = lax.axis_index("wide").astype(jnp.int32).reshape(1)
     wide_count = lax.axis_size("wide")
     row_count = context_lengths.shape[0]
     kgain = key_gain.reshape(1, HD)
 
-    meta, place, slots, part = describe(
-        me, block_request, block_target.reshape(-1), decode_partials, wide_count
-    )
+    target = block_target.reshape(-1)
+    meta, slots, part = describe(block_request, target, decode_partials, wide_count)
     meta = all_to_all(meta)
 
     first = part = add_bf16(part, exchange(part, "kvh", 1))
@@ -667,12 +687,12 @@
     decode_parts = [part, exchange(part, "kvh", 4)]
 
     weight, going = project(
-        prefill_rows, in_gain, key_weight, value_weight, kgain, place, first, slots,
+        prefill_rows, in_gain, key_weight, value_weight, kgain, target, first, slots, wide_count,
     )
     going = hold(going, *decode_parts)
     came = all_to_all(going.reshape(wide_count, META, HD))
     payload, queries = attend(
-        me, place, block_request, context_lengths, decode_queries.reshape(2 * row_count, -1),
+        block_request, target, context_lengths, decode_queries.reshape(2 * row_count, -1),
         query_gain.reshape(1, HD), kv_cache,
         decode_residual, kgain, going, meta, weight, decode_parts,
     )
@@ -682,7 +702,7 @@
     payload = merge(parts, 4)
     parts = [payload] + [exchange(payload, "wide", step) for step in STAGES[2]]
     new_blocks, done = finish(context_lengths, came, meta, payload)
-    attended, new = final(me, queries, done, parts)
+    attended, new = final(queries, done, parts)
     return (
         attended.reshape(2, row_count, -1),
         new_blocks.reshape(wide_count * CAP, BLK, 2, HD),

time: 80 us -> 79.6 us (level)
  waiting for transfers between devices: 12.1 us -> 13.6 us
  starting transfers between devices: 45.4 us -> 44.3 us
  Pallas kernels: 21.4 us -> 20.3 us
    ppermute x10, waiting for transfers between devices: 12 us -> 13.6 us  [exchange(): return lax.ppermute(value, axis, [(i, i ^ step) for i in range(size)])]
    ppermute x10, starting transfers between devices: 21 us -> 19.9 us  [exchange(): return lax.ppermute(value, axis, [(i, i ^ step) for i in range(size)])]
    pallas_call x4, Pallas kernels: 17.8 us -> 16.7 us  [the longest x1 9.93 us: project(): pl.pallas_call(project_kernel, in_specs=[HBM] * 6 + [VMEM, HBM], out_spec...]
  transfers between devices with their start and end apart: 12 -> 12, of which waited for: 7 -> 6; matrix products, arithmetic and copies ran while one was open for 0% -> 0% of each run, Pallas kernels for 23% -> 21%
where the time goes in v4:
time: 79.6 us; the launch traced here: 79.1 us
  starting transfers between devices  44.3 us (56%)
  Pallas kernels  20.3 us (26%)
  waiting for transfers between devices  13.6 us (17%)
    all_to_all x2, starting transfers between devices, all_to_all(): lax.all_to_all(value, 'wide', split_axis=0, concat_axis=0, tiled=True)  24.4 us
    ppermute x10, starting transfers between devices, exchange(): return lax.ppermute(value, axis, [(i, i ^ step) for i in range(size)])  19.9 us
    ppermute x10, waiting for transfers between devices, exchange(): return lax.ppermute(value, axis, [(i, i ^ step) for i in range(size)])  13.6 us
    pallas_call x1, Pallas kernels, project(): pl.pallas_call(project_kernel, in_specs=[HBM] * 6 + [VMEM, HBM], out_spec...  9.93 us
    pallas_call x1, Pallas kernels, attend(): pl.pallas_call(attend_kernel, in_specs=[HBM] * 9 + [VMEM] * 4, out_specs=...  3.47 us
    pallas_call x1, Pallas kernels, finish(): pl.pallas_call(finish_kernel, in_specs=[HBM, HBM, VMEM, VMEM], out_specs=...  2.91 us
    pallas_call x1, Pallas kernels, describe(): pl.pallas_call(meta_kernel, in_specs=[HBM, HBM, HBM], out_specs=[VMEM, HB...  1.81 us
  transfers between devices with their start and end apart: 12, of which 6 were waited for; matrix products, arithmetic and copies ran while one was open for 0% of the time, Pallas kernels for 21%

profile of v4, /device:TPU:1, one launch (start us, length us, event | category | flops | bytes accessed | tf_op | source)
XLA Modules:
  0.0 79.1 jit_solution(13258302450233984751)
XLA Ops:
  0.6 1.8 %describe.1 = (f32[32,1,128]{2,1,0:T(1,128)}, bf16[4096,128]{1,0:T(8,128)(2,1)}, bf16[1,5120]{1,0:T(2,128)(2,1)S(1)}) custom-call(s32[32]{0:T(128)} %req_hbm.3, s32[32]{0:T(128)} %bitcast.12, f32[1,2,16,5120]{3,2,1,0:T(8,128)} %part_hbm.1), custom_call_target="tpu_custom_call" | custom-call | tf_op jit(solution)/shard_map/describe/pallas_call | solution.py:131
  2.4 3.3 %collective-permute-start = (bf16[1,5120]{1,0:T(2,128)(2,1)S(1)}, bf16[1,5120]{1,0:T(2,128)(2,1)S(1)}, u32[]{:S(2)}, u32[]{:S(2)}) collective-permute-start(bf16[1,5120]{1,0:T(2,128)(2,1)S(1)} %get-tuple-element.14), channel_id=1, source_target_pairs={{0,1},{1,0},{2,3},{3,2},{4,5},{5,4},{6,7},{7,6},{8,9},{9,8},{10,11... | collective-permute-start | bytes 30728 | tf_op jit(solution)/shard_map/ppermute | solution.py:651
  5.8 0.8 %collective-permute-done = bf16[1,5120]{1,0:T(2,128)(2,1)S(1)} collective-permute-done((bf16[1,5120]{1,0:T(2,128)(2,1)S(1)}, bf16[1,5120]{1,0:T(2,128)(2,1)S(1)}, u32[]{:S(2)}, u32[]{:S(2)}) %collective-permute-start) | collective-permute-done | bytes 10272 | tf_op jit(solution)/shard_map/ppermute | solution.py:651
  6.7 0.1 collective-permute-start.1
  6.8 12.7 %all-to-all-start = ((f32[32,1,128]{2,1,0:T(1,128)}), f32[32,1,128]{2,1,0:T(1,128)S(1)}, u32[]{:S(2)}, u32[]{:S(2)}) async-start(f32[32,1,128]{2,1,0:T(1,128)} %get-tuple-element.17), calls=%async_computation | async-start | bytes 32768 | tf_op jit(solution)/shard_map/all_to_all | solution.py:659
  19.4 0.0 collective-permute-done.1
  19.5 1.3 %collective-permute-start.2 = (bf16[1,5120]{1,0:T(2,128)(2,1)S(1)}, bf16[1,5120]{1,0:T(2,128)(2,1)S(1)}, u32[]{:S(2)}, u32[]{:S(2)}) collective-permute-start(bf16[1,5120]{1,0:T(2,128)(2,1)S(1)} %add_convert_fusion.refs_1_.a_ref), channel_id=1, source_target_pairs={{0,4},{1,5},{2,6},{3,7},{4,0},{5,1},{6,2},{7,3},{8,12},{9,13},{10,... | collective-permute-start | bytes 30728 | tf_op jit(solution)/shard_map/ppermute | solution.py:651
  20.7 9.9 %project.1 = (bf16[5120,256]{1,0:T(8,128)(2,1)S(1)}, bf16[4096,128]{1,0:T(8,128)(2,1)}) custom-call(bf16[1024,5120]{1,0:T(8,128)(2,1)} %x_hbm.1, f32[40,128]{1,0:T(8,128)} %bitcast.11, bf16[5120,128]{1,0:T(8,128)(2,1)} %wk_hbm.1, bf16[5120,128]{1,0:T(8,128)(2,1)} %wv_hbm.1, f32[1,128]{1,0:T(1,128)} %bitcast.15, ...), custom_call_target="tpu_custom_call", output_to_operand_aliasing={{1}: (7, {})} | custom-call | flops 2684354560 | bytes 10485760 | tf_op jit(solution)/shard_map/project/pallas_call | solution.py:241
  30.7 0.0 collective-permute-done.2.refs_2_.b_ref
  30.7 0.0 all-to-all-done.meta_ref
  30.7 11.8 %all-to-all-start.1 = ((bf16[32,128,128]{2,1,0:T(8,128)(2,1)}), bf16[32,128,128]{2,1,0:T(8,128)(2,1)}, u32[]{:S(2)}, u32[]{:S(2)}) async-start(bf16[32,128,128]{2,1,0:T(8,128)(2,1)} %bitcast.9), calls=%async_computation.1 | async-start | bytes 2097152 | tf_op jit(solution)/shard_map/all_to_all | solution.py:659
  42.5 3.5 %attend.1 = (bf16[272,128]{1,0:T(8,128)(2,1)S(1)}, bf16[256,128]{1,0:T(8,128)(2,1)S(1)}) custom-call(s32[32]{0:T(128)} %req_hbm.3, s32[32]{0:T(128)} %bitcast.14, s32[16]{0:T(128)} %ctx_hbm.3, bf16[32,1024]{1,0:T(8,128)(2,1)} %bitcast.10, f32[1,128]{1,0:T(1,128)} %bitcast.17, bf16[2,16,128,128]{3,2,1,0:T(8,128)(2,1)} %cache_hbm.1, f32[2,16,5120]{2,1,0:T(8,128)} %res_hbm.1, ...), custom_call_target="tpu_custom_call" | custom-call | flops 400000000 | bytes 5000000 | tf_op jit(solution)/shard_map/attend/pallas_call | solution.py:451
  46.0 1.2 %collective-permute-start.3 = (bf16[272,128]{1,0:T(8,128)(2,1)S(1)}, bf16[272,128]{1,0:T(8,128)(2,1)S(1)}, u32[]{:S(2)}, u32[]{:S(2)}) collective-permute-start(bf16[272,128]{1,0:T(8,128)(2,1)S(1)} %get-tuple-element.20.refs_0_), channel_id=1, source_target_pairs={{0,8},{8,0},{16,24},{24,16},{32,40},{40,32},{48,56},{56,48},{64,72... | collective-permute-start | bytes 208904 | tf_op jit(solution)/shard_map/ppermute | solution.py:651
  47.2 2.4 %collective-permute-start.4 = (bf16[272,128]{1,0:T(8,128)(2,1)S(1)}, bf16[272,128]{1,0:T(8,128)(2,1)S(1)}, u32[]{:S(2)}, u32[]{:S(2)}) collective-permute-start(bf16[272,128]{1,0:T(8,128)(2,1)S(1)} %get-tuple-element.20.refs_0_), channel_id=1, source_target_pairs={{0,16},{8,24},{16,0},{24,8},{32,48},{40,56},{48,32},{56,40},{64,80... | collective-permute-start | bytes 208904 | tf_op jit(solution)/shard_map/ppermute | solution.py:651
  49.6 0.3 collective-permute-start.5
  49.9 6.1 %collective-permute-done.3.refs_1_ = bf16[272,128]{1,0:T(8,128)(2,1)S(1)} collective-permute-done((bf16[272,128]{1,0:T(8,128)(2,1)S(1)}, bf16[272,128]{1,0:T(8,128)(2,1)S(1)}, u32[]{:S(2)}, u32[]{:S(2)}) %collective-permute-start.3) | collective-permute-done | bytes 69664 | tf_op jit(solution)/shard_map/ppermute | solution.py:651
  56.0 1.1 %collective-permute-done.4.refs_2_ = bf16[272,128]{1,0:T(8,128)(2,1)S(1)} collective-permute-done((bf16[272,128]{1,0:T(8,128)(2,1)S(1)}, bf16[272,128]{1,0:T(8,128)(2,1)S(1)}, u32[]{:S(2)}, u32[]{:S(2)}) %collective-permute-start.4) | collective-permute-done | bytes 69664 | tf_op jit(solution)/shard_map/ppermute | solution.py:651
  57.2 1.7 %collective-permute-done.5.refs_3_ = bf16[272,128]{1,0:T(8,128)(2,1)S(1)} collective-permute-done((bf16[272,128]{1,0:T(8,128)(2,1)S(1)}, bf16[272,128]{1,0:T(8,128)(2,1)S(1)}, u32[]{:S(2)}, u32[]{:S(2)}) %collective-permute-start.5) | collective-permute-done | bytes 69664 | tf_op jit(solution)/shard_map/ppermute | solution.py:651
  58.9 0.3 merge.2.refs_0_
  59.2 0.1 collective-permute-start.6
  59.3 2.5 %collective-permute-start.7 = (bf16[272,128]{1,0:T(8,128)(2,1)S(1)}, bf16[272,128]{1,0:T(8,128)(2,1)S(1)}, u32[]{:S(2)}, u32[]{:S(2)}) collective-permute-start(bf16[272,128]{1,0:T(8,128)(2,1)S(1)} %merge.2.refs_0_), channel_id=1, source_target_pairs={{0,128},{8,136},{16,144},{24,152},{32,160},{40,168},{48,176},{56,1... | collective-permute-start | bytes 208904 | tf_op jit(solution)/shard_map/ppermute | solution.py:651
  61.8 1.3 %collective-permute-start.8 = (bf16[272,128]{1,0:T(8,128)(2,1)S(1)}, bf16[272,128]{1,0:T(8,128)(2,1)S(1)}, u32[]{:S(2)}, u32[]{:S(2)}) collective-permute-start(bf16[272,128]{1,0:T(8,128)(2,1)S(1)} %merge.2.refs_0_), channel_id=1, source_target_pairs={{0,192},{8,200},{16,208},{24,216},{32,224},{40,232},{48,240},{56,2... | collective-permute-start | bytes 208904 | tf_op jit(solution)/shard_map/ppermute | solution.py:651
  63.2 0.0 collective-permute-done.6.refs_1_
  63.2 2.2 %collective-permute-done.7.refs_2_ = bf16[272,128]{1,0:T(8,128)(2,1)S(1)} collective-permute-done((bf16[272,128]{1,0:T(8,128)(2,1)S(1)}, bf16[272,128]{1,0:T(8,128)(2,1)S(1)}, u32[]{:S(2)}, u32[]{:S(2)}) %collective-permute-start.7) | collective-permute-done | bytes 69664 | tf_op jit(solution)/shard_map/ppermute | solution.py:651
  65.4 1.6 %collective-permute-done.8.refs_3_ = bf16[272,128]{1,0:T(8,128)(2,1)S(1)} collective-permute-done((bf16[272,128]{1,0:T(8,128)(2,1)S(1)}, bf16[272,128]{1,0:T(8,128)(2,1)S(1)}, u32[]{:S(2)}, u32[]{:S(2)}) %collective-permute-start.8) | collective-permute-done | bytes 69664 | tf_op jit(solution)/shard_map/ppermute | solution.py:651
  67.0 0.3 merge.3.after_ref.refs_0_
  67.3 7.3 %collective-permute-start.9 = (bf16[304,128]{1,0:T(8,128)(2,1)S(1)}, bf16[304,128]{1,0:T(8,128)(2,1)S(1)}, u32[]{:S(2)}, u32[]{:S(2)}) collective-permute-start(bf16[304,128]{1,0:T(8,128)(2,1)S(1)} %merge.3.after_ref.refs_0_), channel_id=1, source_target_pairs={{0,32},{8,40},{16,48},{24,56},{32,0},{40,8},{48,16},{56,24},{64,96... | collective-permute-start | bytes 233480 | tf_op jit(solution)/shard_map/ppermute | solution.py:651
  74.6 0.0 all-to-all-done.1.came_hbm
  74.6 2.9 %finish.1 = (bf16[4096,128]{1,0:T(8,128)(2,1)}, f32[8,128]{1,0:T(8,128)S(1)}) custom-call(s32[16]{0:T(128)} %ctx_hbm.3, bf16[32,128,128]{2,1,0:T(8,128)(2,1)} %all-to-all-done.1.came_hbm, f32[32,1,128]{2,1,0:T(1,128)S(1)} %all-to-all-done.meta_ref, bf16[304,128]{1,0:T(8,128)(2,1)S(1)} %merge.3.after_ref.refs_0_), custom_call_target="tpu_custom_call" | custom-call | flops 80000000 | bytes 3000000 | tf_op jit(solution)/shard_map/finish/pallas_call | solution.py:540
  77.5 0.0 collective-permute-done.9.refs_1_
  77.6 1.5 %final.1 = (bf16[32,1024]{1,0:T(8,128)(2,1)}, bf16[64,128]{1,0:T(8,128)(2,1)}) custom-call(bf16[256,128]{1,0:T(8,128)(2,1)S(1)} %get-tuple-element.19.qr_ref, f32[8,128]{1,0:T(8,128)S(1)} %get-tuple-element.21.after_ref, bf16[304,128]{1,0:T(8,128)(2,1)S(1)} %merge.3.after_ref.refs_0_, bf16[304,128]{1,0:T(8,128)(2,1)S(1)} %collective-permute-done.9.refs_1_), custom_call_target="tpu_custom_call" | custom-call | tf_op jit(solution)/shard_map/final/pallas_call | solution.py:636
  (3 shorter events, 0.1 us)
Async XLA Ops:
  2.4 4.2 %collective-permute-start = (bf16[1,5120]{1,0:T(2,128)(2,1)S(1)}, bf16[1,5120]{1,0:T(2,128)(2,1)S(1)}, u32[]{:S(2)}, u32[]{:S(2)}) collective-permute-start(bf16[1,5120]{1,0:T(2,128)(2,1)S(1)} %get-tuple-element.14), channel_id=1, source_target_pairs={{0,1},{1,0},{2,3},{3,2},{4,5},{5,4},{6,7},{7,6},{8,9},{9,8},{10,11... | collective-permute-start | bytes 30728 | tf_op jit(solution)/shard_map/ppermute | solution.py:651
  6.7 12.8 %collective-permute-start.1 = (bf16[1,5120]{1,0:T(2,128)(2,1)S(1)}, bf16[1,5120]{1,0:T(2,128)(2,1)S(1)}, u32[]{:S(2)}, u32[]{:S(2)}) collective-permute-start(bf16[1,5120]{1,0:T(2,128)(2,1)S(1)} %add_convert_fusion.1.after_ref), channel_id=1, source_target_pairs={{0,2},{1,3},{2,0},{3,1},{4,6},{5,7},{6,4},{7,5},{8,10},{9,11},{10,... | collective-permute-start | bytes 30728 | tf_op jit(solution)/shard_map/ppermute | solution.py:651
  6.8 24.0 %all-to-all-start = ((f32[32,1,128]{2,1,0:T(1,128)}), f32[32,1,128]{2,1,0:T(1,128)S(1)}, u32[]{:S(2)}, u32[]{:S(2)}) async-start(f32[32,1,128]{2,1,0:T(1,128)} %get-tuple-element.17), calls=%async_computation | async-start | bytes 32768 | tf_op jit(solution)/shard_map/all_to_all | solution.py:659
  19.5 11.2 %collective-permute-start.2 = (bf16[1,5120]{1,0:T(2,128)(2,1)S(1)}, bf16[1,5120]{1,0:T(2,128)(2,1)S(1)}, u32[]{:S(2)}, u32[]{:S(2)}) collective-permute-start(bf16[1,5120]{1,0:T(2,128)(2,1)S(1)} %add_convert_fusion.refs_1_.a_ref), channel_id=1, source_target_pairs={{0,4},{1,5},{2,6},{3,7},{4,0},{5,1},{6,2},{7,3},{8,12},{9,13},{10,... | collective-permute-start | bytes 30728 | tf_op jit(solution)/shard_map/ppermute | solution.py:651
  30.7 43.9 %all-to-all-start.1 = ((bf16[32,128,128]{2,1,0:T(8,128)(2,1)}), bf16[32,128,128]{2,1,0:T(8,128)(2,1)}, u32[]{:S(2)}, u32[]{:S(2)}) async-start(bf16[32,128,128]{2,1,0:T(8,128)(2,1)} %bitcast.9), calls=%async_computation.1 | async-start | bytes 2097152 | tf_op jit(solution)/shard_map/all_to_all | solution.py:659
  46.0 10.1 %collective-permute-start.3 = (bf16[272,128]{1,0:T(8,128)(2,1)S(1)}, bf16[272,128]{1,0:T(8,128)(2,1)S(1)}, u32[]{:S(2)}, u32[]{:S(2)}) collective-permute-start(bf16[272,128]{1,0:T(8,128)(2,1)S(1)} %get-tuple-element.20.refs_0_), channel_id=1, source_target_pairs={{0,8},{8,0},{16,24},{24,16},{32,40},{40,32},{48,56},{56,48},{64,72... | collective-permute-start | bytes 208904 | tf_op jit(solution)/shard_map/ppermute | solution.py:651
  47.2 10.0 %collective-permute-start.4 = (bf16[272,128]{1,0:T(8,128)(2,1)S(1)}, bf16[272,128]{1,0:T(8,128)(2,1)S(1)}, u32[]{:S(2)}, u32[]{:S(2)}) collective-permute-start(bf16[272,128]{1,0:T(8,128)(2,1)S(1)} %get-tuple-element.20.refs_0_), channel_id=1, source_target_pairs={{0,16},{8,24},{16,0},{24,8},{32,48},{40,56},{48,32},{56,40},{64,80... | collective-permute-start | bytes 208904 | tf_op jit(solution)/shard_map/ppermute | solution.py:651
  49.6 9.2 %collective-permute-start.5 = (bf16[272,128]{1,0:T(8,128)(2,1)S(1)}, bf16[272,128]{1,0:T(8,128)(2,1)S(1)}, u32[]{:S(2)}, u32[]{:S(2)}) collective-permute-start(bf16[272,128]{1,0:T(8,128)(2,1)S(1)} %get-tuple-element.20.refs_0_), channel_id=1, source_target_pairs={{0,24},{8,16},{16,8},{24,0},{32,56},{40,48},{48,40},{56,32},{64,88... | collective-permute-start | bytes 208904 | tf_op jit(solution)/shard_map/ppermute | solution.py:651
  59.2 3.9 %collective-permute-start.6 = (bf16[272,128]{1,0:T(8,128)(2,1)S(1)}, bf16[272,128]{1,0:T(8,128)(2,1)S(1)}, u32[]{:S(2)}, u32[]{:S(2)}) collective-permute-start(bf16[272,128]{1,0:T(8,128)(2,1)S(1)} %merge.2.refs_0_), channel_id=1, source_target_pairs={{0,64},{8,72},{16,80},{24,88},{32,96},{40,104},{48,112},{56,120},{... | collective-permute-start | bytes 208904 | tf_op jit(solution)/shard_map/ppermute | solution.py:651
  59.3 6.1 %collective-permute-start.7 = (bf16[272,128]{1,0:T(8,128)(2,1)S(1)}, bf16[272,128]{1,0:T(8,128)(2,1)S(1)}, u32[]{:S(2)}, u32[]{:S(2)}) collective-permute-start(bf16[272,128]{1,0:T(8,128)(2,1)S(1)} %merge.2.refs_0_), channel_id=1, source_target_pairs={{0,128},{8,136},{16,144},{24,152},{32,160},{40,168},{48,176},{56,1... | collective-permute-start | bytes 208904 | tf_op jit(solution)/shard_map/ppermute | solution.py:651
  61.8 5.1 %collective-permute-start.8 = (bf16[272,128]{1,0:T(8,128)(2,1)S(1)}, bf16[272,128]{1,0:T(8,128)(2,1)S(1)}, u32[]{:S(2)}, u32[]{:S(2)}) collective-permute-start(bf16[272,128]{1,0:T(8,128)(2,1)S(1)} %merge.2.refs_0_), channel_id=1, source_target_pairs={{0,192},{8,200},{16,208},{24,216},{32,224},{40,232},{48,240},{56,2... | collective-permute-start | bytes 208904 | tf_op jit(solution)/shard_map/ppermute | solution.py:651
  67.3 10.2 %collective-permute-start.9 = (bf16[304,128]{1,0:T(8,128)(2,1)S(1)}, bf16[304,128]{1,0:T(8,128)(2,1)S(1)}, u32[]{:S(2)}, u32[]{:S(2)}) collective-permute-start(bf16[304,128]{1,0:T(8,128)(2,1)S(1)} %merge.3.after_ref.refs_0_), channel_id=1, source_target_pairs={{0,32},{8,40},{16,48},{24,56},{32,0},{40,8},{48,16},{56,24},{64,96... | collective-permute-start | bytes 233480 | tf_op jit(solution)/shard_map/ppermute | solution.py:651
